TPU v7x, 256 devices: a whole 4x4x8 slice. The times are simulated.
256 devices in a mesh: row: 8 (over x, z_hi), col: 32 (over y, z_lo, core).
Axes of the slice: x: 4, y: 4, z: 8 (z_hi: 2, z_lo: 4; z = z_hi * 4 + z_lo), core: 2. Of those that a mesh axis runs over, the one named last changes fastest.
Arguments:
- inputs: bfloat16 [1024, 12288], P('col', 'row'), may hold values from -6 to 6
- preact: bfloat16 [1024, 24576], P('row', 'col'), may hold values from -6 to 6
- w_in: bfloat16 [12288, 24576], P('row', 'col'), may hold values from -0.0546875 to 0.0546875
- w_out: bfloat16 [24576, 12288], P('col', 'row'), may hold values from -0.0390625 to 0.0390625
- out_grad: bfloat16 [1024, 12288], P('col', 'row'), may hold values from -27 to 27
Outputs:
- input_grad: bfloat16 [1024, 12288], P('col', 'row')
- w_in_grad: bfloat16 [12288, 24576], P('row', 'col')
- w_out_grad: bfloat16 [24576, 12288], P('col', 'row')
- amaxes: float32 [2], replicated
All inputs are finite; a program needn't handle non-finite values. Where the computation divides by a largest or mean magnitude, that divisor is 1e-20 or more.
Results may differ from a plain program's by a relative error of at most 0.0058.
Values may be sent and summed in bfloat16 or wider, within the bound.
No kernel may reach another device: no remote copies, remote signals or barrier semaphores. Data moves between devices by JAX's collectives and lax.ppermute only.
A program may use at most 64 MiB of HBM per device.

v0:
```python
import math

import jax
import jax.numpy as jnp
from jax import lax
from jax.sharding import PartitionSpec as P

coef = math.sqrt(2.0 / math.pi)


def gelu_parts(pre):
    inner = coef * (pre + 0.044715 * pre * pre * pre)
    tval = jnp.tanh(inner)
    value = 0.5 * pre * (1.0 + tval)
    slope = 0.5 * (1.0 + tval) + 0.5 * pre * (1.0 - tval * tval) * coef * (
        1.0 + 3.0 * 0.044715 * pre * pre
    )
    return (value, slope)


def contract_last(left, right):
    return lax.dot_general(
        left, right, (((1,), (1,)), ((), ())), preferred_element_type=jnp.float32
    )


def contract_first(left, right):
    return lax.dot_general(
        left, right, (((0,), (0,)), ((), ())), preferred_element_type=jnp.float32
    )


def local(inputs, preact, w_in, w_out, out_grad):
    inputs_all, grad_all = (
        lax.all_gather(inputs, "col", axis=0, tiled=True),
        lax.all_gather(out_grad, "col", axis=0, tiled=True),
    )
    amax_y = lax.pmax(jnp.max(jnp.abs(out_grad.astype(jnp.float32))), ("row", "col"))
    s_y = 448.0 / (amax_y + 1e-06)
    grad_q = (grad_all.astype(jnp.float32) * s_y).astype(jnp.bfloat16)
    value, slope = gelu_parts(preact.astype(jnp.float32))
    hidden = value.astype(jnp.bfloat16)
    back = lax.psum_scatter(contract_last(grad_q, w_out), "row", scatter_dimension=0, tiled=True)
    hidden_grad = back / s_y * slope
    amax_h = lax.pmax(jnp.max(jnp.abs(hidden_grad)), ("row", "col"))
    s_h = 448.0 / (amax_h + 1e-06)
    hidden_q = (hidden_grad * s_h).astype(jnp.bfloat16)
    hidden_all, hq_all = (
        lax.all_gather(hidden, "row", axis=0, tiled=True),
        lax.all_gather(hidden_q, "row", axis=0, tiled=True),
    )
    w_out_grad = (contract_first(hidden_all, grad_q) / s_y).astype(jnp.bfloat16)
    w_in_grad = (contract_first(inputs_all, hq_all) / s_h).astype(jnp.bfloat16)
    partial_terms = contract_last(hq_all, w_in)
    summed = lax.psum_scatter(partial_terms, "col", scatter_dimension=0, tiled=True)
    input_grad = (summed / s_h).astype(jnp.bfloat16)
    amaxes = jnp.stack([amax_y, amax_h])
    return (input_grad, w_in_grad, w_out_grad, amaxes)


def solution(mesh):
    placed = (P("col", "row"), P("row", "col"), P("row", "col"), P("col", "row"), P("col", "row"))
    return jax.shard_map(
        local,
        mesh=mesh,
        in_specs=placed,
        out_specs=(P("col", "row"), P("row", "col"), P("col", "row"), P()),
        check_vma=False,
    )
```

profile of v0, /device:TPU:1, one launch (start us, length us, event | category | flops | bytes accessed | tf_op | source)
XLA Modules:
  0.0 636.9 jit_solution(4773139189830147642)
XLA Ops:
  7.2 0.0 copy-start
  7.2 0.0 all-gather.5.cloned.1.call-start
  7.2 0.7 all-gather.5.cloned.1.call-update
  7.9 0.0 reduce-scatter.3.cloned.1.call-start
  8.0 1.5 abs_reduce_fusion.1
  9.5 81.4 %pmax.14 = f32[]{:T(128)} all-reduce(f32[]{:T(128)} %abs_reduce_fusion.1), channel_id=1, replica_groups=mesh['row'=8,'col'=32] {'row','col'}, use_global_device_ids=true, to_apply=%region_1.0 | all-reduce | flops 1 | bytes 8 | tf_op jit(solution)/shard_map/pmax | solution.py:38
  91.6 0.0 all-gather.5.cloned.1.call-done
  91.6 6.9 %fusion.1 = f32[1024,768]{1,0:T(8,128)} fusion(bf16[768,1536]{1,0:T(8,128)(2,1)} %param.8, bf16[1024,1536]{1,0:T(8,128)(2,1)} %all-gather.5.cloned.1.call-done, f32[]{:T(128)S(6)} %div.31), kind=kOutput, calls=%fused_computation.4 | convolution fusion | flops 2420637696 | bytes 8650756 | tf_op jit(solution)/shard_map/dot_general | solution.py:22
  98.5 0.0 reduce-scatter.3.cloned.1.call-update
  98.5 0.0 all-gather.7.cloned.1.call-start
  98.6 104.6 %reduce-scatter.3.cloned.1.call-done = f32[128,768]{1,0:T(8,128)} async-done(((f32[1024,768]{1,0:T(8,128)}), f32[128,768]{1,0:T(8,128)}) %reduce-scatter.3.cloned.1.call-update) | async-done | bytes 393232 | tf_op jit(solution)/shard_map/reduce_scatter | solution.py:43
  203.1 0.0 copy-done.1
  203.1 2.6 abs_reduce_fusion
  205.7 75.2 %pmax.15 = f32[]{:T(128)} all-reduce(f32[]{:T(128)} %get-tuple-element.8), channel_id=1, replica_groups=mesh['row'=8,'col'=32] {'row','col'}, use_global_device_ids=true, to_apply=%region_4.0 | all-reduce | flops 1 | bytes 8 | tf_op jit(solution)/shard_map/pmax | solution.py:45
  281.6 0.7 multiply_convert_fusion.3
  282.3 0.0 all-gather.7.cloned.1.call-update
  282.3 0.0 all-gather.9.cloned.1.call-start
  282.4 0.5 all-gather.9.cloned.1.call-update
  282.9 0.0 all-gather.11.cloned.1.call-start
  282.9 0.5 all-gather.11.cloned.1.call-update
  283.5 0.0 reduce-scatter.5.cloned.1.call-start
  283.5 60.0 %all-gather.7.cloned.1.call-done = bf16[1024,768]{1,0:T(8,128)(2,1)} async-done(((bf16[128,768]{1,0:T(8,128)(2,1)}), bf16[1024,768]{1,0:T(8,128)(2,1)}) %all-gather.7.cloned.1.call-update) | async-done | bytes 1572880 | tf_op jit(solution)/shard_map/all_gather | solution.py:50
  343.5 6.0 fusion.13
  349.5 0.0 reduce-scatter.5.cloned.1.call-update
  349.6 1.9 pad_maximum_fusion
  351.4 54.6 %all-gather.9.cloned.1.call-done = bf16[1024,1536]{1,0:T(8,128)(2,1)} async-done(((bf16[32,1536]{1,0:T(8,128)(2,1)}), bf16[1024,1536]{1,0:T(8,128)(2,1)}) %all-gather.9.cloned.1.call-update) | async-done | bytes 3145744 | tf_op jit(solution)/shard_map/all_gather | solution.py:35
  406.0 6.4 %fusion = bf16[1536,768]{0,1:T(8,128)(2,1)} fusion(bf16[1024,768]{1,0:T(8,128)(2,1)} %all-gather.7.cloned.1.call-done, bf16[1024,1536]{1,0:T(8,128)(2,1)} %all-gather.9.cloned.1.call-done, f32[]{:T(128)S(6)} %div.34), kind=kOutput, calls=%fused_computation.3 | convolution fusion | flops 2418278400 | bytes 7077892 | tf_op jit(solution)/shard_map/dot_general | solution.py:28
  412.4 4.3 copy.9
  416.7 57.0 %all-gather.11.cloned.1.call-done = bf16[1024,768]{1,0:T(8,128)(2,1)} async-done(((bf16[128,768]{1,0:T(8,128)(2,1)}), bf16[1024,768]{1,0:T(8,128)(2,1)}) %all-gather.11.cloned.1.call-update) | async-done | bytes 1572880 | tf_op jit(solution)/shard_map/all_gather | solution.py:49
  473.6 6.4 %divide_convert_fusion = bf16[768,1536]{1,0:T(8,128)(2,1)} fusion(bf16[1024,768]{1,0:T(8,128)(2,1)} %all-gather.11.cloned.1.call-done, bf16[1024,1536]{1,0:T(8,128)(2,1)} %all-gather.5.cloned.1.call-done, f32[]{:T(128)S(6)} %div.31), kind=kOutput, calls=%fused_computation.1 | convolution fusion | flops 2422996992 | bytes 7077892 | tf_op jit(solution)/shard_map/dot_general | solution.py:28
  480.1 148.4 %reduce-scatter.5.cloned.1.call-done = f32[32,1536]{1,0:T(8,128)} async-done(((f32[1024,1536]{1,0:T(8,128)}), f32[32,1536]{1,0:T(8,128)}) %reduce-scatter.5.cloned.1.call-update) | async-done | bytes 196624 | tf_op jit(solution)/shard_map/reduce_scatter | solution.py:55
  628.5 1.6 divide_convert_fusion.2
  (2 shorter events, 0.0 us)
Async XLA Ops:
  7.2 336.3 %copy-start = (bf16[1536,768]{1,0:T(8,128)(2,1)S(1)}, bf16[1536,768]{1,0:T(8,128)(2,1)}, u32[]{:S(2)}) copy-start(bf16[1536,768]{1,0:T(8,128)(2,1)} %param.7) | copy-start | bytes 7077892
  7.2 84.4 %all-gather.5.cloned.1.call-start = ((), (), s32[]{:S(2)}) async-start(), calls=%async_computation.2 | async-start | bytes 3244032 | tf_op jit(solution)/shard_map/all_gather | solution.py:36
  7.9 195.2 %reduce-scatter.3.cloned.1.call-start = ((), (), s32[]{:S(2)}) async-start(), calls=%async_computation.3 | async-start | bytes 3538944 | tf_op jit(solution)/shard_map/reduce_scatter | solution.py:43
  98.5 104.6 %copy-start.1 = (bf16[128,768]{1,0:T(8,128)(2,1)S(1)}, bf16[128,768]{1,0:T(8,128)(2,1)}, u32[]{:S(2)}) copy-start(bf16[128,768]{1,0:T(8,128)(2,1)} %param.6) | copy-start | bytes 589828
  98.5 245.0 %all-gather.7.cloned.1.call-start = ((), (), s32[]{:S(2)}) async-start(), calls=%async_computation.4 | async-start | bytes 1769472 | tf_op jit(solution)/shard_map/all_gather | solution.py:50
  282.3 123.7 %all-gather.9.cloned.1.call-start = ((), (), s32[]{:S(2)}) async-start(), calls=%async_computation.6 | async-start | bytes 3244032 | tf_op jit(solution)/shard_map/all_gather | solution.py:35
  282.9 190.7 %all-gather.11.cloned.1.call-start = ((), (), s32[]{:S(2)}) async-start(), calls=%async_computation.7 | async-start | bytes 1769472 | tf_op jit(solution)/shard_map/all_gather | solution.py:49
  283.5 345.0 %reduce-scatter.5.cloned.1.call-start = ((), (), s32[]{:S(2)}) async-start(), calls=%async_computation.5 | async-start | bytes 6488064 | tf_op jit(solution)/shard_map/reduce_scatter | solution.py:55
Sparse Core Ops, SparseCore 0:
  9.9 65.9 all-gather.4
  98.6 104.4 reduce-scatter.2
  282.4 61.0 all-gather.6
  345.4 60.6 all-gather.8
  408.8 64.8 all-gather.10
  476.2 152.1 reduce-scatter.4
where the time goes:
time: 640 us; the launch traced here: 637 us
  waiting for transfers between devices  426 us (67%)
  blocking collectives  157 us (25%)
  matrix products  25.8 us (4%)
  between operations  15.5 us (2%)
  other arithmetic  8.25 us (1%)
    reduce_scatter x1, waiting for transfers between devices, local(): lax.psum_scatter(partial_terms, 'col', scatter_dimension=0, tiled=True)  148 us
    reduce_scatter x1, waiting for transfers between devices, local(): lax.psum_scatter(contract_last(grad_q, w_out), 'row', scatter_dimension=0...  105 us
    pmax x1, blocking collectives, local(): lax.pmax(jnp.max(jnp.abs(out_grad.astype(jnp.float32))), ('row', 'col'))  81.4 us
    pmax x1, blocking collectives, local(): amax_h = lax.pmax(jnp.max(jnp.abs(hidden_grad)), ('row', 'col'))  75.2 us
    all_gather x1, waiting for transfers between devices, local(): lax.all_gather(hidden_q, 'row', axis=0, tiled=True)  60 us
    all_gather x1, waiting for transfers between devices, local(): lax.all_gather(hidden, 'row', axis=0, tiled=True)  57 us
    all_gather x1, waiting for transfers between devices, local(): lax.all_gather(inputs, 'col', axis=0, tiled=True)  54.6 us
    dot_general x2, matrix products, contract_last(): lax.dot_general(left, right, (((1,), (1,)), ((), ())), preferred_element_...  13 us
  transfers between devices with their start and end apart: 6, of which 5 were waited for; matrix products, arithmetic and copies ran while one was open for 4% of the time, Pallas kernels for 0%

commit v1 on v0

v1 whole, which is shorter than its diff:
```python
import math

import jax
import jax.numpy as jnp
from jax import lax
from jax.sharding import PartitionSpec as P

coef = math.sqrt(2.0 / math.pi)
f32, bf16 = jnp.float32, jnp.bfloat16
CHUNKS = 1


def gelu_parts(pre):
    inner = coef * (pre + 0.044715 * pre * pre * pre)
    tval = jnp.tanh(inner)
    value = 0.5 * pre * (1.0 + tval)
    slope = 0.5 * (1.0 + tval) + 0.5 * pre * (1.0 - tval * tval) * coef * (
        1.0 + 3.0 * 0.044715 * pre * pre
    )
    return (value, slope)


def dot(left, right, dims):
    return lax.dot_general(left, right, (dims, ((), ())), preferred_element_type=f32)


def to_core(v):
    return lax.ppermute(v, "col", [(i, i ^ 1) for i in range(32)])


def to_l(v, k):
    return lax.ppermute(v, "col", [(i, i ^ (2 * k)) for i in range(32)])


def to_y(v, k):
    return lax.ppermute(v, "col", [(i, (i + 8 * k) % 32) for i in range(32)])


def to_x(v, k):
    return lax.ppermute(v, "row", [(i, (i + 2 * k) % 8) for i in range(8)])


def to_h(v):
    return lax.ppermute(v, "row", [(i, i ^ 1) for i in range(8)])


def pick(stacked, at):
    return lax.dynamic_index_in_dim(stacked, at, 0, keepdims=False)


def place(blocks, spots):
    out = jnp.zeros((len(blocks),) + blocks[0].shape, blocks[0].dtype)
    for block, spot in zip(blocks, spots):
        out = lax.dynamic_update_index_in_dim(out, block, spot, 0)
    return out


def by_core(c, mine, other, axis):
    first = jnp.where(c == 0, mine, other)
    second = jnp.where(c == 0, other, mine)
    return jnp.stack([first, second], axis=axis)


def spread_max(v):
    for axis, size, bits in (("row", 8, (1, 2, 4)), ("col", 32, (1, 2, 4, 8, 16))):
        for bit in bits:
            v = jnp.maximum(v, lax.ppermute(v, axis, [(i, i ^ bit) for i in range(size)]))
    return v


def local(inputs, preact, w_in, w_out, out_grad):
    row, col = lax.axis_index("row"), lax.axis_index("col")
    x, h = row // 2, row % 2
    y, l, c = col // 8, (col // 2) % 4, col % 2
    n = 32 // CHUNKS
    d, ff = out_grad.shape[1], preact.shape[1]

    inputs_all = lax.all_gather(inputs, "col", axis=0, tiled=True)
    value, _ = gelu_parts(preact.astype(f32))
    hidden_all = lax.all_gather(value.astype(bf16), "row", axis=0, tiled=True)

    w_out_both = jnp.concatenate([w_out, to_core(w_out)], axis=0)
    w_in_both = jnp.concatenate([w_in, to_core(w_in)], axis=1)
    pre = preact.reshape(4, 32, ff)
    pre_mine = jnp.stack([pick(pre, c), pick(pre, 2 + c)])
    pre_other = jnp.stack([pick(pre, 1 - c), pick(pre, 3 - c)])
    pre_mine = jnp.concatenate([pre_mine, to_core(pre_other)], axis=-1)
    pre_two = by_core(h, pre_mine, to_h(pre_mine), 0).reshape(4, 32, 2 * ff)
    pre_two = lax.optimization_barrier(pre_two)
    _, slope = gelu_parts(pre_two.astype(f32))

    grads, hqs, outs = [], [], []
    top = jnp.zeros((), f32)
    for s in range(CHUNKS):
        rows = slice(s * n, (s + 1) * n)
        mine = out_grad[rows]
        got = place([mine] + [to_l(mine, k) for k in (1, 2, 3)], [l, l ^ 1, l ^ 2, l ^ 3])
        got = got.reshape(4 * n, d)
        grad = place([got] + [to_y(got, k) for k in (1, 2, 3)], [(y - k) % 4 for k in range(4)])
        grads.append(grad.reshape(4, 4, n, d))

        back = None
        parts = []
        for j in (2, 1, 3):
            part = dot(pick(grad, (x + j) % 4), w_out_both, ((1,), (1,))).astype(bf16)
            parts.append(to_x(part, j))
        back = dot(pick(grad, x), w_out_both, ((1,), (1,)))
        for part in parts:
            back = back + part.astype(f32)
        sent = back.astype(bf16)
        back = sent.astype(f32) + to_h(sent).astype(f32)
        hidden_grad = back.reshape(4, n, 2 * ff) * slope[:, rows]
        top = jnp.maximum(top, jnp.max(jnp.abs(hidden_grad)))
        hq = hidden_grad.astype(bf16).reshape(4 * n, 2 * ff)
        hq_all = place([hq] + [to_x(hq, k) for k in (1, 2, 3)], [(x - k) % 4 for k in range(4)])
        hqs.append(hq_all.reshape(4, 4, n, 2 * ff))

        parts = []
        for k in (2, 1, 3):
            part = dot(pick(hq_all, (y + k) % 4), w_in_both, ((1,), (1,))).astype(bf16)
            parts.append(to_y(part, k))
        total = dot(pick(hq_all, y), w_in_both, ((1,), (1,)))
        for part in parts:
            total = total + part.astype(f32)
        total = total.reshape(4, n, d)
        out = pick(total, l)
        for k in (1, 2, 3):
            out = out + to_l(pick(total, l ^ k).astype(bf16), k).astype(f32)
        outs.append(out.astype(bf16))
    input_grad = jnp.concatenate(outs, axis=0)

    grad = jnp.concatenate(grads, axis=2)
    grad_all = lax.optimization_barrier(by_core(c, grad, to_core(grad), 2).reshape(1024, d))
    w_out_grad = dot(hidden_all, grad_all, ((0,), (0,))).astype(bf16)
    hq = jnp.concatenate(hqs, axis=2)
    hq_all = lax.optimization_barrier(by_core(c, hq[..., :ff], to_core(hq[..., ff:]), 2).reshape(1024, ff))
    w_in_grad = dot(inputs_all, hq_all, ((0,), (0,))).astype(bf16)

    amax_y = jnp.max(jnp.abs(out_grad.astype(f32)))
    both = jnp.where(lax.broadcasted_iota(jnp.int32, (8, 128), 0) == 0, amax_y, top)
    amaxes = spread_max(both)[:2, 0]
    return (input_grad, w_in_grad, w_out_grad, amaxes)


def solution(mesh):
    placed = (P("col", "row"), P("row", "col"), P("row", "col"), P("col", "row"), P("col", "row"))
    return jax.shard_map(
        local,
        mesh=mesh,
        in_specs=placed,
        out_specs=(P("col", "row"), P("row", "col"), P("col", "row"), P()),
        check_vma=False,
    )
```

time: 640 us -> 209 us (0.33)
  waiting for transfers between devices: 426 us -> 73.6 us
  blocking collectives: 157 us -> 0 us
  starting transfers between devices: 0.24 us -> 63.2 us
  local copies, waits for them, and re-layouts: 4.28 us -> 14.2 us
    reduce_scatter x2 -> x0, waiting for transfers between devices: 253 us -> none  [the longest x1 148 us: local(): lax.psum_scatter(partial_terms, 'col', scatter_dimension=0, tiled=True)]
    all_gather x4 -> x2, waiting for transfers between devices: 171 us -> 0.01 us  [the longest x1 0.01 us: local(): inputs_all = lax.all_gather(inputs, 'col', axis=0, tiled=True)]
    pmax x2 -> x0, blocking collectives: 157 us -> none  [the longest x1 81.4 us: local(): lax.pmax(jnp.max(jnp.abs(out_grad.astype(jnp.float32))), ('row', 'col'))]
    ppermute x0 -> x33, waiting for transfers between devices: none -> 73.6 us  [the longest x6 20.4 us: to_y(): return lax.ppermute(v, 'col', [(i, (i + 8 * k) % 32) for i in range(32)])]
    ppermute x0 -> x33, starting transfers between devices: none -> 63.1 us  [the longest x8 12.6 us: spread_max(): lax.ppermute(v, axis, [(i, i ^ bit) for i in range(size)])]
    dot_general x4 -> x10, matrix products: 25.8 us -> 28.7 us  [dot(): lax.dot_general(left, right, (dims, ((), ())), preferred_element_type=f32)]
  transfers between devices with their start and end apart: 6 -> 35, of which waited for: 5 -> 17; matrix products, arithmetic and copies ran while one was open for 4% -> 23% of each run, Pallas kernels for 0% -> 0%
where the time goes in v1:
time: 209 us; the launch traced here: 206 us
  waiting for transfers between devices  73.6 us (35%)
  starting transfers between devices  63.2 us (30%)
  matrix products  28.7 us (14%)
  between operations  15.2 us (7%)
  local copies, waits for them, and re-layouts  14.2 us (7%)
  other arithmetic  11.3 us (5%)
    dot_general x10, matrix products, dot(): lax.dot_general(left, right, (dims, ((), ())), preferred_element_type=f32)  28.7 us
    ppermute x6, waiting for transfers between devices, to_y(): return lax.ppermute(v, 'col', [(i, (i + 8 * k) % 32) for i in range(32)])  20.4 us
    ppermute x2, waiting for transfers between devices, to_h(): return lax.ppermute(v, 'row', [(i, i ^ 1) for i in range(8)])  19.4 us
    ppermute x6, waiting for transfers between devices, to_x(): return lax.ppermute(v, 'row', [(i, (i + 2 * k) % 8) for i in range(8)])  17.4 us
    ppermute x8, starting transfers between devices, spread_max(): lax.ppermute(v, axis, [(i, i ^ bit) for i in range(size)])  12.6 us
    ppermute x5, starting transfers between devices, to_core(): return lax.ppermute(v, 'col', [(i, i ^ 1) for i in range(32)])  12.2 us
    ppermute x2, starting transfers between devices, to_h(): return lax.ppermute(v, 'row', [(i, i ^ 1) for i in range(8)])  10.7 us
    ppermute x6, starting transfers between devices, to_y(): return lax.ppermute(v, 'col', [(i, (i + 8 * k) % 32) for i in range(32)])  9.65 us
  transfers between devices with their start and end apart: 35, of which 17 were waited for; matrix products, arithmetic and copies ran while one was open for 23% of the time, Pallas kernels for 0%

profile of v1, /device:TPU:1, one launch (start us, length us, event | category | flops | bytes accessed | tf_op | source)
XLA Modules:
  0.0 206.2 jit_solution(15726865050292049188)
XLA Ops:
  7.2 2.6 %collective-permute-start = (bf16[32,1536]{1,0:T(8,128)(2,1)}, bf16[32,1536]{1,0:T(8,128)(2,1)S(1)}, u32[]{:S(2)}, u32[]{:S(2)}) collective-permute-start(bf16[32,1536]{1,0:T(8,128)(2,1)} %param.9), channel_id=1, source_target_pairs={{0,2},{1,3},{2,0},{3,1},{4,6},{5,7},{6,4},{7,5},{8,10},{9,11},{10,... | collective-permute-start | bytes 294920 | tf_op jit(solution)/shard_map/ppermute | solution.py:32
  9.8 3.0 %collective-permute-start.1 = (bf16[32,1536]{1,0:T(8,128)(2,1)}, bf16[32,1536]{1,0:T(8,128)(2,1)S(1)}, u32[]{:S(2)}, u32[]{:S(2)}) collective-permute-start(bf16[32,1536]{1,0:T(8,128)(2,1)} %param.9), channel_id=1, source_target_pairs={{0,4},{1,5},{2,6},{3,7},{4,0},{5,1},{6,2},{7,3},{8,12},{9,13},{10,... | collective-permute-start | bytes 294920 | tf_op jit(solution)/shard_map/ppermute | solution.py:32
  12.8 2.2 %collective-permute-start.16 = (bf16[1536,768]{1,0:T(8,128)(2,1)}, bf16[1536,768]{1,0:T(8,128)(2,1)}, u32[]{:S(2)}, u32[]{:S(2)}) collective-permute-start(bf16[1536,768]{1,0:T(8,128)(2,1)} %param.7), channel_id=1, source_target_pairs={{0,1},{1,0},{2,3},{3,2},{4,5},{5,4},{6,7},{7,6},{8,9},{9,8},{10,11... | collective-permute-start | bytes 7077896 | tf_op jit(solution)/shard_map/ppermute | solution.py:28
  20.7 3.2 %constant_dynamic-update-slice_fusion.1 = bf16[1536,1536]{1,0:T(8,128)(2,1)} fusion(bf16[768,1536]{1,0:T(8,128)(2,1)} %param.8), kind=kLoop, calls=%fused_computation.95 | loop fusion | bytes 4718592
  23.9 2.7 %collective-permute-start.4 = (bf16[128,1536]{1,0:T(8,128)(2,1)S(1)}, bf16[128,1536]{1,0:T(8,128)(2,1)S(1)}, u32[]{:S(2)}, u32[]{:S(2)}) collective-permute-start(bf16[128,1536]{1,0:T(8,128)(2,1)S(1)} %bitcast.119), channel_id=1, source_target_pairs={{0,16},{1,17},{2,18},{3,19},{4,20},{5,21},{6,22},{7,23},{8,24},{9,... | collective-permute-start | bytes 1179656 | tf_op jit(solution)/shard_map/ppermute | solution.py:36
  28.6 9.6 %collective-permute-done.4 = bf16[128,1536]{1,0:T(8,128)(2,1)S(1)} collective-permute-done((bf16[128,1536]{1,0:T(8,128)(2,1)S(1)}, bf16[128,1536]{1,0:T(8,128)(2,1)S(1)}, u32[]{:S(2)}, u32[]{:S(2)}) %collective-permute-start.4) | collective-permute-done | bytes 393248 | tf_op jit(solution)/shard_map/ppermute | solution.py:36
  38.2 4.4 %collective-permute-done.5 = bf16[128,1536]{1,0:T(8,128)(2,1)S(1)} collective-permute-done((bf16[128,1536]{1,0:T(8,128)(2,1)S(1)}, bf16[128,1536]{1,0:T(8,128)(2,1)S(1)}, u32[]{:S(2)}, u32[]{:S(2)}) %collective-permute-start.5) | collective-permute-done | bytes 393248 | tf_op jit(solution)/shard_map/ppermute | solution.py:36
  46.2 2.5 %collective-permute-start.9 = (bf16[128,1536]{1,0:T(8,128)(2,1)S(1)}, bf16[128,1536]{1,0:T(8,128)(2,1)S(1)}, u32[]{:S(2)}, u32[]{:S(2)}) collective-permute-start(bf16[128,1536]{1,0:T(8,128)(2,1)S(1)} %convolution_convert_fusion.5), channel_id=1, source_target_pairs={{0,192},{32,224},{64,0},{96,32},{128,64},{160,96},{192,128},{224,1... | collective-permute-start | bytes 1179656 | tf_op jit(solution)/shard_map/ppermute | solution.py:40
  54.6 2.8 %collective-permute-start.11 = (bf16[2,32,768]{2,1,0:T(8,128)(2,1)}, bf16[2,32,768]{2,1,0:T(8,128)(2,1)S(1)}, u32[]{:S(2)}, u32[]{:S(2)}) collective-permute-start(bf16[2,32,768]{2,1,0:T(8,128)(2,1)} %pad_maximum_fusion.4), channel_id=1, source_target_pairs={{0,1},{1,0},{2,3},{3,2},{4,5},{5,4},{6,7},{7,6},{8,9},{9,8},{10,11... | collective-permute-start | bytes 294920 | tf_op jit(solution)/shard_map/ppermute | solution.py:28
  58.5 5.3 %collective-permute-start.12 = (bf16[2,32,1536]{2,1,0:T(8,128)(2,1)S(1)}, bf16[2,32,1536]{2,1,0:T(8,128)(2,1)S(1)}, u32[]{:S(2)}, u32[]{:S(2)}) collective-permute-start(bf16[2,32,1536]{2,1,0:T(8,128)(2,1)S(1)} %pad_maximum_fusion.3), channel_id=1, source_target_pairs={{0,32},{32,0},{64,96},{96,64},{128,160},{160,128},{192,224},{224,1... | collective-permute-start | bytes 589832 | tf_op jit(solution)/shard_map/ppermute | solution.py:44
  63.8 6.2 %collective-permute-done.7 = bf16[128,1536]{1,0:T(8,128)(2,1)} collective-permute-done((bf16[128,1536]{1,0:T(8,128)(2,1)S(1)}, bf16[128,1536]{1,0:T(8,128)(2,1)}, u32[]{:S(2)}, u32[]{:S(2)}) %collective-permute-start.7) | collective-permute-done | bytes 393248 | tf_op jit(solution)/shard_map/ppermute | solution.py:40
  70.1 4.2 %fusion.5 = bf16[128,1536]{1,0:T(8,128)(2,1)S(1)} fusion(bf16[1536,1536]{1,0:T(8,128)(2,1)} %copy-done.1, bf16[128,1536]{1,0:T(8,128)(2,1)S(1)} %collective-permute-done.9, bf16[128,1536]{1,0:T(8,128)(2,1)} %collective-permute-done.8, bf16[128,1536]{1,0:T(8,128)(2,1)} %collective-permute-done.7, ...), kind=kOutput, calls=%fused_computation.10 | convolution fusion | flops 605356032 | bytes 6684676 | tf_op jit(solution)/shard_map/dot_general | solution.py:24
  74.3 5.4 %collective-permute-start.10 = (bf16[128,1536]{1,0:T(8,128)(2,1)S(1)}, bf16[128,1536]{1,0:T(8,128)(2,1)S(1)}, u32[]{:S(2)}, u32[]{:S(2)}) collective-permute-start(bf16[128,1536]{1,0:T(8,128)(2,1)S(1)} %fusion.5), channel_id=1, source_target_pairs={{0,32},{32,0},{64,96},{96,64},{128,160},{160,128},{192,224},{224,1... | collective-permute-start | bytes 1179656 | tf_op jit(solution)/shard_map/ppermute | solution.py:44
  79.8 5.2 %collective-permute-start.24 = (bf16[4,4,32,1536]{3,2,1,0:T(8,128)(2,1)S(1)}, bf16[4,4,32,1536]{3,2,1,0:T(8,128)(2,1)}, u32[]{:S(2)}, u32[]{:S(2)}) collective-permute-start(bf16[4,4,32,1536]{3,2,1,0:T(8,128)(2,1)S(1)} %bitcast.110), channel_id=1, source_target_pairs={{0,1},{1,0},{2,3},{3,2},{4,5},{5,4},{6,7},{7,6},{8,9},{9,8},{10,11... | collective-permute-start | bytes 4718600 | tf_op jit(solution)/shard_map/ppermute | solution.py:28
  85.0 19.4 %collective-permute-done.10 = bf16[128,1536]{1,0:T(8,128)(2,1)S(1)} collective-permute-done((bf16[128,1536]{1,0:T(8,128)(2,1)S(1)}, bf16[128,1536]{1,0:T(8,128)(2,1)S(1)}, u32[]{:S(2)}, u32[]{:S(2)}) %collective-permute-start.10) | collective-permute-done | bytes 393248 | tf_op jit(solution)/shard_map/ppermute | solution.py:44
  106.9 2.8 %collective-permute-start.25 = (f32[8,128]{0,1:T(8,128)S(1)}, f32[8,128]{0,1:T(8,128)S(1)}, u32[]{:S(2)}, u32[]{:S(2)}) collective-permute-start(f32[8,128]{0,1:T(8,128)S(1)} %iota.7), channel_id=1, source_target_pairs={{0,32},{32,0},{64,96},{96,64},{128,160},{160,128},{192,224},{224,1... | collective-permute-start | bytes 12296 | tf_op jit(solution)/shard_map/ppermute | solution.py:67
  109.7 3.3 %constant_dynamic-update-slice_fusion.3 = bf16[1536,1536]{1,0:T(8,128)(2,1)} fusion(bf16[1536,768]{1,0:T(8,128)(2,1)} %param.7), kind=kLoop, calls=%fused_computation.97 | loop fusion | bytes 4718592
  117.3 2.8 %collective-permute-start.27 = (f32[8,128]{0,1:T(8,128)S(1)}, f32[8,128]{0,1:T(8,128)S(1)}, u32[]{:S(2)}, u32[]{:S(2)}) collective-permute-start(f32[8,128]{0,1:T(8,128)S(1)} %fusion.63), channel_id=1, source_target_pairs={{0,128},{32,160},{64,192},{96,224},{128,0},{160,32},{192,64},{224,... | collective-permute-start | bytes 12296 | tf_op jit(solution)/shard_map/ppermute | solution.py:67
  122.4 4.2 %collective-permute-start.28 = (f32[8,128]{0,1:T(8,128)S(1)}, f32[8,128]{0,1:T(8,128)S(1)}, u32[]{:S(2)}, u32[]{:S(2)}) collective-permute-start(f32[8,128]{0,1:T(8,128)S(1)} %max.26), channel_id=1, source_target_pairs={{0,1},{1,0},{2,3},{3,2},{4,5},{5,4},{6,7},{7,6},{8,9},{9,8},{10,11... | collective-permute-start | bytes 12296 | tf_op jit(solution)/shard_map/ppermute | solution.py:67
  126.6 2.0 pad_maximum_fusion
  132.4 2.5 %collective-permute-start.14 = (bf16[128,1536]{1,0:T(8,128)(2,1)S(1)}, bf16[128,1536]{1,0:T(8,128)(2,1)S(1)}, u32[]{:S(2)}, u32[]{:S(2)}) collective-permute-start(bf16[128,1536]{1,0:T(8,128)(2,1)S(1)} %bitcast.123), channel_id=1, source_target_pairs={{0,128},{32,160},{64,192},{96,224},{128,0},{160,32},{192,64},{224,... | collective-permute-start | bytes 1179656 | tf_op jit(solution)/shard_map/ppermute | solution.py:40
  135.3 4.5 %collective-permute-done.30 = f32[8,128]{0,1:T(8,128)S(1)} collective-permute-done((f32[8,128]{0,1:T(8,128)S(1)}, f32[8,128]{0,1:T(8,128)S(1)}, u32[]{:S(2)}, u32[]{:S(2)}) %collective-permute-start.30) | collective-permute-done | bytes 4128 | tf_op jit(solution)/shard_map/ppermute | solution.py:67
  141.2 9.4 %collective-permute-done.14 = bf16[128,1536]{1,0:T(8,128)(2,1)S(1)} collective-permute-done((bf16[128,1536]{1,0:T(8,128)(2,1)S(1)}, bf16[128,1536]{1,0:T(8,128)(2,1)S(1)}, u32[]{:S(2)}, u32[]{:S(2)}) %collective-permute-start.14) | collective-permute-done | bytes 393248 | tf_op jit(solution)/shard_map/ppermute | solution.py:40
  155.2 2.4 %convolution_convert_fusion.3 = bf16[128,1536]{1,0:T(8,128)(2,1)} fusion(bf16[1536,1536]{1,0:T(8,128)(2,1)S(1)} %constant_dynamic-update-slice_fusion.2, bf16[4,128,1536]{2,1,0:T(8,128)(2,1)S(1)} %bitcast_dynamic-update-slice_fusion, s32[]{:T(128)S(6)} %select_n.247), kind=kOutput, calls=%fused_computation.12 | convolution fusion | flops 604176384 | bytes 5505028 | tf_op jit(solution)/shard_map/dot_general | solution.py:24
  157.9 2.4 %convolution_convert_fusion.4 = bf16[128,1536]{1,0:T(8,128)(2,1)} fusion(bf16[1536,1536]{1,0:T(8,128)(2,1)S(1)} %constant_dynamic-update-slice_fusion.2, bf16[4,128,1536]{2,1,0:T(8,128)(2,1)S(1)} %bitcast_dynamic-update-slice_fusion, s32[]{:T(128)S(6)} %select_n.245), kind=kOutput, calls=%fused_computation.13 | convolution fusion | flops 604176384 | bytes 5505028 | tf_op jit(solution)/shard_map/dot_general | solution.py:24
  160.3 2.8 %collective-permute-start.17 = (bf16[128,1536]{1,0:T(8,128)(2,1)}, bf16[128,1536]{1,0:T(8,128)(2,1)S(1)}, u32[]{:S(2)}, u32[]{:S(2)}) collective-permute-start(bf16[128,1536]{1,0:T(8,128)(2,1)} %convolution_convert_fusion.4), channel_id=1, source_target_pairs={{0,16},{1,17},{2,18},{3,19},{4,20},{5,21},{6,22},{7,23},{8,24},{9,... | collective-permute-start | bytes 1179656 | tf_op jit(solution)/shard_map/ppermute | solution.py:36
  163.1 6.6 %convolution_convert_fusion = bf16[768,1536]{1,0:T(8,128)(2,1)} fusion(bf16[1024,768]{1,0:T(8,128)(2,1)} %all-gather.5.cloned.1.call-done, bf16[1024,1536]{1,0:T(8,128)(2,1)} %bitcast.112), kind=kOutput, calls=%fused_computation | convolution fusion | flops 2417098752 | bytes 7077888 | tf_op jit(solution)/shard_map/dot_general | solution.py:24
  170.0 2.0 collective-permute-start.23
  172.0 5.7 %collective-permute-done.17 = bf16[128,1536]{1,0:T(8,128)(2,1)S(1)} collective-permute-done((bf16[128,1536]{1,0:T(8,128)(2,1)}, bf16[128,1536]{1,0:T(8,128)(2,1)S(1)}, u32[]{:S(2)}, u32[]{:S(2)}) %collective-permute-start.17) | collective-permute-done | bytes 393248 | tf_op jit(solution)/shard_map/ppermute | solution.py:36
  185.0 4.8 %collective-permute-done.21 = bf16[32,1536]{1,0:T(8,128)(2,1)S(1)} collective-permute-done((bf16[32,1536]{1,0:T(8,128)(2,1)S(1)}, bf16[32,1536]{1,0:T(8,128)(2,1)S(1)}, u32[]{:S(2)}, u32[]{:S(2)}) %collective-permute-start.21) | collective-permute-done | bytes 98336 | tf_op jit(solution)/shard_map/ppermute | solution.py:32
  191.9 5.0 %fusion = bf16[1536,768]{0,1:T(8,128)(2,1)S(1)} fusion(bf16[1024,768]{1,0:T(8,128)(2,1)} %bitcast.116, bf16[1024,1536]{1,0:T(8,128)(2,1)} %all-gather.3.cloned.1.call-done), kind=kOutput, calls=%fused_computation.3 | convolution fusion | flops 2417098752 | bytes 7077888 | tf_op jit(solution)/shard_map/dot_general | solution.py:24
  196.9 2.4 %copy.12 = bf16[1536,768]{1,0:T(8,128)(2,1)} copy(bf16[1536,768]{0,1:T(8,128)(2,1)S(1)} %fusion) | data formatting | bytes 4718592
  (113 shorter events, 46.8 us)
Async XLA Ops:
  7.2 155.9 %all-gather.5.cloned.1.call-start = ((), (), s32[]{:S(2)}) async-start(), calls=%async_computation.1 | async-start | bytes 1769472 | tf_op jit(solution)/shard_map/all_gather | solution.py:80
  7.2 10.5 %collective-permute-start = (bf16[32,1536]{1,0:T(8,128)(2,1)}, bf16[32,1536]{1,0:T(8,128)(2,1)S(1)}, u32[]{:S(2)}, u32[]{:S(2)}) collective-permute-start(bf16[32,1536]{1,0:T(8,128)(2,1)} %param.9), channel_id=1, source_target_pairs={{0,2},{1,3},{2,0},{3,1},{4,6},{5,7},{6,4},{7,5},{8,10},{9,11},{10,... | collective-permute-start | bytes 294920 | tf_op jit(solution)/shard_map/ppermute | solution.py:32
  9.8 8.0 %collective-permute-start.1 = (bf16[32,1536]{1,0:T(8,128)(2,1)}, bf16[32,1536]{1,0:T(8,128)(2,1)S(1)}, u32[]{:S(2)}, u32[]{:S(2)}) collective-permute-start(bf16[32,1536]{1,0:T(8,128)(2,1)} %param.9), channel_id=1, source_target_pairs={{0,4},{1,5},{2,6},{3,7},{4,0},{5,1},{6,2},{7,3},{8,12},{9,13},{10,... | collective-permute-start | bytes 294920 | tf_op jit(solution)/shard_map/ppermute | solution.py:32
  12.8 6.5 %collective-permute-start.2 = (bf16[32,1536]{1,0:T(8,128)(2,1)}, bf16[32,1536]{1,0:T(8,128)(2,1)S(1)}, u32[]{:S(2)}, u32[]{:S(2)}) collective-permute-start(bf16[32,1536]{1,0:T(8,128)(2,1)} %param.9), channel_id=1, source_target_pairs={{0,6},{1,7},{2,4},{3,5},{4,2},{5,3},{6,0},{7,1},{8,14},{9,15},{10,... | collective-permute-start | bytes 294920 | tf_op jit(solution)/shard_map/ppermute | solution.py:32
  12.8 117.8 %collective-permute-start.16 = (bf16[1536,768]{1,0:T(8,128)(2,1)}, bf16[1536,768]{1,0:T(8,128)(2,1)}, u32[]{:S(2)}, u32[]{:S(2)}) collective-permute-start(bf16[1536,768]{1,0:T(8,128)(2,1)} %param.7), channel_id=1, source_target_pairs={{0,1},{1,0},{2,3},{3,2},{4,5},{5,4},{6,7},{7,6},{8,9},{9,8},{10,11... | collective-permute-start | bytes 7077896 | tf_op jit(solution)/shard_map/ppermute | solution.py:28
  14.9 27.8 %collective-permute-start.6 = (bf16[768,1536]{1,0:T(8,128)(2,1)}, bf16[768,1536]{1,0:T(8,128)(2,1)}, u32[]{:S(2)}, u32[]{:S(2)}) collective-permute-start(bf16[768,1536]{1,0:T(8,128)(2,1)} %param.8), channel_id=1, source_target_pairs={{0,1},{1,0},{2,3},{3,2},{4,5},{5,4},{6,7},{7,6},{8,9},{9,8},{10,11... | collective-permute-start | bytes 7077896 | tf_op jit(solution)/shard_map/ppermute | solution.py:28
  16.7 175.2 %all-gather.3.cloned.1.call-start = ((), (), s32[]{:S(2)}) async-start(), calls=%async_computation | async-start | bytes 3244032 | tf_op jit(solution)/shard_map/all_gather | solution.py:78
  19.3 9.3 %collective-permute-start.3 = (bf16[128,1536]{1,0:T(8,128)(2,1)S(1)}, bf16[128,1536]{1,0:T(8,128)(2,1)S(1)}, u32[]{:S(2)}, u32[]{:S(2)}) collective-permute-start(bf16[128,1536]{1,0:T(8,128)(2,1)S(1)} %bitcast.118), channel_id=1, source_target_pairs={{0,8},{1,9},{2,10},{3,11},{4,12},{5,13},{6,14},{7,15},{8,16},{9,17... | collective-permute-start | bytes 1179656 | tf_op jit(solution)/shard_map/ppermute | solution.py:36
  23.9 14.3 %collective-permute-start.4 = (bf16[128,1536]{1,0:T(8,128)(2,1)S(1)}, bf16[128,1536]{1,0:T(8,128)(2,1)S(1)}, u32[]{:S(2)}, u32[]{:S(2)}) collective-permute-start(bf16[128,1536]{1,0:T(8,128)(2,1)S(1)} %bitcast.119), channel_id=1, source_target_pairs={{0,16},{1,17},{2,18},{3,19},{4,20},{5,21},{6,22},{7,23},{8,24},{9,... | collective-permute-start | bytes 1179656 | tf_op jit(solution)/shard_map/ppermute | solution.py:36
  26.6 16.0 %collective-permute-start.5 = (bf16[128,1536]{1,0:T(8,128)(2,1)S(1)}, bf16[128,1536]{1,0:T(8,128)(2,1)S(1)}, u32[]{:S(2)}, u32[]{:S(2)}) collective-permute-start(bf16[128,1536]{1,0:T(8,128)(2,1)S(1)} %bitcast.120), channel_id=1, source_target_pairs={{0,24},{1,25},{2,26},{3,27},{4,28},{5,29},{6,30},{7,31},{8,0},{9,1... | collective-permute-start | bytes 1179656 | tf_op jit(solution)/shard_map/ppermute | solution.py:36
  46.2 17.6 %collective-permute-start.9 = (bf16[128,1536]{1,0:T(8,128)(2,1)S(1)}, bf16[128,1536]{1,0:T(8,128)(2,1)S(1)}, u32[]{:S(2)}, u32[]{:S(2)}) collective-permute-start(bf16[128,1536]{1,0:T(8,128)(2,1)S(1)} %convolution_convert_fusion.5), channel_id=1, source_target_pairs={{0,192},{32,224},{64,0},{96,32},{128,64},{160,96},{192,128},{224,1... | collective-permute-start | bytes 1179656 | tf_op jit(solution)/shard_map/ppermute | solution.py:40
  50.4 13.4 %collective-permute-start.8 = (bf16[128,1536]{1,0:T(8,128)(2,1)S(1)}, bf16[128,1536]{1,0:T(8,128)(2,1)}, u32[]{:S(2)}, u32[]{:S(2)}) collective-permute-start(bf16[128,1536]{1,0:T(8,128)(2,1)S(1)} %convolution_convert_fusion.6), channel_id=1, source_target_pairs={{0,64},{32,96},{64,128},{96,160},{128,192},{160,224},{192,0},{224,... | collective-permute-start | bytes 1179656 | tf_op jit(solution)/shard_map/ppermute | solution.py:40
  52.1 17.9 %collective-permute-start.7 = (bf16[128,1536]{1,0:T(8,128)(2,1)S(1)}, bf16[128,1536]{1,0:T(8,128)(2,1)}, u32[]{:S(2)}, u32[]{:S(2)}) collective-permute-start(bf16[128,1536]{1,0:T(8,128)(2,1)S(1)} %convolution_convert_fusion.7), channel_id=1, source_target_pairs={{0,128},{32,160},{64,192},{96,224},{128,0},{160,32},{192,64},{224,... | collective-permute-start | bytes 1179656 | tf_op jit(solution)/shard_map/ppermute | solution.py:40
  58.5 21.2 %collective-permute-start.12 = (bf16[2,32,1536]{2,1,0:T(8,128)(2,1)S(1)}, bf16[2,32,1536]{2,1,0:T(8,128)(2,1)S(1)}, u32[]{:S(2)}, u32[]{:S(2)}) collective-permute-start(bf16[2,32,1536]{2,1,0:T(8,128)(2,1)S(1)} %pad_maximum_fusion.3), channel_id=1, source_target_pairs={{0,32},{32,0},{64,96},{96,64},{128,160},{160,128},{192,224},{224,1... | collective-permute-start | bytes 589832 | tf_op jit(solution)/shard_map/ppermute | solution.py:44
  74.3 30.1 %collective-permute-start.10 = (bf16[128,1536]{1,0:T(8,128)(2,1)S(1)}, bf16[128,1536]{1,0:T(8,128)(2,1)S(1)}, u32[]{:S(2)}, u32[]{:S(2)}) collective-permute-start(bf16[128,1536]{1,0:T(8,128)(2,1)S(1)} %fusion.5), channel_id=1, source_target_pairs={{0,32},{32,0},{64,96},{96,64},{128,160},{160,128},{192,224},{224,1... | collective-permute-start | bytes 1179656 | tf_op jit(solution)/shard_map/ppermute | solution.py:44
  79.8 40.3 %collective-permute-start.24 = (bf16[4,4,32,1536]{3,2,1,0:T(8,128)(2,1)S(1)}, bf16[4,4,32,1536]{3,2,1,0:T(8,128)(2,1)}, u32[]{:S(2)}, u32[]{:S(2)}) collective-permute-start(bf16[4,4,32,1536]{3,2,1,0:T(8,128)(2,1)S(1)} %bitcast.110), channel_id=1, source_target_pairs={{0,1},{1,0},{2,3},{3,2},{4,5},{5,4},{6,7},{7,6},{8,9},{9,8},{10,11... | collective-permute-start | bytes 4718600 | tf_op jit(solution)/shard_map/ppermute | solution.py:28
  106.9 7.1 %collective-permute-start.25 = (f32[8,128]{0,1:T(8,128)S(1)}, f32[8,128]{0,1:T(8,128)S(1)}, u32[]{:S(2)}, u32[]{:S(2)}) collective-permute-start(f32[8,128]{0,1:T(8,128)S(1)} %iota.7), channel_id=1, source_target_pairs={{0,32},{32,0},{64,96},{96,64},{128,160},{160,128},{192,224},{224,1... | collective-permute-start | bytes 12296 | tf_op jit(solution)/shard_map/ppermute | solution.py:67
  117.3 5.1 %collective-permute-start.27 = (f32[8,128]{0,1:T(8,128)S(1)}, f32[8,128]{0,1:T(8,128)S(1)}, u32[]{:S(2)}, u32[]{:S(2)}) collective-permute-start(f32[8,128]{0,1:T(8,128)S(1)} %fusion.63), channel_id=1, source_target_pairs={{0,128},{32,160},{64,192},{96,224},{128,0},{160,32},{192,64},{224,... | collective-permute-start | bytes 12296 | tf_op jit(solution)/shard_map/ppermute | solution.py:67
  122.4 8.0 %collective-permute-start.28 = (f32[8,128]{0,1:T(8,128)S(1)}, f32[8,128]{0,1:T(8,128)S(1)}, u32[]{:S(2)}, u32[]{:S(2)}) collective-permute-start(f32[8,128]{0,1:T(8,128)S(1)} %max.26), channel_id=1, source_target_pairs={{0,1},{1,0},{2,3},{3,2},{4,5},{5,4},{6,7},{7,6},{8,9},{9,8},{10,11... | collective-permute-start | bytes 12296 | tf_op jit(solution)/shard_map/ppermute | solution.py:67
  128.7 12.5 %collective-permute-start.13 = (bf16[128,1536]{1,0:T(8,128)(2,1)S(1)}, bf16[128,1536]{1,0:T(8,128)(2,1)S(1)}, u32[]{:S(2)}, u32[]{:S(2)}) collective-permute-start(bf16[128,1536]{1,0:T(8,128)(2,1)S(1)} %bitcast.122), channel_id=1, source_target_pairs={{0,64},{32,96},{64,128},{96,160},{128,192},{160,224},{192,0},{224,... | collective-permute-start | bytes 1179656 | tf_op jit(solution)/shard_map/ppermute | solution.py:40
  132.4 18.1 %collective-permute-start.14 = (bf16[128,1536]{1,0:T(8,128)(2,1)S(1)}, bf16[128,1536]{1,0:T(8,128)(2,1)S(1)}, u32[]{:S(2)}, u32[]{:S(2)}) collective-permute-start(bf16[128,1536]{1,0:T(8,128)(2,1)S(1)} %bitcast.123), channel_id=1, source_target_pairs={{0,128},{32,160},{64,192},{96,224},{128,0},{160,32},{192,64},{224,... | collective-permute-start | bytes 1179656 | tf_op jit(solution)/shard_map/ppermute | solution.py:40
  135.0 17.1 %collective-permute-start.15 = (bf16[128,1536]{1,0:T(8,128)(2,1)S(1)}, bf16[128,1536]{1,0:T(8,128)(2,1)S(1)}, u32[]{:S(2)}, u32[]{:S(2)}) collective-permute-start(bf16[128,1536]{1,0:T(8,128)(2,1)S(1)} %bitcast.124), channel_id=1, source_target_pairs={{0,192},{32,224},{64,0},{96,32},{128,64},{160,96},{192,128},{224,1... | collective-permute-start | bytes 1179656 | tf_op jit(solution)/shard_map/ppermute | solution.py:40
  135.0 4.7 %collective-permute-start.30 = (f32[8,128]{0,1:T(8,128)S(1)}, f32[8,128]{0,1:T(8,128)S(1)}, u32[]{:S(2)}, u32[]{:S(2)}) collective-permute-start(f32[8,128]{0,1:T(8,128)S(1)} %max.28), channel_id=1, source_target_pairs={{0,4},{1,5},{2,6},{3,7},{4,0},{5,1},{6,2},{7,3},{8,12},{9,13},{10,... | collective-permute-start | bytes 12296 | tf_op jit(solution)/shard_map/ppermute | solution.py:67
  139.8 29.8 %collective-permute-start.31 = (f32[8,128]{0,1:T(8,128)S(1)}, f32[8,128]{0,1:T(8,128)S(1)}, u32[]{:S(2)}, u32[]{:S(2)}) collective-permute-start(f32[8,128]{0,1:T(8,128)S(1)} %max.29), channel_id=1, source_target_pairs={{0,8},{1,9},{2,10},{3,11},{4,12},{5,13},{6,14},{7,15},{8,0},{9,1},... | collective-permute-start | bytes 12296 | tf_op jit(solution)/shard_map/ppermute | solution.py:67
  153.8 18.3 %collective-permute-start.19 = (bf16[128,1536]{1,0:T(8,128)(2,1)S(1)}, bf16[128,1536]{1,0:T(8,128)(2,1)S(1)}, u32[]{:S(2)}, u32[]{:S(2)}) collective-permute-start(bf16[128,1536]{1,0:T(8,128)(2,1)S(1)} %convolution_convert_fusion.2), channel_id=1, source_target_pairs={{0,24},{1,25},{2,26},{3,27},{4,28},{5,29},{6,30},{7,31},{8,0},{9,1... | collective-permute-start | bytes 1179656 | tf_op jit(solution)/shard_map/ppermute | solution.py:36
  157.6 14.5 %collective-permute-start.18 = (bf16[128,1536]{1,0:T(8,128)(2,1)}, bf16[128,1536]{1,0:T(8,128)(2,1)S(1)}, u32[]{:S(2)}, u32[]{:S(2)}) collective-permute-start(bf16[128,1536]{1,0:T(8,128)(2,1)} %convolution_convert_fusion.3), channel_id=1, source_target_pairs={{0,8},{1,9},{2,10},{3,11},{4,12},{5,13},{6,14},{7,15},{8,16},{9,17... | collective-permute-start | bytes 1179656 | tf_op jit(solution)/shard_map/ppermute | solution.py:36
  160.3 17.5 %collective-permute-start.17 = (bf16[128,1536]{1,0:T(8,128)(2,1)}, bf16[128,1536]{1,0:T(8,128)(2,1)S(1)}, u32[]{:S(2)}, u32[]{:S(2)}) collective-permute-start(bf16[128,1536]{1,0:T(8,128)(2,1)} %convolution_convert_fusion.4), channel_id=1, source_target_pairs={{0,16},{1,17},{2,18},{3,19},{4,20},{5,21},{6,22},{7,23},{8,24},{9,... | collective-permute-start | bytes 1179656 | tf_op jit(solution)/shard_map/ppermute | solution.py:36
  169.6 13.5 %collective-permute-start.32 = (f32[8,128]{0,1:T(8,128)S(1)}, f32[8,128]{0,1:T(8,128)S(1)}, u32[]{:S(2)}, u32[]{:S(2)}) collective-permute-start(f32[8,128]{0,1:T(8,128)S(1)} %max.30), channel_id=1, source_target_pairs={{0,16},{1,17},{2,18},{3,19},{4,20},{5,21},{6,22},{7,23},{8,24},{9,... | collective-permute-start | bytes 12296 | tf_op jit(solution)/shard_map/ppermute | solution.py:67
  170.0 20.5 %collective-permute-start.23 = (bf16[4,4,32,768]{3,2,1,0:T(8,128)(2,1)S(1)}, bf16[4,4,32,768]{3,2,1,0:T(8,128)(2,1)S(1)}, u32[]{:S(2)}, u32[]{:S(2)}) collective-permute-start(bf16[4,4,32,768]{3,2,1,0:T(8,128)(2,1)S(1)} %slice.13), channel_id=1, source_target_pairs={{0,1},{1,0},{2,3},{3,2},{4,5},{5,4},{6,7},{7,6},{8,9},{9,8},{10,11... | collective-permute-start | bytes 2359304 | tf_op jit(solution)/shard_map/ppermute | solution.py:28
  179.5 5.5 %collective-permute-start.22 = (bf16[32,1536]{1,0:T(8,128)(2,1)S(1)}, bf16[32,1536]{1,0:T(8,128)(2,1)S(1)}, u32[]{:S(2)}, u32[]{:S(2)}) collective-permute-start(bf16[32,1536]{1,0:T(8,128)(2,1)S(1)} %get-tuple-element.19), channel_id=1, source_target_pairs={{0,6},{1,7},{2,4},{3,5},{4,2},{5,3},{6,0},{7,1},{8,14},{9,15},{10,... | collective-permute-start | bytes 294920 | tf_op jit(solution)/shard_map/ppermute | solution.py:32
  180.3 9.5 %collective-permute-start.21 = (bf16[32,1536]{1,0:T(8,128)(2,1)S(1)}, bf16[32,1536]{1,0:T(8,128)(2,1)S(1)}, u32[]{:S(2)}, u32[]{:S(2)}) collective-permute-start(bf16[32,1536]{1,0:T(8,128)(2,1)S(1)} %get-tuple-element.20), channel_id=1, source_target_pairs={{0,4},{1,5},{2,6},{3,7},{4,0},{5,1},{6,2},{7,3},{8,12},{9,13},{10,... | collective-permute-start | bytes 294920 | tf_op jit(solution)/shard_map/ppermute | solution.py:32
  181.7 8.1 %collective-permute-start.20 = (bf16[32,1536]{1,0:T(8,128)(2,1)S(1)}, bf16[32,1536]{1,0:T(8,128)(2,1)S(1)}, u32[]{:S(2)}, u32[]{:S(2)}) collective-permute-start(bf16[32,1536]{1,0:T(8,128)(2,1)S(1)} %get-tuple-element.18), channel_id=1, source_target_pairs={{0,2},{1,3},{2,0},{3,1},{4,6},{5,7},{6,4},{7,5},{8,10},{9,11},{10,... | collective-permute-start | bytes 294920 | tf_op jit(solution)/shard_map/ppermute | solution.py:32
  (11 other events, 114.3 us)
Sparse Core Ops, SparseCore 0:
  16.8 85.9 all-gather.4
  104.6 61.0 all-gather.2

commit v2 on v0

v2 whole, which is shorter than its diff:
```python
import math

import jax
import jax.numpy as jnp
from jax import lax
from jax.experimental import pallas as pl
from jax.experimental.pallas import tpu as pltpu
from jax.sharding import PartitionSpec as P

coef = math.sqrt(2.0 / math.pi)
f32, bf16 = jnp.float32, jnp.bfloat16
barrier = lax.optimization_barrier
D, FF, T = 1536, 768, 128
W = 2 * FF
B = 256


def gelu_value(pre):
    inner = coef * (pre + 0.044715 * pre * pre * pre)
    return 0.5 * pre * (1.0 + jnp.tanh(inner))


def gelu_slope(pre):
    inner = coef * (pre + 0.044715 * pre * pre * pre)
    tval = jnp.tanh(inner)
    return 0.5 * (1.0 + tval) + 0.5 * pre * (1.0 - tval * tval) * coef * (
        1.0 + 3.0 * 0.044715 * pre * pre
    )


def across(left, right):
    return lax.dot_general(left, right, (((1,), (1,)), ((), ())), preferred_element_type=f32)


def over_tokens(left, right):
    return lax.dot_general(left, right, (((0,), (0,)), ((), ())), preferred_element_type=f32)


def to_core(v):
    return lax.ppermute(v, "col", [(i, i ^ 1) for i in range(32)])


def to_l(v, k):
    return lax.ppermute(v, "col", [(i, i ^ (2 * k)) for i in range(32)])


def to_y(v, k):
    return lax.ppermute(v, "col", [(i, (i + 8 * k) % 32) for i in range(32)])


def to_x(v, k):
    return lax.ppermute(v, "row", [(i, (i + 2 * k) % 8) for i in range(8)])


def to_h(v):
    return lax.ppermute(v, "row", [(i, i ^ 1) for i in range(8)])


def pick(stacked, at):
    return lax.dynamic_index_in_dim(stacked, at % stacked.shape[0], 0, keepdims=False)


def ring(v, send):
    far, near, behind = send(v, 2), send(v, 3), send(v, 1)
    return [v, near, far, behind]


def put_tops(ref, top_h, top_y):
    row = lax.broadcasted_iota(jnp.int32, (ref.shape[0], 128), 0)
    high = top_h.astype(bf16).astype(f32)
    mid = (top_h - high).astype(bf16).astype(f32)
    low = top_h - high - mid
    extra = jnp.where(row == 0, high, jnp.where(row == 1, mid, jnp.where(row == 2, low, 0.0)))
    ref[:, D : D + 128] = jnp.where(row == 3, top_y, extra).astype(bf16)


def get_tops(refs):
    top_h = top_y = jnp.zeros((1, 128), f32)
    for ref in refs:
        extra = ref[0:16, D : D + 128].astype(f32)
        top_h = jnp.maximum(top_h, extra[0:1] + extra[1:2] + extra[2:3])
        top_y = jnp.maximum(top_y, extra[3:4])
    return top_h, top_y


def spots(shift, s):
    return (s - shift + 4) & 3


def back_kernel(t, g0, g1, g2, g3, wa, wb, own, p1, p2, p3, stacked, blocks):
    i = pl.program_id(0)

    @pl.when(i == 0)
    def _():
        for s, g in enumerate((g0, g1, g2, g3)):
            blocks[spots(t[0], s)] = g[...]
            stacked[s * T : (s + 1) * T] = g[...]

    def work(w):
        out = across(blocks[...].reshape(4 * T, D), w[...])
        at = pl.ds(pl.multiple_of(i * B, B), B)
        own[:, at] = out[:T]
        for k, p in enumerate((p1, p2, p3)):
            p[:, at] = out[(k + 1) * T : (k + 2) * T].astype(bf16)

    pl.when(i < FF // B)(lambda: work(wa))
    pl.when(i >= FF // B)(lambda: work(wb))


def sum_kernel(own, r1, r2, r3, tops, msg):
    for k in range(T // 16):
        at = slice(16 * k, 16 * (k + 1))
        total = own[at] + r1[at].astype(f32) + r2[at].astype(f32) + r3[at].astype(f32)
        msg[at, :W] = total.astype(bf16)
    put_tops(msg, jnp.zeros((1, 128), f32), tops[0:1])


def slope_kernel(mine, other, pre, msg):
    _, top_y = get_tops((mine, other))
    top = jnp.zeros((16, W), f32)
    for k in range(T // 16):
        at = slice(16 * k, 16 * (k + 1))
        back = mine[at, :W].astype(f32) + other[at, :W].astype(f32)
        hidden_grad = back * gelu_slope(pre[at].astype(f32))
        top = jnp.maximum(top, jnp.abs(hidden_grad))
        msg[at, :W] = hidden_grad.astype(bf16)
    top = jnp.max(top, axis=0, keepdims=True)
    top_h = top[:, :128]
    for k in range(1, W // 128):
        top_h = jnp.maximum(top_h, top[:, 128 * k : 128 * (k + 1)])
    put_tops(msg, top_h, top_y)


def grad_kernel(t, m0, m1, m2, m3, wa, wb, own, p1, p2, p3, qa, qb, blocks):
    i = pl.program_id(0)

    @pl.when(i == 0)
    def _():
        for s, m in enumerate((m0, m1, m2, m3)):
            blocks[spots(t[0], s)] = m[:, :W]
            qa[s * T : (s + 1) * T] = m[:, :FF]
            qb[s * T : (s + 1) * T] = m[:, FF:W]
        top_h, top_y = get_tops((m0, m1, m2, m3))
        for p in (p1, p2, p3):
            put_tops(p, top_h, top_y)

    hq = blocks[...].reshape(4 * T, W)
    out = across(hq[:, :FF], wa[...]) + across(hq[:, FF:], wb[...])
    at = pl.ds(pl.multiple_of(i * B, B), B)
    own[:, at] = out[:T]
    for k, p in enumerate((p1, p2, p3)):
        p[:, at] = out[(k + 1) * T : (k + 2) * T].astype(bf16)


def gather_kernel(own, r1, r2, r3, mine, kept, s1, s2, s3):
    top_h, top_y = get_tops((r1, r2, r3, mine))
    for m, out in enumerate((kept, s1, s2, s3)):
        at = slice(32 * m, 32 * (m + 1))
        total = own[at] + r1[at, :D].astype(f32) + r2[at, :D].astype(f32) + r3[at, :D].astype(f32)
        out[:, :D] = total.astype(out.dtype)
    for out in (s1, s2, s3):
        put_tops(out, top_h, top_y)


def last_kernel(kept, r1, r2, r3, mine, out, tops):
    top_h, top_y = get_tops((r1, r2, r3, mine))
    total = kept[...] + r1[:, :D].astype(f32) + r2[:, :D].astype(f32) + r3[:, :D].astype(f32)
    out[...] = total.astype(bf16)
    row = lax.broadcasted_iota(jnp.int32, (8, 128), 0)
    tops[...] = jnp.where(row == 0, top_y, jnp.where(row == 1, top_h, 0.0))


def w_out_kernel(t, r0, r1, r2, r3, mine, other, out, hidden):
    @pl.when(pl.program_id(0) == 0)
    def _():
        for s, r in enumerate((r0, r1, r2, r3)):
            k = spots(t[0], s)
            for c in range(2):
                hidden[c, k] = gelu_value(r[c].astype(f32)).astype(bf16)

    half = hidden[...].reshape(2, 4 * T, FF)
    out[...] = (over_tokens(half[0], mine[...]) + over_tokens(half[1], other[...])).astype(bf16)


def w_in_kernel(at, inputs, mine, other, out, hq):
    @pl.when(pl.program_id(0) == 0)
    def _():
        x, l, c = at[0], at[1], at[2]
        for k in range(4):
            for m in range(4):
                rows = slice(k * T + m * 32, k * T + (m + 1) * 32)
                to = ((x + k) & 3) * 4 + (l ^ m)
                hq[to, c] = mine[rows]
                hq[to, 1 - c] = other[rows]

    out[...] = over_tokens(inputs[...], hq[...].reshape(8 * T, FF)).astype(bf16)


def like(*shape, dtype=bf16):
    return jax.ShapeDtypeStruct(shape, dtype)


def call(kernel, name, outs, args, flops=0, **spec):
    outs = list(outs)
    size = sum(math.prod(a.shape) * a.dtype.itemsize for a in list(args) + outs)
    return pl.pallas_call(
        kernel,
        out_shape=outs,
        name=name,
        compiler_params=pltpu.CompilerParams(vmem_limit_bytes=30 * 2**20),
        cost_estimate=pl.CostEstimate(flops=flops, bytes_accessed=size, transcendentals=0),
        **spec,
    )(*args)


def whole(a):
    zeros = (0,) * len(a.shape)
    return pl.BlockSpec(a.shape, lambda i, t: zeros)


def local(inputs, preact, w_in, w_out, out_grad):
    row, col = lax.axis_index("row"), lax.axis_index("col")
    x, h = row // 2, row % 2
    y, l, c = col // 8, (col // 2) % 4, col % 2
    steps = D // B
    big = 2 * 4 * T * D * W

    grad = jnp.stack([out_grad] + [to_l(out_grad, k) for k in (1, 2, 3)]).reshape(T, D)
    w_out_o = to_core(w_out)
    top_y = jnp.broadcast_to(jnp.max(jnp.abs(out_grad)).astype(f32), (8, 128))
    grad, preact, w_in_late = barrier((grad, preact, w_in))
    grads = ring(grad, to_y)

    pre = preact.reshape(2, 2, 32, FF)
    theirs = to_h(preact).reshape(2, 2, 32, FF)
    pre = jnp.stack([jnp.where(h == 0, pre, theirs), jnp.where(h == 0, theirs, pre)])
    pre = barrier(pre.reshape(4, 2, 32, FF))
    pre = jnp.stack([pick(pre, l ^ m) for m in range(4)])
    pre = jnp.stack([jnp.where(c == 0, pre[:, 0], pre[:, 1]), jnp.where(c == 0, pre[:, 1], pre[:, 0])])
    pre = barrier(pre.reshape(2, T, FF))
    pre_mine = barrier(jnp.concatenate([pre[0], to_core(pre[1])], axis=1))
    w_in_o = to_core(w_in_late)

    *grads, inputs = barrier((*grads, inputs))
    inputs_all = lax.all_gather(inputs, "col", axis=0, tiled=True)

    args = (jnp.reshape((x - y) & 3, (1,)).astype(jnp.int32), *grads, w_out, w_out_o)
    outs = [like(T, W, dtype=f32)] + [like(T, W)] * 3 + [like(4 * T, D)]
    last = FF // B - 1
    own, p1, p2, p3, stacked = call(
        back_kernel,
        "back",
        outs,
        args,
        big,
        grid_spec=pltpu.PrefetchScalarGridSpec(
            num_scalar_prefetch=1,
            grid=(W // B,),
            in_specs=[whole(g) for g in grads]
            + [
                pl.BlockSpec((B, D), lambda i, t: (jnp.minimum(i, last), 0)),
                pl.BlockSpec((B, D), lambda i, t: (jnp.maximum(i - last - 1, 0), 0)),
            ],
            out_specs=[whole(o) for o in outs],
            scratch_shapes=[pltpu.VMEM((4, T, D), bf16)],
        ),
    )
    r2, r1, r3 = to_x(p2, 2), to_x(p1, 1), to_x(p3, 3)
    (sent,) = call(sum_kernel, "back_sum", [like(T, W + 128)], (own, r1, r2, r3, top_y))
    other = to_h(sent)
    pre, sent = barrier((pre, sent))
    pres = ring(pre, to_x)
    stacked_o = to_core(stacked)
    (msg,) = call(slope_kernel, "slope", [like(T, W + 128)], (sent, other, pre_mine))
    msgs = ring(msg, to_x)

    turn = jnp.reshape((y - x) & 3, (1,)).astype(jnp.int32)
    args = (turn, *pres, stacked, stacked_o)
    outs = [like(FF, D)]
    (w_out_grad,) = call(
        w_out_kernel,
        "w_out_grad",
        outs,
        args,
        big,
        grid_spec=pltpu.PrefetchScalarGridSpec(
            num_scalar_prefetch=1,
            grid=(steps,),
            in_specs=[whole(p) for p in pres] + [pl.BlockSpec((4 * T, B), lambda i, t: (0, i))] * 2,
            out_specs=[pl.BlockSpec((FF, B), lambda i, t: (0, i))],
            scratch_shapes=[pltpu.VMEM((2, 4, T, FF), bf16)],
        ),
    )
    *far, w_out_grad = barrier((*msgs[1:], w_out_grad))
    msgs = [msgs[0], *far]

    args = (turn, *msgs, w_in, w_in_o)
    outs = [like(T, D, dtype=f32)] + [like(T, D + 128)] * 3 + [like(4 * T, FF)] * 2
    own, p1, p2, p3, hq_a, hq_b = call(
        grad_kernel,
        "input_grad",
        outs,
        args,
        big,
        grid_spec=pltpu.PrefetchScalarGridSpec(
            num_scalar_prefetch=1,
            grid=(steps,),
            in_specs=[whole(m) for m in msgs] + [pl.BlockSpec((B, FF), lambda i, t: (i, 0))] * 2,
            out_specs=[whole(o) for o in outs],
            scratch_shapes=[pltpu.VMEM((4, T, W), bf16)],
        ),
    )
    r2, r1, r3 = to_y(p2, 2), to_y(p1, 1), to_y(p3, 3)
    hq_b = to_core(hq_b)
    outs = [like(D, FF)]
    (w_in_grad,) = call(
        w_in_kernel,
        "w_in_grad",
        outs,
        (jnp.stack([x, l, c]).astype(jnp.int32), inputs_all, hq_a, hq_b),
        big,
        grid_spec=pltpu.PrefetchScalarGridSpec(
            num_scalar_prefetch=1,
            grid=(steps,),
            in_specs=[pl.BlockSpec((8 * T, B), lambda i, t: (0, i)), whole(hq_a), whole(hq_b)],
            out_specs=[pl.BlockSpec((B, FF), lambda i, t: (i, 0))],
            scratch_shapes=[pltpu.VMEM((16, 2, 32, FF), bf16)],
        ),
    )
    r1, r2, r3, w_in_grad = barrier((r1, r2, r3, w_in_grad))
    outs = [like(32, D, dtype=f32)] + [like(32, D + 128)] * 3
    kept, s1, s2, s3 = call(gather_kernel, "y_sum", outs, (own, r1, r2, r3, p1))
    r2, r3, r1 = to_l(s2, 2), to_l(s3, 3), to_l(s1, 1)
    outs = [like(32, D), like(8, 128, dtype=f32)]
    input_grad, tops = call(last_kernel, "l_sum", outs, (kept, r1, r2, r3, s1))
    amaxes = jnp.max(jnp.maximum(tops, to_core(tops)), axis=1)[:2]
    return (input_grad, w_in_grad, w_out_grad, amaxes)


def solution(mesh):
    placed = (P("col", "row"), P("row", "col"), P("row", "col"), P("col", "row"), P("col", "row"))
    return jax.shard_map(
        local,
        mesh=mesh,
        in_specs=placed,
        out_specs=(P("col", "row"), P("row", "col"), P("col", "row"), P()),
        check_vma=False,
    )
```

time: 640 us -> 208 us (0.33)
  waiting for transfers between devices: 426 us -> 86.4 us
  blocking collectives: 157 us -> 0 us
  starting transfers between devices: 0.24 us -> 60.5 us
  Pallas kernels: 0 us -> 28.8 us
  matrix products: 25.8 us -> 0 us
  local copies, waits for them, and re-layouts: 4.28 us -> 12.5 us
    reduce_scatter x2 -> x0, waiting for transfers between devices: 253 us -> none  [the longest x1 148 us: local(): lax.psum_scatter(partial_terms, 'col', scatter_dimension=0, tiled=True)]
    all_gather x4 -> x1, waiting for transfers between devices: 171 us -> 0.01 us  [local(): inputs_all = lax.all_gather(inputs, 'col', axis=0, tiled=True)]
    pmax x2 -> x0, blocking collectives: 157 us -> none  [the longest x1 81.4 us: local(): lax.pmax(jnp.max(jnp.abs(out_grad.astype(jnp.float32))), ('row', 'col'))]
    ppermute x0 -> x29, waiting for transfers between devices: none -> 86.3 us  [the longest x6 30.9 us: to_y(): return lax.ppermute(v, 'col', [(i, (i + 8 * k) % 32) for i in range(32)])]
    ppermute x0 -> x29, starting transfers between devices: none -> 60.4 us  [the longest x6 22.9 us: to_l(): return lax.ppermute(v, 'col', [(i, i ^ 2 * k) for i in range(32)])]
    pallas_call x0 -> x8, Pallas kernels: none -> 28.8 us  [call(): pl.pallas_call(kernel, out_shape=outs, name=name, compiler_params=pltpu.C...]
    dot_general x4 -> x0, matrix products: 25.8 us -> none  [the longest x2 13 us: contract_last(): lax.dot_general(left, right, (((1,), (1,)), ((), ())), preferred_element_...]
    unnamed x5 -> x30, local copies, waits for them, and re-layouts: 4.28 us -> 11.7 us
  transfers between devices with their start and end apart: 6 -> 30, of which waited for: 5 -> 16; matrix products, arithmetic and copies ran while one was open for 4% -> 2% of each run, Pallas kernels for 0% -> 14%
where the time goes in v2:
time: 208 us; the launch traced here: 207 us
  waiting for transfers between devices  86.4 us (42%)
  starting transfers between devices  60.5 us (29%)
  Pallas kernels  28.8 us (14%)
  between operations  14.2 us (7%)
  local copies, waits for them, and re-layouts  12.5 us (6%)
  other arithmetic  4.52 us (2%)
    ppermute x6, waiting for transfers between devices, to_y(): return lax.ppermute(v, 'col', [(i, (i + 8 * k) % 32) for i in range(32)])  30.9 us
    pallas_call x8, Pallas kernels, call(): pl.pallas_call(kernel, out_shape=outs, name=name, compiler_params=pltpu.C...  28.8 us
    ppermute x9, waiting for transfers between devices, to_x(): return lax.ppermute(v, 'row', [(i, (i + 2 * k) % 8) for i in range(8)])  25.7 us
    ppermute x6, starting transfers between devices, to_l(): return lax.ppermute(v, 'col', [(i, i ^ 2 * k) for i in range(32)])  22.9 us
    ppermute x6, waiting for transfers between devices, to_l(): return lax.ppermute(v, 'col', [(i, i ^ 2 * k) for i in range(32)])  14.5 us
    ppermute x2, waiting for transfers between devices, to_h(): return lax.ppermute(v, 'row', [(i, i ^ 1) for i in range(8)])  13.4 us
    ppermute x6, starting transfers between devices, to_core(): return lax.ppermute(v, 'col', [(i, i ^ 1) for i in range(32)])  12.7 us
    unnamed x30, local copies, waits for them, and re-layouts  11.7 us
  transfers between devices with their start and end apart: 30, of which 16 were waited for; matrix products, arithmetic and copies ran while one was open for 2% of the time, Pallas kernels for 14%

profile of v2, /device:TPU:1, one launch (start us, length us, event | category | flops | bytes accessed | tf_op | source)
XLA Modules:
  0.0 206.9 jit_solution(3833425186106251038)
XLA Ops:
  7.2 2.6 %collective-permute-start = (bf16[32,1536]{1,0:T(8,128)(2,1)}, bf16[32,1536]{1,0:T(8,128)(2,1)S(1)}, u32[]{:S(2)}, u32[]{:S(2)}) collective-permute-start(bf16[32,1536]{1,0:T(8,128)(2,1)} %param.9), channel_id=1, source_target_pairs={{0,2},{1,3},{2,0},{3,1},{4,6},{5,7},{6,4},{7,5},{8,10},{9,11},{10,... | collective-permute-start | bytes 294920 | tf_op jit(solution)/shard_map/ppermute | solution.py:44
  9.8 3.0 %collective-permute-start.1 = (bf16[32,1536]{1,0:T(8,128)(2,1)}, bf16[32,1536]{1,0:T(8,128)(2,1)S(1)}, u32[]{:S(2)}, u32[]{:S(2)}) collective-permute-start(bf16[32,1536]{1,0:T(8,128)(2,1)} %param.9), channel_id=1, source_target_pairs={{0,4},{1,5},{2,6},{3,7},{4,0},{5,1},{6,2},{7,3},{8,12},{9,13},{10,... | collective-permute-start | bytes 294920 | tf_op jit(solution)/shard_map/ppermute | solution.py:44
  12.8 2.8 %collective-permute-done.1 = bf16[32,1536]{1,0:T(8,128)(2,1)S(1)} collective-permute-done((bf16[32,1536]{1,0:T(8,128)(2,1)}, bf16[32,1536]{1,0:T(8,128)(2,1)S(1)}, u32[]{:S(2)}, u32[]{:S(2)}) %collective-permute-start.1) | collective-permute-done | bytes 98336 | tf_op jit(solution)/shard_map/ppermute | solution.py:44
  15.6 3.7 %collective-permute-done.2 = bf16[32,1536]{1,0:T(8,128)(2,1)S(1)} collective-permute-done((bf16[32,1536]{1,0:T(8,128)(2,1)}, bf16[32,1536]{1,0:T(8,128)(2,1)S(1)}, u32[]{:S(2)}, u32[]{:S(2)}) %collective-permute-start.2) | collective-permute-done | bytes 98336 | tf_op jit(solution)/shard_map/ppermute | solution.py:44
  20.2 2.8 %collective-permute-start.4 = (bf16[128,1536]{1,0:T(8,128)(2,1)S(1)}, bf16[128,1536]{1,0:T(8,128)(2,1)S(1)}, u32[]{:S(2)}, u32[]{:S(2)}) collective-permute-start(bf16[128,1536]{1,0:T(8,128)(2,1)S(1)} %bitcast.20), channel_id=1, source_target_pairs={{0,24},{1,25},{2,26},{3,27},{4,28},{5,29},{6,30},{7,31},{8,0},{9,1... | collective-permute-start | bytes 1179656 | tf_op jit(solution)/shard_map/ppermute | solution.py:48
  24.1 5.7 %collective-permute-done.4.g1 = bf16[128,1536]{1,0:T(8,128)(2,1)S(1)} collective-permute-done((bf16[128,1536]{1,0:T(8,128)(2,1)S(1)}, bf16[128,1536]{1,0:T(8,128)(2,1)S(1)}, u32[]{:S(2)}, u32[]{:S(2)}) %collective-permute-start.4) | collective-permute-done | bytes 393248 | tf_op jit(solution)/shard_map/ppermute | solution.py:48
  29.8 2.5 %collective-permute-done.5.g2 = bf16[128,1536]{1,0:T(8,128)(2,1)S(1)} collective-permute-done((bf16[128,1536]{1,0:T(8,128)(2,1)S(1)}, bf16[128,1536]{1,0:T(8,128)(2,1)S(1)}, u32[]{:S(2)}, u32[]{:S(2)}) %collective-permute-start.5) | collective-permute-done | bytes 393248 | tf_op jit(solution)/shard_map/ppermute | solution.py:48
  32.2 11.8 %collective-permute-done.6.g3 = bf16[128,1536]{1,0:T(8,128)(2,1)S(1)} collective-permute-done((bf16[128,1536]{1,0:T(8,128)(2,1)S(1)}, bf16[128,1536]{1,0:T(8,128)(2,1)S(1)}, u32[]{:S(2)}, u32[]{:S(2)}) %collective-permute-start.6) | collective-permute-done | bytes 393248 | tf_op jit(solution)/shard_map/ppermute | solution.py:48
  45.3 5.1 %collective-permute-start.3 = (bf16[128,768]{1,0:T(8,128)(2,1)}, bf16[128,768]{1,0:T(8,128)(2,1)}, u32[]{:S(2)}, u32[]{:S(2)}) collective-permute-start(bf16[128,768]{1,0:T(8,128)(2,1)} %param.6), channel_id=1, source_target_pairs={{0,32},{32,0},{64,96},{96,64},{128,160},{160,128},{192,224},{224,1... | collective-permute-start | bytes 589832 | tf_op jit(solution)/shard_map/ppermute | solution.py:56
  50.4 1.6 abs_reduce_fusion
  52.4 3.6 %collective-permute-done.3 = bf16[128,768]{1,0:T(8,128)(2,1)} collective-permute-done((bf16[128,768]{1,0:T(8,128)(2,1)}, bf16[128,768]{1,0:T(8,128)(2,1)}, u32[]{:S(2)}, u32[]{:S(2)}) %collective-permute-start.3) | collective-permute-done | bytes 196640 | tf_op jit(solution)/shard_map/ppermute | solution.py:56
  57.2 6.8 %back.1 = (f32[128,1536]{1,0:T(8,128)S(1)}, bf16[128,1536]{1,0:T(8,128)(2,1)S(1)}, bf16[128,1536]{1,0:T(8,128)(2,1)S(1)}, bf16[128,1536]{1,0:T(8,128)(2,1)S(1)}, bf16[512,1536]{1,0:T(8,128)(2,1)}) custom-call(s32[1]{0:T(128)} %bitcast.11.t, bf16[128,1536]{1,0:T(8,128)(2,1)S(1)} %bitcast.23, bf16[128,1536]{1,0:T(8,128)(2,1)S(1)} %collective-permute-done.4.g1, ...), custom_call_target="tpu_custom_call" | custom-call | flops 2415919104 | bytes 9830404 | tf_op jit(solution)/shard_map/back/pallas_call | solution.py:206
  65.1 2.5 %collective-permute-start.10 = (bf16[128,1536]{1,0:T(8,128)(2,1)S(1)}, bf16[128,1536]{1,0:T(8,128)(2,1)S(1)}, u32[]{:S(2)}, u32[]{:S(2)}) collective-permute-start(bf16[128,1536]{1,0:T(8,128)(2,1)S(1)} %get-tuple-element.48), channel_id=1, source_target_pairs={{0,192},{32,224},{64,0},{96,32},{128,64},{160,96},{192,128},{224,1... | collective-permute-start | bytes 1179656 | tf_op jit(solution)/shard_map/ppermute | solution.py:52
  67.6 1.7 collective-permute-start.9
  69.5 15.0 %collective-permute-done.10.r3 = bf16[128,1536]{1,0:T(8,128)(2,1)S(1)} collective-permute-done((bf16[128,1536]{1,0:T(8,128)(2,1)S(1)}, bf16[128,1536]{1,0:T(8,128)(2,1)S(1)}, u32[]{:S(2)}, u32[]{:S(2)}) %collective-permute-start.10) | collective-permute-done | bytes 393248 | tf_op jit(solution)/shard_map/ppermute | solution.py:52
  84.4 3.2 %collective-permute-done.8.r1 = bf16[128,1536]{1,0:T(8,128)(2,1)S(1)} collective-permute-done((bf16[128,1536]{1,0:T(8,128)(2,1)S(1)}, bf16[128,1536]{1,0:T(8,128)(2,1)S(1)}, u32[]{:S(2)}, u32[]{:S(2)}) %collective-permute-start.8) | collective-permute-done | bytes 393248 | tf_op jit(solution)/shard_map/ppermute | solution.py:52
  88.6 5.1 %collective-permute-start.11 = (bf16[128,1664]{1,0:T(8,128)(2,1)S(1)}, bf16[128,1664]{1,0:T(8,128)(2,1)S(1)}, u32[]{:S(2)}, u32[]{:S(2)}) collective-permute-start(bf16[128,1664]{1,0:T(8,128)(2,1)S(1)} %back_sum.1.mine), channel_id=1, source_target_pairs={{0,32},{32,0},{64,96},{96,64},{128,160},{160,128},{192,224},{224,1... | collective-permute-start | bytes 1277960 | tf_op jit(solution)/shard_map/ppermute | solution.py:56
  93.7 1.5 collective-permute-start.12
  96.5 9.7 %collective-permute-done.11.other = bf16[128,1664]{1,0:T(8,128)(2,1)S(1)} collective-permute-done((bf16[128,1664]{1,0:T(8,128)(2,1)S(1)}, bf16[128,1664]{1,0:T(8,128)(2,1)S(1)}, u32[]{:S(2)}, u32[]{:S(2)}) %collective-permute-start.11) | collective-permute-done | bytes 426016 | tf_op jit(solution)/shard_map/ppermute | solution.py:56
  107.7 2.7 %collective-permute-start.13 = (bf16[128,1664]{1,0:T(8,128)(2,1)S(1)}, bf16[128,1664]{1,0:T(8,128)(2,1)S(1)}, u32[]{:S(2)}, u32[]{:S(2)}) collective-permute-start(bf16[128,1664]{1,0:T(8,128)(2,1)S(1)} %slope.1.m0), channel_id=1, source_target_pairs={{0,192},{32,224},{64,0},{96,32},{128,64},{160,96},{192,128},{224,1... | collective-permute-start | bytes 1277960 | tf_op jit(solution)/shard_map/ppermute | solution.py:52
  111.4 6.0 %collective-permute-done.18.r3 = bf16[2,128,768]{2,1,0:T(8,128)(2,1)S(1)} collective-permute-done((bf16[2,128,768]{2,1,0:T(8,128)(2,1)S(1)}, bf16[2,128,768]{2,1,0:T(8,128)(2,1)S(1)}, u32[]{:S(2)}, u32[]{:S(2)}) %collective-permute-start.18) | collective-permute-done | bytes 393248 | tf_op jit(solution)/shard_map/ppermute | solution.py:52
  121.8 8.0 %w_out_grad.1 = bf16[768,1536]{1,0:T(8,128)(2,1)} custom-call(s32[1]{0:T(128)} %bitcast.t, bf16[2,128,768]{2,1,0:T(8,128)(2,1)S(1)} %pad_maximum_fusion.3.r0, bf16[2,128,768]{2,1,0:T(8,128)(2,1)S(1)} %copy-done.8, bf16[2,128,768]{2,1,0:T(8,128)(2,1)S(1)} %copy-done.10, bf16[2,128,768]{2,1,0:T(8,128)(2,1)S(1)} %copy-done.12, ...), custom_call_target="tpu_custom_call" | custom-call | flops 2415919104 | bytes 7077892 | tf_op jit(solution)/shard_map/w_out_grad/pallas_call | solution.py:206
  130.6 1.5 collective-permute-done.15.m3
  133.1 6.7 %input_grad.1 = (f32[128,1536]{1,0:T(8,128)S(1)}, bf16[128,1664]{1,0:T(8,128)(2,1)S(1)}, bf16[128,1664]{1,0:T(8,128)(2,1)}, bf16[128,1664]{1,0:T(8,128)(2,1)}, b...) custom-call(s32[1]{0:T(128)} %bitcast.t, bf16[128,1664]{1,0:T(8,128)(2,1)S(1)} %slope.1.m0, ...), custom_call_target="tpu_custom_call" | custom-call | flops 2415919104 | bytes 10059780 | tf_op jit(solution)/shard_map/input_grad/pallas_call | solution.py:206
  140.7 8.7 %collective-permute-start.24 = (bf16[512,768]{1,0:T(8,128)(2,1)S(1)}, bf16[512,768]{1,0:T(8,128)(2,1)S(1)}, u32[]{:S(2)}, u32[]{:S(2)}) collective-permute-start(bf16[512,768]{1,0:T(8,128)(2,1)S(1)} %get-tuple-element.62), channel_id=1, source_target_pairs={{0,1},{1,0},{2,3},{3,2},{4,5},{5,4},{6,7},{7,6},{8,9},{9,8},{10,11... | collective-permute-start | bytes 2359304 | tf_op jit(solution)/shard_map/ppermute | solution.py:40
  149.5 2.7 %collective-permute-start.23 = (bf16[128,1664]{1,0:T(8,128)(2,1)}, bf16[128,1664]{1,0:T(8,128)(2,1)S(1)}, u32[]{:S(2)}, u32[]{:S(2)}) collective-permute-start(bf16[128,1664]{1,0:T(8,128)(2,1)} %get-tuple-element.59), channel_id=1, source_target_pairs={{0,24},{1,25},{2,26},{3,27},{4,28},{5,29},{6,30},{7,31},{8,0},{9,1... | collective-permute-start | bytes 1277960 | tf_op jit(solution)/shard_map/ppermute | solution.py:48
  152.2 1.9 copy-done
  155.2 5.6 %w_in_grad.1 = bf16[1536,768]{1,0:T(8,128)(2,1)} custom-call(s32[3]{0:T(128)S(1)} %pad_add_fusion.at, bf16[1024,1536]{1,0:T(8,128)(2,1)S(1)} %copy-done, bf16[512,768]{1,0:T(8,128)(2,1)S(1)} %copy-done.14, bf16[512,768]{1,0:T(8,128)(2,1)S(1)} %collective-permute-done.24.other), custom_call_target="tpu_custom_call" | custom-call | flops 2415919104 | bytes 7077900 | tf_op jit(solution)/shard_map/w_in_grad/pallas_call | solution.py:206
  160.8 10.4 %collective-permute-done.21.r1 = bf16[128,1664]{1,0:T(8,128)(2,1)S(1)} collective-permute-done((bf16[128,1664]{1,0:T(8,128)(2,1)S(1)}, bf16[128,1664]{1,0:T(8,128)(2,1)S(1)}, u32[]{:S(2)}, u32[]{:S(2)}) %collective-permute-start.21) | collective-permute-done | bytes 426016 | tf_op jit(solution)/shard_map/ppermute | solution.py:48
  171.9 15.2 %collective-permute-start.25 = (bf16[32,1664]{1,0:T(8,128)(2,1)S(1)}, bf16[32,1664]{1,0:T(8,128)(2,1)S(1)}, u32[]{:S(2)}, u32[]{:S(2)}) collective-permute-start(bf16[32,1664]{1,0:T(8,128)(2,1)S(1)} %get-tuple-element.67.mine), channel_id=1, source_target_pairs={{0,2},{1,3},{2,0},{3,1},{4,6},{5,7},{6,4},{7,5},{8,10},{9,11},{10,... | collective-permute-start | bytes 319496 | tf_op jit(solution)/shard_map/ppermute | solution.py:44
  187.1 2.2 %collective-permute-start.27 = (bf16[32,1664]{1,0:T(8,128)(2,1)S(1)}, bf16[32,1664]{1,0:T(8,128)(2,1)S(1)}, u32[]{:S(2)}, u32[]{:S(2)}) collective-permute-start(bf16[32,1664]{1,0:T(8,128)(2,1)S(1)} %get-tuple-element.69), channel_id=1, source_target_pairs={{0,6},{1,7},{2,4},{3,5},{4,2},{5,3},{6,0},{7,1},{8,14},{9,15},{10,... | collective-permute-start | bytes 319496 | tf_op jit(solution)/shard_map/ppermute | solution.py:44
  189.3 8.0 %collective-permute-done.26.r2 = bf16[32,1664]{1,0:T(8,128)(2,1)S(1)} collective-permute-done((bf16[32,1664]{1,0:T(8,128)(2,1)S(1)}, bf16[32,1664]{1,0:T(8,128)(2,1)S(1)}, u32[]{:S(2)}, u32[]{:S(2)}) %collective-permute-start.26) | collective-permute-done | bytes 106528 | tf_op jit(solution)/shard_map/ppermute | solution.py:44
  (81 shorter events, 22.5 us)
Async XLA Ops:
  7.2 50.0 %copy-start.1 = (bf16[768,1536]{1,0:T(8,128)(2,1)S(1)}, bf16[768,1536]{1,0:T(8,128)(2,1)}, u32[]{:S(2)}) copy-start(bf16[768,1536]{1,0:T(8,128)(2,1)} %wa.2) | copy-start | bytes 7077892
  7.2 145.0 %all-gather.2.cloned.1.call-start = ((), (), s32[]{:S(2)}) async-start(), calls=%async_computation | async-start | bytes 3244032 | tf_op jit(solution)/shard_map/all_gather | solution.py:245
  7.2 5.6 %collective-permute-start = (bf16[32,1536]{1,0:T(8,128)(2,1)}, bf16[32,1536]{1,0:T(8,128)(2,1)S(1)}, u32[]{:S(2)}, u32[]{:S(2)}) collective-permute-start(bf16[32,1536]{1,0:T(8,128)(2,1)} %param.9), channel_id=1, source_target_pairs={{0,2},{1,3},{2,0},{3,1},{4,6},{5,7},{6,4},{7,5},{8,10},{9,11},{10,... | collective-permute-start | bytes 294920 | tf_op jit(solution)/shard_map/ppermute | solution.py:44
  9.8 5.8 %collective-permute-start.1 = (bf16[32,1536]{1,0:T(8,128)(2,1)}, bf16[32,1536]{1,0:T(8,128)(2,1)S(1)}, u32[]{:S(2)}, u32[]{:S(2)}) collective-permute-start(bf16[32,1536]{1,0:T(8,128)(2,1)} %param.9), channel_id=1, source_target_pairs={{0,4},{1,5},{2,6},{3,7},{4,0},{5,1},{6,2},{7,3},{8,12},{9,13},{10,... | collective-permute-start | bytes 294920 | tf_op jit(solution)/shard_map/ppermute | solution.py:44
  12.8 6.5 %collective-permute-start.2 = (bf16[32,1536]{1,0:T(8,128)(2,1)}, bf16[32,1536]{1,0:T(8,128)(2,1)S(1)}, u32[]{:S(2)}, u32[]{:S(2)}) collective-permute-start(bf16[32,1536]{1,0:T(8,128)(2,1)} %param.9), channel_id=1, source_target_pairs={{0,6},{1,7},{2,4},{3,5},{4,2},{5,3},{6,0},{7,1},{8,14},{9,15},{10,... | collective-permute-start | bytes 294920 | tf_op jit(solution)/shard_map/ppermute | solution.py:44
  20.2 9.6 %collective-permute-start.4 = (bf16[128,1536]{1,0:T(8,128)(2,1)S(1)}, bf16[128,1536]{1,0:T(8,128)(2,1)S(1)}, u32[]{:S(2)}, u32[]{:S(2)}) collective-permute-start(bf16[128,1536]{1,0:T(8,128)(2,1)S(1)} %bitcast.20), channel_id=1, source_target_pairs={{0,24},{1,25},{2,26},{3,27},{4,28},{5,29},{6,30},{7,31},{8,0},{9,1... | collective-permute-start | bytes 1179656 | tf_op jit(solution)/shard_map/ppermute | solution.py:48
  23.0 9.2 %collective-permute-start.5 = (bf16[128,1536]{1,0:T(8,128)(2,1)S(1)}, bf16[128,1536]{1,0:T(8,128)(2,1)S(1)}, u32[]{:S(2)}, u32[]{:S(2)}) collective-permute-start(bf16[128,1536]{1,0:T(8,128)(2,1)S(1)} %bitcast.21), channel_id=1, source_target_pairs={{0,16},{1,17},{2,18},{3,19},{4,20},{5,21},{6,22},{7,23},{8,24},{9,... | collective-permute-start | bytes 1179656 | tf_op jit(solution)/shard_map/ppermute | solution.py:48
  23.4 20.6 %collective-permute-start.6 = (bf16[128,1536]{1,0:T(8,128)(2,1)S(1)}, bf16[128,1536]{1,0:T(8,128)(2,1)S(1)}, u32[]{:S(2)}, u32[]{:S(2)}) collective-permute-start(bf16[128,1536]{1,0:T(8,128)(2,1)S(1)} %bitcast.22), channel_id=1, source_target_pairs={{0,8},{1,9},{2,10},{3,11},{4,12},{5,13},{6,14},{7,15},{8,16},{9,17... | collective-permute-start | bytes 1179656 | tf_op jit(solution)/shard_map/ppermute | solution.py:48
  44.8 12.4 %collective-permute-start.7 = (bf16[768,1536]{1,0:T(8,128)(2,1)}, bf16[768,1536]{1,0:T(8,128)(2,1)}, u32[]{:S(2)}, u32[]{:S(2)}) collective-permute-start(bf16[768,1536]{1,0:T(8,128)(2,1)} %wa.2), channel_id=1, source_target_pairs={{0,1},{1,0},{2,3},{3,2},{4,5},{5,4},{6,7},{7,6},{8,9},{9,8},{10,11... | collective-permute-start | bytes 7077896 | tf_op jit(solution)/shard_map/ppermute | solution.py:40
  45.3 10.7 %collective-permute-start.3 = (bf16[128,768]{1,0:T(8,128)(2,1)}, bf16[128,768]{1,0:T(8,128)(2,1)}, u32[]{:S(2)}, u32[]{:S(2)}) collective-permute-start(bf16[128,768]{1,0:T(8,128)(2,1)} %param.6), channel_id=1, source_target_pairs={{0,32},{32,0},{64,96},{96,64},{128,160},{160,128},{192,224},{224,1... | collective-permute-start | bytes 589832 | tf_op jit(solution)/shard_map/ppermute | solution.py:56
  52.1 80.1 %collective-permute-start.20 = (bf16[1536,768]{1,0:T(8,128)(2,1)}, bf16[1536,768]{1,0:T(8,128)(2,1)}, u32[]{:S(2)}, u32[]{:S(2)}) collective-permute-start(bf16[1536,768]{1,0:T(8,128)(2,1)} %wa.3), channel_id=1, source_target_pairs={{0,1},{1,0},{2,3},{3,2},{4,5},{5,4},{6,7},{7,6},{8,9},{9,8},{10,11... | collective-permute-start | bytes 7077896 | tf_op jit(solution)/shard_map/ppermute | solution.py:40
  64.0 54.8 %collective-permute-start.19 = (bf16[512,1536]{1,0:T(8,128)(2,1)}, bf16[512,1536]{1,0:T(8,128)(2,1)}, u32[]{:S(2)}, u32[]{:S(2)}) collective-permute-start(bf16[512,1536]{1,0:T(8,128)(2,1)} %get-tuple-element.51.mine), channel_id=1, source_target_pairs={{0,1},{1,0},{2,3},{3,2},{4,5},{5,4},{6,7},{7,6},{8,9},{9,8},{10,11... | collective-permute-start | bytes 4718600 | tf_op jit(solution)/shard_map/ppermute | solution.py:40
  65.1 19.4 %collective-permute-start.10 = (bf16[128,1536]{1,0:T(8,128)(2,1)S(1)}, bf16[128,1536]{1,0:T(8,128)(2,1)S(1)}, u32[]{:S(2)}, u32[]{:S(2)}) collective-permute-start(bf16[128,1536]{1,0:T(8,128)(2,1)S(1)} %get-tuple-element.48), channel_id=1, source_target_pairs={{0,192},{32,224},{64,0},{96,32},{128,64},{160,96},{192,128},{224,1... | collective-permute-start | bytes 1179656 | tf_op jit(solution)/shard_map/ppermute | solution.py:52
  67.6 20.1 %collective-permute-start.8 = (bf16[128,1536]{1,0:T(8,128)(2,1)S(1)}, bf16[128,1536]{1,0:T(8,128)(2,1)S(1)}, u32[]{:S(2)}, u32[]{:S(2)}) collective-permute-start(bf16[128,1536]{1,0:T(8,128)(2,1)S(1)} %get-tuple-element.46), channel_id=1, source_target_pairs={{0,64},{32,96},{64,128},{96,160},{128,192},{160,224},{192,0},{224,... | collective-permute-start | bytes 1179656 | tf_op jit(solution)/shard_map/ppermute | solution.py:52
  67.6 20.1 %collective-permute-start.9 = (bf16[128,1536]{1,0:T(8,128)(2,1)S(1)}, bf16[128,1536]{1,0:T(8,128)(2,1)S(1)}, u32[]{:S(2)}, u32[]{:S(2)}) collective-permute-start(bf16[128,1536]{1,0:T(8,128)(2,1)S(1)} %get-tuple-element.47), channel_id=1, source_target_pairs={{0,128},{32,160},{64,192},{96,224},{128,0},{160,32},{192,64},{224,... | collective-permute-start | bytes 1179656 | tf_op jit(solution)/shard_map/ppermute | solution.py:52
  88.6 17.7 %collective-permute-start.11 = (bf16[128,1664]{1,0:T(8,128)(2,1)S(1)}, bf16[128,1664]{1,0:T(8,128)(2,1)S(1)}, u32[]{:S(2)}, u32[]{:S(2)}) collective-permute-start(bf16[128,1664]{1,0:T(8,128)(2,1)S(1)} %back_sum.1.mine), channel_id=1, source_target_pairs={{0,32},{32,0},{64,96},{96,64},{128,160},{160,128},{192,224},{224,1... | collective-permute-start | bytes 1277960 | tf_op jit(solution)/shard_map/ppermute | solution.py:56
  93.7 2.6 %collective-permute-start.12 = (bf16[128,768]{1,0:T(8,128)(2,1)S(1)}, bf16[128,768]{1,0:T(8,128)(2,1)S(1)}, u32[]{:S(2)}, u32[]{:S(2)}) collective-permute-start(bf16[128,768]{1,0:T(8,128)(2,1)S(1)} %get-tuple-element.75), channel_id=1, source_target_pairs={{0,1},{1,0},{2,3},{3,2},{4,5},{5,4},{6,7},{7,6},{8,9},{9,8},{10,11... | collective-permute-start | bytes 589832 | tf_op jit(solution)/shard_map/ppermute | solution.py:40
  95.2 11.8 %collective-permute-start.16 = (bf16[2,128,768]{2,1,0:T(8,128)(2,1)S(1)}, bf16[2,128,768]{2,1,0:T(8,128)(2,1)S(1)}, u32[]{:S(2)}, u32[]{:S(2)}) collective-permute-start(bf16[2,128,768]{2,1,0:T(8,128)(2,1)S(1)} %pad_maximum_fusion.3.r0), channel_id=1, source_target_pairs={{0,192},{32,224},{64,0},{96,32},{128,64},{160,96},{192,128},{224,1... | collective-permute-start | bytes 1179656 | tf_op jit(solution)/shard_map/ppermute | solution.py:52
  96.3 14.1 %collective-permute-start.17 = (bf16[2,128,768]{2,1,0:T(8,128)(2,1)S(1)}, bf16[2,128,768]{2,1,0:T(8,128)(2,1)S(1)}, u32[]{:S(2)}, u32[]{:S(2)}) collective-permute-start(bf16[2,128,768]{2,1,0:T(8,128)(2,1)S(1)} %pad_maximum_fusion.3.r0), channel_id=1, source_target_pairs={{0,128},{32,160},{64,192},{96,224},{128,0},{160,32},{192,64},{224,... | collective-permute-start | bytes 1179656 | tf_op jit(solution)/shard_map/ppermute | solution.py:52
  106.3 11.1 %collective-permute-start.18 = (bf16[2,128,768]{2,1,0:T(8,128)(2,1)S(1)}, bf16[2,128,768]{2,1,0:T(8,128)(2,1)S(1)}, u32[]{:S(2)}, u32[]{:S(2)}) collective-permute-start(bf16[2,128,768]{2,1,0:T(8,128)(2,1)S(1)} %pad_maximum_fusion.3.r0), channel_id=1, source_target_pairs={{0,64},{32,96},{64,128},{96,160},{128,192},{160,224},{192,0},{224,... | collective-permute-start | bytes 1179656 | tf_op jit(solution)/shard_map/ppermute | solution.py:52
  107.7 22.1 %collective-permute-start.13 = (bf16[128,1664]{1,0:T(8,128)(2,1)S(1)}, bf16[128,1664]{1,0:T(8,128)(2,1)S(1)}, u32[]{:S(2)}, u32[]{:S(2)}) collective-permute-start(bf16[128,1664]{1,0:T(8,128)(2,1)S(1)} %slope.1.m0), channel_id=1, source_target_pairs={{0,192},{32,224},{64,0},{96,32},{128,64},{160,96},{192,128},{224,1... | collective-permute-start | bytes 1277960 | tf_op jit(solution)/shard_map/ppermute | solution.py:52
  111.2 18.6 %collective-permute-start.14 = (bf16[128,1664]{1,0:T(8,128)(2,1)S(1)}, bf16[128,1664]{1,0:T(8,128)(2,1)S(1)}, u32[]{:S(2)}, u32[]{:S(2)}) collective-permute-start(bf16[128,1664]{1,0:T(8,128)(2,1)S(1)} %slope.1.m0), channel_id=1, source_target_pairs={{0,128},{32,160},{64,192},{96,224},{128,0},{160,32},{192,64},{224,... | collective-permute-start | bytes 1277960 | tf_op jit(solution)/shard_map/ppermute | solution.py:52
  118.2 14.0 %collective-permute-start.15 = (bf16[128,1664]{1,0:T(8,128)(2,1)S(1)}, bf16[128,1664]{1,0:T(8,128)(2,1)}, u32[]{:S(2)}, u32[]{:S(2)}) collective-permute-start(bf16[128,1664]{1,0:T(8,128)(2,1)S(1)} %slope.1.m0), channel_id=1, source_target_pairs={{0,64},{32,96},{64,128},{96,160},{128,192},{160,224},{192,0},{224,... | collective-permute-start | bytes 1277960 | tf_op jit(solution)/shard_map/ppermute | solution.py:52
  121.8 10.3 %copy-start.2 = (bf16[1536,768]{1,0:T(8,128)(2,1)S(1)}, bf16[1536,768]{1,0:T(8,128)(2,1)}, u32[]{:S(2)}) copy-start(bf16[1536,768]{1,0:T(8,128)(2,1)} %wa.3) | copy-start | bytes 7077892
  140.7 11.5 %collective-permute-start.24 = (bf16[512,768]{1,0:T(8,128)(2,1)S(1)}, bf16[512,768]{1,0:T(8,128)(2,1)S(1)}, u32[]{:S(2)}, u32[]{:S(2)}) collective-permute-start(bf16[512,768]{1,0:T(8,128)(2,1)S(1)} %get-tuple-element.62), channel_id=1, source_target_pairs={{0,1},{1,0},{2,3},{3,2},{4,5},{5,4},{6,7},{7,6},{8,9},{9,8},{10,11... | collective-permute-start | bytes 2359304 | tf_op jit(solution)/shard_map/ppermute | solution.py:40
  149.5 21.8 %collective-permute-start.21 = (bf16[128,1664]{1,0:T(8,128)(2,1)S(1)}, bf16[128,1664]{1,0:T(8,128)(2,1)S(1)}, u32[]{:S(2)}, u32[]{:S(2)}) collective-permute-start(bf16[128,1664]{1,0:T(8,128)(2,1)S(1)} %get-tuple-element.57.mine), channel_id=1, source_target_pairs={{0,8},{1,9},{2,10},{3,11},{4,12},{5,13},{6,14},{7,15},{8,16},{9,17... | collective-permute-start | bytes 1277960 | tf_op jit(solution)/shard_map/ppermute | solution.py:48
  149.5 21.8 %collective-permute-start.22 = (bf16[128,1664]{1,0:T(8,128)(2,1)}, bf16[128,1664]{1,0:T(8,128)(2,1)S(1)}, u32[]{:S(2)}, u32[]{:S(2)}) collective-permute-start(bf16[128,1664]{1,0:T(8,128)(2,1)} %get-tuple-element.58), channel_id=1, source_target_pairs={{0,16},{1,17},{2,18},{3,19},{4,20},{5,21},{6,22},{7,23},{8,24},{9,... | collective-permute-start | bytes 1277960 | tf_op jit(solution)/shard_map/ppermute | solution.py:48
  149.5 22.3 %collective-permute-start.23 = (bf16[128,1664]{1,0:T(8,128)(2,1)}, bf16[128,1664]{1,0:T(8,128)(2,1)S(1)}, u32[]{:S(2)}, u32[]{:S(2)}) collective-permute-start(bf16[128,1664]{1,0:T(8,128)(2,1)} %get-tuple-element.59), channel_id=1, source_target_pairs={{0,24},{1,25},{2,26},{3,27},{4,28},{5,29},{6,30},{7,31},{8,0},{9,1... | collective-permute-start | bytes 1277960 | tf_op jit(solution)/shard_map/ppermute | solution.py:48
  171.9 17.4 %collective-permute-start.25 = (bf16[32,1664]{1,0:T(8,128)(2,1)S(1)}, bf16[32,1664]{1,0:T(8,128)(2,1)S(1)}, u32[]{:S(2)}, u32[]{:S(2)}) collective-permute-start(bf16[32,1664]{1,0:T(8,128)(2,1)S(1)} %get-tuple-element.67.mine), channel_id=1, source_target_pairs={{0,2},{1,3},{2,0},{3,1},{4,6},{5,7},{6,4},{7,5},{8,10},{9,11},{10,... | collective-permute-start | bytes 319496 | tf_op jit(solution)/shard_map/ppermute | solution.py:44
  187.1 10.2 %collective-permute-start.26 = (bf16[32,1664]{1,0:T(8,128)(2,1)S(1)}, bf16[32,1664]{1,0:T(8,128)(2,1)S(1)}, u32[]{:S(2)}, u32[]{:S(2)}) collective-permute-start(bf16[32,1664]{1,0:T(8,128)(2,1)S(1)} %get-tuple-element.68), channel_id=1, source_target_pairs={{0,4},{1,5},{2,6},{3,7},{4,0},{5,1},{6,2},{7,3},{8,12},{9,13},{10,... | collective-permute-start | bytes 319496 | tf_op jit(solution)/shard_map/ppermute | solution.py:44
  187.1 10.2 %collective-permute-start.27 = (bf16[32,1664]{1,0:T(8,128)(2,1)S(1)}, bf16[32,1664]{1,0:T(8,128)(2,1)S(1)}, u32[]{:S(2)}, u32[]{:S(2)}) collective-permute-start(bf16[32,1664]{1,0:T(8,128)(2,1)S(1)} %get-tuple-element.69), channel_id=1, source_target_pairs={{0,6},{1,7},{2,4},{3,5},{4,2},{5,3},{6,0},{7,1},{8,14},{9,15},{10,... | collective-permute-start | bytes 319496 | tf_op jit(solution)/shard_map/ppermute | solution.py:44
  198.0 1.4 collective-permute-start.28
  (13 other events, 18.5 us)
Sparse Core Ops, SparseCore 0:
  44.9 69.7 all-gather.1

commit v3 on v2

v3 whole, which is shorter than its diff:
```python
import math

import jax
import jax.numpy as jnp
from jax import lax
from jax.experimental import pallas as pl
from jax.experimental.pallas import tpu as pltpu
from jax.sharding import PartitionSpec as P

coef = math.sqrt(2.0 / math.pi)
f32, bf16 = jnp.float32, jnp.bfloat16
barrier = lax.optimization_barrier
D, FF, T = 1536, 768, 128
W = 2 * FF
B = 256


def gelu_value(pre):
    inner = coef * (pre + 0.044715 * pre * pre * pre)
    return 0.5 * pre * (1.0 + jnp.tanh(inner))


def gelu_slope(pre):
    inner = coef * (pre + 0.044715 * pre * pre * pre)
    tval = jnp.tanh(inner)
    return 0.5 * (1.0 + tval) + 0.5 * pre * (1.0 - tval * tval) * coef * (
        1.0 + 3.0 * 0.044715 * pre * pre
    )


def across(left, right):
    return lax.dot_general(left, right, (((1,), (1,)), ((), ())), preferred_element_type=f32)


def over_tokens(left, right):
    return lax.dot_general(left, right, (((0,), (0,)), ((), ())), preferred_element_type=f32)


def to_core(v):
    return lax.ppermute(v, "col", [(i, i ^ 1) for i in range(32)])


def to_l(v, k):
    return lax.ppermute(v, "col", [(i, i ^ (2 * k)) for i in range(32)])


def to_y(v, k):
    return lax.ppermute(v, "col", [(i, (i + 8 * k) % 32) for i in range(32)])


def to_x(v, k):
    return lax.ppermute(v, "row", [(i, (i + 2 * k) % 8) for i in range(8)])


def to_h(v):
    return lax.ppermute(v, "row", [(i, i ^ 1) for i in range(8)])


def ring(v, send):
    far, near, behind = send(v, 2), send(v, 3), send(v, 1)
    return [v, near, far, behind]


def put_tops(ref, top_h, top_y):
    row = lax.broadcasted_iota(jnp.int32, (ref.shape[0], 128), 0)
    high = top_h.astype(bf16).astype(f32)
    mid = (top_h - high).astype(bf16).astype(f32)
    low = top_h - high - mid
    extra = jnp.where(row == 0, high, jnp.where(row == 1, mid, jnp.where(row == 2, low, 0.0)))
    ref[:, D : D + 128] = jnp.where(row == 3, top_y, extra).astype(bf16)


def get_tops(refs):
    top_h = top_y = jnp.zeros((1, 128), f32)
    for ref in refs:
        extra = ref[0:16, D : D + 128].astype(f32)
        top_h = jnp.maximum(top_h, extra[0:1] + extra[1:2] + extra[2:3])
        top_y = jnp.maximum(top_y, extra[3:4])
    return top_h, top_y


def place(at):
    row, col = at[0], at[1]
    return row >> 1, row & 1, col >> 3, (col >> 1) & 3, col & 1


def copy(src, dst, sem):
    return pltpu.make_async_copy(src, dst, sem)


def back_kernel(
    t, g0, g1, g2, g3, wa, wb, here, there, own, p1, p2, p3, stacked, pre, pre_other, blocks, weights, sems, wsems
):
    i = pl.program_id(0)
    x, h, y, l, c = place(t)
    shift = x - y
    last = FF // B

    def weight(k):
        ref, at = (wa, k) if k < last else (wb, k - last)
        return copy(ref.at[at * B : (at + 1) * B], weights.at[k], wsems.at[k])

    def moves():
        out = []
        for high in range(2):
            for low in range(2):
                for core in range(2):
                    rows = slice((low * 2 + core) * 32, (low * 2 + core + 1) * 32)
                    ref, slot = (here, there)[high], (2 * (h ^ high) + low) ^ l
                    out.append(copy(ref.at[rows], pre.at[c ^ core, slot], sems.at[5 + len(out)]))
        return out

    def blocks_in():
        return [copy(g, blocks.at[(s - shift) & 3], sems.at[s]) for s, g in enumerate((g0, g1, g2, g3))]

    @pl.when(i == 0)
    def _():
        for move in blocks_in():
            move.start()
        for k in range(W // B):
            weight(k).start()
        for move in moves():
            move.start()
        for move in blocks_in():
            move.wait()
        copy(blocks, stacked, sems.at[4]).start()

    for k in range(W // B):
        pl.when(i == k)(weight(k).wait)
    out = across(blocks[...].reshape(4 * T, D), weights[i])
    at = pl.ds(pl.multiple_of(i * B, B), B)
    own[:, at] = out[:T]
    for k, p in enumerate((p1, p2, p3)):
        p[:, at] = out[(k + 1) * T : (k + 2) * T].astype(bf16)

    @pl.when(i == 0)
    def _():
        for move in moves():
            move.wait()
        copy(pre.at[1], pre_other, sems.at[5]).start()

    @pl.when(i == pl.num_programs(0) - 1)
    def _():
        copy(pre.at[1], pre_other, sems.at[5]).wait()
        copy(blocks, stacked, sems.at[4]).wait()


def sum_kernel(own, r1, r2, r3, tops, msg):
    for k in range(T // 16):
        at = slice(16 * k, 16 * (k + 1))
        total = own[at] + r1[at].astype(f32) + r2[at].astype(f32) + r3[at].astype(f32)
        msg[at, :W] = total.astype(bf16)
    put_tops(msg, jnp.zeros((1, 128), f32), tops[0:1])


def slope_kernel(mine, other, pre_a, pre_b, msg):
    _, top_y = get_tops((mine, other))
    top = jnp.zeros((16, FF), f32)
    for k in range(T // 16):
        at = slice(16 * k, 16 * (k + 1))
        for half, pre in enumerate((pre_a, pre_b)):
            cols = slice(half * FF, (half + 1) * FF)
            back = mine[at, cols].astype(f32) + other[at, cols].astype(f32)
            hidden_grad = back * gelu_slope(pre[at].astype(f32))
            top = jnp.maximum(top, jnp.abs(hidden_grad))
            msg[at, cols] = hidden_grad.astype(bf16)
    top = jnp.max(top, axis=0, keepdims=True)
    top_h = top[:, :128]
    for k in range(1, FF // 128):
        top_h = jnp.maximum(top_h, top[:, 128 * k : 128 * (k + 1)])
    put_tops(msg, top_h, top_y)


def grad_kernel(t, m0, m1, m2, m3, wa, wb, own, p1, p2, p3, hq_b, blocks, weights, sems, wsems):
    i = pl.program_id(0)
    x, _, y, _, _ = place(t)

    def weight(k):
        rows = slice(k * B, (k + 1) * B)
        return [copy(w.at[rows], weights.at[s, k], wsems.at[s, k]) for s, w in enumerate((wa, wb))]

    def blocks_in():
        return [copy(m, blocks.at[(s - y + x) & 3], sems.at[s]) for s, m in enumerate((m0, m1, m2, m3))]

    def blocks_out():
        return [
            copy(blocks.at[(s - y + x) & 3, :, FF:W], hq_b.at[s * T : (s + 1) * T], sems.at[4 + s])
            for s in range(4)
        ]

    @pl.when(i == 0)
    def _():
        for move in blocks_in():
            move.start()
        for k in range(D // B):
            for move in weight(k):
                move.start()
        for move in blocks_in():
            move.wait()
        for move in blocks_out():
            move.start()
        top_h, top_y = get_tops([blocks.at[s] for s in range(4)])
        for p in (p1, p2, p3):
            put_tops(p, top_h, top_y)

    for k in range(D // B):

        @pl.when(i == k)
        def _():
            for move in weight(k):
                move.wait()

    hq = blocks[:, :, :W].reshape(4 * T, W)
    out = across(hq[:, :FF], weights[0, i]) + across(hq[:, FF:], weights[1, i])
    at = pl.ds(pl.multiple_of(i * B, B), B)
    own[:, at] = out[:T]
    for k, p in enumerate((p1, p2, p3)):
        p[:, at] = out[(k + 1) * T : (k + 2) * T].astype(bf16)

    @pl.when(i == pl.num_programs(0) - 1)
    def _():
        for move in blocks_out():
            move.wait()


def gather_kernel(own, r1, r2, r3, mine, kept, s1, s2, s3):
    top_h, top_y = get_tops((r1, r2, r3, mine))
    for m, out in enumerate((kept, s1, s2, s3)):
        at = slice(32 * m, 32 * (m + 1))
        total = own[at] + r1[at, :D].astype(f32) + r2[at, :D].astype(f32) + r3[at, :D].astype(f32)
        out[:, :D] = total.astype(out.dtype)
    for out in (s1, s2, s3):
        put_tops(out, top_h, top_y)


def last_kernel(kept, r1, r2, r3, mine, out, tops):
    top_h, top_y = get_tops((r1, r2, r3, mine))
    total = kept[...] + r1[:, :D].astype(f32) + r2[:, :D].astype(f32) + r3[:, :D].astype(f32)
    out[...] = total.astype(bf16)
    row = lax.broadcasted_iota(jnp.int32, (8, 128), 0)
    tops[...] = jnp.where(row == 0, top_y, jnp.where(row == 1, top_h, 0.0))


def w_out_kernel(r0, r1, r2, r3, mine, other, out, raw, hidden, grads, sems, gsems):
    i = pl.program_id(0)

    def parts(k):
        cols = slice(k * B, (k + 1) * B)
        return [copy(g.at[:, cols], grads.at[k, s], gsems.at[s, k]) for s, g in enumerate((mine, other))]

    def pres():
        return [copy(r, raw.at[s], sems.at[s]) for s, r in enumerate((r0, r1, r2, r3))]

    @pl.when(i == 0)
    def _():
        for move in pres():
            move.start()
        for k in range(D // B):
            for move in parts(k):
                move.start()
        for s, move in enumerate(pres()):
            move.wait()
            for c in range(2):
                hidden[c, s * T : (s + 1) * T] = gelu_value(raw[s, c].astype(f32)).astype(bf16)

    for k in range(D // B):

        @pl.when(i == k)
        def _():
            for move in parts(k):
                move.wait()

    half = grads[i]
    out[...] = (over_tokens(hidden[0], half[0]) + over_tokens(hidden[1], half[1])).astype(bf16)


def w_in_kernel(at, inputs, m0, m1, m2, m3, other, out, hq, cols, sems, csems):
    i = pl.program_id(0)
    x, _, _, l, c = place(at)

    def part(k):
        return copy(inputs.at[:, k * B : (k + 1) * B], cols.at[k], csems.at[k])

    def blocks_in():
        out = []
        for k, m in enumerate((m0, m1, m2, m3)):
            for s in range(4):
                to = ((x + k) & 3) * 4 + (s ^ l)
                rows = slice(s * 32, (s + 1) * 32)
                out.append(copy(m.at[rows, 0:FF], hq.at[to, c], sems.at[len(out)]))
                rows = slice(k * T + s * 32, k * T + (s + 1) * 32)
                out.append(copy(other.at[rows], hq.at[to, 1 - c], sems.at[len(out)]))
        return out

    @pl.when(i == 0)
    def _():
        for move in blocks_in():
            move.start()
        for k in range(D // B):
            part(k).start()
        for move in blocks_in():
            move.wait()

    for k in range(D // B):
        pl.when(i == k)(part(k).wait)
    out[...] = over_tokens(cols[i], hq[...].reshape(8 * T, FF)).astype(bf16)


def like(*shape, dtype=bf16):
    return jax.ShapeDtypeStruct(shape, dtype)


def call(kernel, name, outs, args, flops=0, mib=8, **spec):
    outs = list(outs)
    size = sum(math.prod(a.shape) * a.dtype.itemsize for a in list(args) + outs)
    return pl.pallas_call(
        kernel,
        out_shape=outs,
        name=name,
        compiler_params=pltpu.CompilerParams(vmem_limit_bytes=mib * 2**20),
        cost_estimate=pl.CostEstimate(flops=flops, bytes_accessed=size, transcendentals=0),
        **spec,
    )(*args)


def whole(a):
    zeros = (0,) * len(a.shape)
    return pl.BlockSpec(a.shape, lambda i, *t: zeros, pipeline_mode=pl.Buffered(1))


def here(args):
    return [pl.BlockSpec(memory_space=pltpu.HBM)] * len(args)


dma = pltpu.SemaphoreType.DMA


def local(inputs, preact, w_in, w_out, out_grad):
    row, col = lax.axis_index("row"), lax.axis_index("col")
    at, out_grad, inputs = barrier((jnp.stack([row, col]).astype(jnp.int32), out_grad, inputs))
    steps = D // B
    big = 2 * 4 * T * D * W

    inputs_all = lax.all_gather(inputs, "col", axis=0, tiled=True)

    grad = jnp.stack([out_grad] + [to_l(out_grad, k) for k in (1, 2, 3)]).reshape(T, D)
    w_out_o = to_core(w_out)
    top_y = jnp.broadcast_to(jnp.max(jnp.abs(out_grad)).astype(f32), (8, 128))
    grad, w_out_o, top_y, w_in_late, pre_late = barrier((grad, w_out_o, top_y, w_in, preact))
    grads = ring(grad, to_y)
    w_in_o = to_core(w_in_late)
    there = to_h(pre_late)
    *grads, w_in_o, there = barrier((*grads, w_in_o, there))

    args = (at, *grads, w_out, w_out_o, preact, there)
    outs = [like(T, W, dtype=f32)] + [like(T, W)] * 3
    apart = [like(4, T, D), like(2, 4, 32, FF), like(4, 32, FF)]
    own, p1, p2, p3, stacked, pre, pre_other = call(
        back_kernel,
        "back",
        outs + apart,
        args,
        big,
        20,
        grid_spec=pltpu.PrefetchScalarGridSpec(
            num_scalar_prefetch=1,
            grid=(W // B,),
            in_specs=here(args[1:]),
            out_specs=[whole(o) for o in outs] + here(apart),
            scratch_shapes=[
                pltpu.VMEM((4, T, D), bf16),
                pltpu.VMEM((W // B, B, D), bf16),
                dma((13,)),
                dma((W // B,)),
            ],
        ),
    )
    r2, r1, r3 = to_x(p2, 2), to_x(p1, 1), to_x(p3, 3)
    pre_b = to_core(pre_other.reshape(T, FF))
    r1, r2, r3, pre_b = barrier((r1, r2, r3, pre_b))

    (sent,) = call(sum_kernel, "back_sum", [like(T, W + 128)], (own, r1, r2, r3, top_y))
    other = to_h(sent)
    pre, sent = barrier((pre.reshape(2, T, FF), sent))
    pre_near, pre_behind = to_x(pre, 3), to_x(pre, 1)
    other, pre_near, pre_behind = barrier((other, pre_near, pre_behind))
    pre_a = pre[0]
    (msg,) = call(slope_kernel, "slope", [like(T, W + 128)], (sent, other, pre_a, pre_b))
    msgs = ring(msg, to_x)
    stacked, _ = barrier((stacked.reshape(4 * T, D), msg))
    stacked_o = to_core(stacked)
    *far, stacked_o = barrier((*msgs[1:], stacked_o))
    msgs = [msgs[0], *far]

    args = (at, *msgs, w_in, w_in_o)
    outs = [like(T, D, dtype=f32)] + [like(T, D + 128)] * 3
    apart = [like(4 * T, FF)]
    own, p1, p2, p3, hq_b = call(
        grad_kernel,
        "input_grad",
        outs + apart,
        args,
        big,
        20,
        grid_spec=pltpu.PrefetchScalarGridSpec(
            num_scalar_prefetch=1,
            grid=(steps,),
            in_specs=here(args[1:]),
            out_specs=[whole(o) for o in outs] + here(apart),
            scratch_shapes=[
                pltpu.VMEM((4, T, W + 128), bf16),
                pltpu.VMEM((2, steps, B, FF), bf16),
                dma((8,)),
                dma((2, steps)),
            ],
        ),
    )
    r2, r1, r3 = to_y(p2, 2), to_y(p1, 1), to_y(p3, 3)
    hq_o = to_core(hq_b)
    pre, _ = barrier((pre, hq_b))
    pre_far = to_x(pre, 2)
    args = (at, inputs_all, *msgs, hq_o)
    (w_in_grad,) = call(
        w_in_kernel,
        "w_in_grad",
        [like(D, FF)],
        args,
        big,
        20,
        grid_spec=pltpu.PrefetchScalarGridSpec(
            num_scalar_prefetch=1,
            grid=(steps,),
            in_specs=here(args[1:]),
            out_specs=[pl.BlockSpec((B, FF), lambda i, t: (i, 0))],
            scratch_shapes=[
                pltpu.VMEM((16, 2, 32, FF), bf16),
                pltpu.VMEM((steps, 8 * T, B), bf16),
                dma((32,)),
                dma((steps,)),
            ],
        ),
    )
    pre_far, w_in_grad = barrier((pre_far, w_in_grad))
    args = (pre, pre_near, pre_far, pre_behind, stacked, stacked_o)
    (w_out_grad,) = call(
        w_out_kernel,
        "w_out_grad",
        [like(FF, D)],
        args,
        big,
        20,
        grid=(steps,),
        in_specs=here(args),
        out_specs=[pl.BlockSpec((FF, B), lambda i: (0, i))],
        scratch_shapes=[
            pltpu.VMEM((4, 2, T, FF), bf16),
            pltpu.VMEM((2, 4 * T, FF), bf16),
            pltpu.VMEM((steps, 2, 4 * T, B), bf16),
            dma((4,)),
            dma((2, steps)),
        ],
    )
    r1, r2, r3, w_out_grad = barrier((r1, r2, r3, w_out_grad))
    outs = [like(32, D, dtype=f32)] + [like(32, D + 128)] * 3
    kept, s1, s2, s3 = call(gather_kernel, "y_sum", outs, (own, r1, r2, r3, p1))
    r2, r3, r1 = to_l(s2, 2), to_l(s3, 3), to_l(s1, 1)
    outs = [like(32, D), like(8, 128, dtype=f32)]
    input_grad, tops = call(last_kernel, "l_sum", outs, (kept, r1, r2, r3, s1))
    amaxes = jnp.max(jnp.maximum(tops, to_core(tops)), axis=1)[:2]
    return (input_grad, w_in_grad, w_out_grad, amaxes)


def solution(mesh):
    placed = (P("col", "row"), P("row", "col"), P("row", "col"), P("col", "row"), P("col", "row"))
    return jax.shard_map(
        local,
        mesh=mesh,
        in_specs=placed,
        out_specs=(P("col", "row"), P("row", "col"), P("col", "row"), P()),
        check_vma=False,
    )
```

time: 208 us -> 188 us (0.904)
  waiting for transfers between devices: 86.4 us -> 74.5 us
  starting transfers between devices: 60.5 us -> 56 us
  local copies, waits for them, and re-layouts: 12.5 us -> 8.22 us
  Pallas kernels: 28.8 us -> 31 us
    ppermute x6, waiting for transfers between devices: 30.9 us -> 9.86 us  [to_y(): return lax.ppermute(v, 'col', [(i, (i + 8 * k) % 32) for i in range(32)])]
    ppermute x9, waiting for transfers between devices: 25.7 us -> 45.9 us  [to_x(): return lax.ppermute(v, 'row', [(i, (i + 2 * k) % 8) for i in range(8)])]
    ppermute x6, starting transfers between devices: 22.9 us -> 8.47 us  [to_l(): return lax.ppermute(v, 'col', [(i, i ^ 2 * k) for i in range(32)])]
    ppermute x2, waiting for transfers between devices: 13.4 us -> 5.85 us  [to_h(): return lax.ppermute(v, 'row', [(i, i ^ 1) for i in range(8)])]
    ppermute x6, starting transfers between devices: 6.53 us -> 12.7 us  [to_y(): return lax.ppermute(v, 'col', [(i, (i + 8 * k) % 32) for i in range(32)])]
    unnamed x30 -> x36, local copies, waits for them, and re-layouts: 11.7 us -> 7.56 us
    ppermute x6, waiting for transfers between devices: 14.5 us -> 11 us  [to_l(): return lax.ppermute(v, 'col', [(i, i ^ 2 * k) for i in range(32)])]
    ppermute x9, starting transfers between devices: 8.11 us -> 10.5 us  [to_x(): return lax.ppermute(v, 'row', [(i, (i + 2 * k) % 8) for i in range(8)])]
  transfers between devices with their start and end apart: 30 -> 30, of which waited for: 16 -> 18; matrix products, arithmetic and copies ran while one was open for 2% -> 2% of each run, Pallas kernels for 14% -> 16%
where the time goes in v3:
time: 188 us; the launch traced here: 187 us
  waiting for transfers between devices  74.5 us (40%)
  starting transfers between devices  56 us (30%)
  Pallas kernels  31 us (16%)
  between operations  14.3 us (8%)
  local copies, waits for them, and re-layouts  8.22 us (4%)
  other arithmetic  3.16 us (2%)
    ppermute x9, waiting for transfers between devices, to_x(): return lax.ppermute(v, 'row', [(i, (i + 2 * k) % 8) for i in range(8)])  45.9 us
    pallas_call x8, Pallas kernels, call(): pl.pallas_call(kernel, out_shape=outs, name=name, compiler_params=pltpu.C...  31 us
    ppermute x6, starting transfers between devices, to_core(): return lax.ppermute(v, 'col', [(i, i ^ 1) for i in range(32)])  12.9 us
    ppermute x6, starting transfers between devices, to_y(): return lax.ppermute(v, 'col', [(i, (i + 8 * k) % 32) for i in range(32)])  12.7 us
    ppermute x2, starting transfers between devices, to_h(): return lax.ppermute(v, 'row', [(i, i ^ 1) for i in range(8)])  11.4 us
    ppermute x6, waiting for transfers between devices, to_l(): return lax.ppermute(v, 'col', [(i, i ^ 2 * k) for i in range(32)])  11 us
    ppermute x9, starting transfers between devices, to_x(): return lax.ppermute(v, 'row', [(i, (i + 2 * k) % 8) for i in range(8)])  10.5 us
    ppermute x6, waiting for transfers between devices, to_y(): return lax.ppermute(v, 'col', [(i, (i + 8 * k) % 32) for i in range(32)])  9.86 us
  transfers between devices with their start and end apart: 30, of which 18 were waited for; matrix products, arithmetic and copies ran while one was open for 2% of the time, Pallas kernels for 16%

profile of v3, /device:TPU:1, one launch (start us, length us, event | category | flops | bytes accessed | tf_op | source)
XLA Modules:
  0.0 187.1 jit_solution(13150481448399837533)
XLA Ops:
  7.2 3.3 %collective-permute-start.3 = (bf16[768,1536]{1,0:T(8,128)(2,1)}, bf16[768,1536]{1,0:T(8,128)(2,1)S(1)}, u32[]{:S(2)}, u32[]{:S(2)}) collective-permute-start(bf16[768,1536]{1,0:T(8,128)(2,1)} %wa.2), channel_id=1, source_target_pairs={{0,1},{1,0},{2,3},{3,2},{4,5},{5,4},{6,7},{7,6},{8,9},{9,8},{10,11... | collective-permute-start | bytes 7077896 | tf_op jit(solution)/shard_map/ppermute | solution.py:40
  10.6 2.9 %collective-permute-start.1 = (bf16[32,1536]{1,0:T(8,128)(2,1)}, bf16[32,1536]{1,0:T(8,128)(2,1)S(1)}, u32[]{:S(2)}, u32[]{:S(2)}) collective-permute-start(bf16[32,1536]{1,0:T(8,128)(2,1)} %param.9), channel_id=1, source_target_pairs={{0,4},{1,5},{2,6},{3,7},{4,0},{5,1},{6,2},{7,3},{8,12},{9,13},{10,... | collective-permute-start | bytes 294920 | tf_op jit(solution)/shard_map/ppermute | solution.py:44
  17.0 3.7 %collective-permute-done.2 = bf16[32,1536]{1,0:T(8,128)(2,1)S(1)} collective-permute-done((bf16[32,1536]{1,0:T(8,128)(2,1)}, bf16[32,1536]{1,0:T(8,128)(2,1)S(1)}, u32[]{:S(2)}, u32[]{:S(2)}) %collective-permute-start.2) | collective-permute-done | bytes 98336 | tf_op jit(solution)/shard_map/ppermute | solution.py:44
  22.3 1.6 collective-permute-start.7
  23.9 2.7 %collective-permute-start.4 = (bf16[128,1536]{1,0:T(8,128)(2,1)S(1)}, bf16[128,1536]{1,0:T(8,128)(2,1)S(1)}, u32[]{:S(2)}, u32[]{:S(2)}) collective-permute-start(bf16[128,1536]{1,0:T(8,128)(2,1)S(1)} %bitcast.13), channel_id=1, source_target_pairs={{0,24},{1,25},{2,26},{3,27},{4,28},{5,29},{6,30},{7,31},{8,0},{9,1... | collective-permute-start | bytes 1179656 | tf_op jit(solution)/shard_map/ppermute | solution.py:48
  27.6 5.7 %collective-permute-start.8 = (bf16[128,768]{1,0:T(8,128)(2,1)}, bf16[128,768]{1,0:T(8,128)(2,1)S(1)}, u32[]{:S(2)}, u32[]{:S(2)}) collective-permute-start(bf16[128,768]{1,0:T(8,128)(2,1)} %here.1), channel_id=1, source_target_pairs={{0,32},{32,0},{64,96},{96,64},{128,160},{160,128},{192,224},{224,1... | collective-permute-start | bytes 589832 | tf_op jit(solution)/shard_map/ppermute | solution.py:56
  33.3 5.8 %collective-permute-done.8.there = bf16[128,768]{1,0:T(8,128)(2,1)S(1)} collective-permute-done((bf16[128,768]{1,0:T(8,128)(2,1)}, bf16[128,768]{1,0:T(8,128)(2,1)S(1)}, u32[]{:S(2)}, u32[]{:S(2)}) %collective-permute-start.8) | collective-permute-done | bytes 196640 | tf_op jit(solution)/shard_map/ppermute | solution.py:56
  39.2 1.9 collective-permute-done.5.g2
  41.0 8.0 %collective-permute-done.6.g3 = bf16[128,1536]{1,0:T(8,128)(2,1)S(1)} collective-permute-done((bf16[128,1536]{1,0:T(8,128)(2,1)S(1)}, bf16[128,1536]{1,0:T(8,128)(2,1)S(1)}, u32[]{:S(2)}, u32[]{:S(2)}) %collective-permute-start.6) | collective-permute-done | bytes 393248 | tf_op jit(solution)/shard_map/ppermute | solution.py:48
  49.0 1.7 copy-done.1
  51.6 6.5 %back.1 = (f32[128,1536]{1,0:T(8,128)S(1)}, bf16[128,1536]{1,0:T(8,128)(2,1)S(1)}, bf16[128,1536]{1,0:T(8,128)(2,1)S(1)}, bf16[128,1536]{1,0:T(8,128)(2,1)S(1)},...) custom-call(s32[2]{0:T(128)S(1)} %pad_add_fusion.t.at, ...), custom_call_target="tpu_custom_call" | custom-call | flops 2415919104 | bytes 10813448 | tf_op jit(solution)/shard_map/back/pallas_call | solution.py:316
  58.2 3.3 %collective-permute-start.10 = (bf16[128,1536]{1,0:T(8,128)(2,1)S(1)}, bf16[128,1536]{1,0:T(8,128)(2,1)S(1)}, u32[]{:S(2)}, u32[]{:S(2)}) collective-permute-start(bf16[128,1536]{1,0:T(8,128)(2,1)S(1)} %get-tuple-element.71), channel_id=1, source_target_pairs={{0,128},{32,160},{64,192},{96,224},{128,0},{160,32},{192,64},{224,... | collective-permute-start | bytes 1179656 | tf_op jit(solution)/shard_map/ppermute | solution.py:52
  65.4 4.8 %collective-permute-done.10.r2 = bf16[128,1536]{1,0:T(8,128)(2,1)S(1)} collective-permute-done((bf16[128,1536]{1,0:T(8,128)(2,1)S(1)}, bf16[128,1536]{1,0:T(8,128)(2,1)S(1)}, u32[]{:S(2)}, u32[]{:S(2)}) %collective-permute-start.10) | collective-permute-done | bytes 393248 | tf_op jit(solution)/shard_map/ppermute | solution.py:52
  70.2 8.5 %collective-permute-done.11.r3 = bf16[128,1536]{1,0:T(8,128)(2,1)S(1)} collective-permute-done((bf16[128,1536]{1,0:T(8,128)(2,1)S(1)}, bf16[128,1536]{1,0:T(8,128)(2,1)S(1)}, u32[]{:S(2)}, u32[]{:S(2)}) %collective-permute-start.11) | collective-permute-done | bytes 393248 | tf_op jit(solution)/shard_map/ppermute | solution.py:52
  79.7 5.7 %collective-permute-start.13 = (bf16[128,1664]{1,0:T(8,128)(2,1)S(1)}, bf16[128,1664]{1,0:T(8,128)(2,1)S(1)}, u32[]{:S(2)}, u32[]{:S(2)}) collective-permute-start(bf16[128,1664]{1,0:T(8,128)(2,1)S(1)} %back_sum.1.mine), channel_id=1, source_target_pairs={{0,32},{32,0},{64,96},{96,64},{128,160},{160,128},{192,224},{224,1... | collective-permute-start | bytes 1277960 | tf_op jit(solution)/shard_map/ppermute | solution.py:56
  85.4 2.5 %collective-permute-start.14 = (bf16[2,128,768]{2,1,0:T(8,128)(2,1)S(1)}, bf16[2,128,768]{2,1,0:T(8,128)(2,1)S(1)}, u32[]{:S(2)}, u32[]{:S(2)}) collective-permute-start(bf16[2,128,768]{2,1,0:T(8,128)(2,1)S(1)} %bitcast.17), channel_id=1, source_target_pairs={{0,192},{32,224},{64,0},{96,32},{128,64},{160,96},{192,128},{224,1... | collective-permute-start | bytes 1179656 | tf_op jit(solution)/shard_map/ppermute | solution.py:52
  87.9 7.6 %collective-permute-done.14.r1 = bf16[2,128,768]{2,1,0:T(8,128)(2,1)S(1)} collective-permute-done((bf16[2,128,768]{2,1,0:T(8,128)(2,1)S(1)}, bf16[2,128,768]{2,1,0:T(8,128)(2,1)S(1)}, u32[]{:S(2)}, u32[]{:S(2)}) %collective-permute-start.14) | collective-permute-done | bytes 393248 | tf_op jit(solution)/shard_map/ppermute | solution.py:52
  95.5 3.1 %collective-permute-done.15.r3 = bf16[2,128,768]{2,1,0:T(8,128)(2,1)S(1)} collective-permute-done((bf16[2,128,768]{2,1,0:T(8,128)(2,1)S(1)}, bf16[2,128,768]{2,1,0:T(8,128)(2,1)S(1)}, u32[]{:S(2)}, u32[]{:S(2)}) %collective-permute-start.15) | collective-permute-done | bytes 393248 | tf_op jit(solution)/shard_map/ppermute | solution.py:52
  99.3 2.2 %collective-permute-start.19 = (bf16[512,1536]{1,0:T(8,128)(2,1)S(1)}, bf16[512,1536]{1,0:T(8,128)(2,1)S(1)}, u32[]{:S(2)}, u32[]{:S(2)}) collective-permute-start(bf16[512,1536]{1,0:T(8,128)(2,1)S(1)} %bitcast.22), channel_id=1, source_target_pairs={{0,1},{1,0},{2,3},{3,2},{4,5},{5,4},{6,7},{7,6},{8,9},{9,8},{10,11... | collective-permute-start | bytes 4718600 | tf_op jit(solution)/shard_map/ppermute | solution.py:40
  101.6 1.6 collective-permute-start.16
  104.4 8.5 %collective-permute-done.16.m1 = bf16[128,1664]{1,0:T(8,128)(2,1)S(1)} collective-permute-done((bf16[128,1664]{1,0:T(8,128)(2,1)S(1)}, bf16[128,1664]{1,0:T(8,128)(2,1)S(1)}, u32[]{:S(2)}, u32[]{:S(2)}) %collective-permute-start.16) | collective-permute-done | bytes 426016 | tf_op jit(solution)/shard_map/ppermute | solution.py:52
  112.9 2.8 %collective-permute-done.17.m2 = bf16[128,1664]{1,0:T(8,128)(2,1)S(1)} collective-permute-done((bf16[128,1664]{1,0:T(8,128)(2,1)S(1)}, bf16[128,1664]{1,0:T(8,128)(2,1)S(1)}, u32[]{:S(2)}, u32[]{:S(2)}) %collective-permute-start.17) | collective-permute-done | bytes 426016 | tf_op jit(solution)/shard_map/ppermute | solution.py:52
  115.8 9.8 %collective-permute-done.18.m3 = bf16[128,1664]{1,0:T(8,128)(2,1)S(1)} collective-permute-done((bf16[128,1664]{1,0:T(8,128)(2,1)S(1)}, bf16[128,1664]{1,0:T(8,128)(2,1)S(1)}, u32[]{:S(2)}, u32[]{:S(2)}) %collective-permute-start.18) | collective-permute-done | bytes 426016 | tf_op jit(solution)/shard_map/ppermute | solution.py:52
  125.6 8.6 %input_grad.1 = (f32[128,1536]{1,0:T(8,128)S(1)}, bf16[128,1664]{1,0:T(8,128)(2,1)S(1)}, bf16[128,1664]{1,0:T(8,128)(2,1)}, bf16[128,1664]{1,0:T(8,128)(2,1)}, bf16[512,768]{1,0:T(8,128)(2,1)}) custom-call(s32[2]{0:T(128)S(1)} %pad_add_fusion.t.at, bf16[128,1664]{1,0:T(8,128)(2,1)S(1)} %slope.1.m0, bf16[128,1664]{1,0:T(8,128)(2,1)S(1)} %collective-permute-done.16.m1, ...), custom_call_target="tpu_custom_call" | custom-call | flops 2415919104 | bytes 9273352 | tf_op jit(solution)/shard_map/input_grad/pallas_call | solution.py:316
  136.5 7.7 %collective-permute-start.21 = (bf16[128,1664]{1,0:T(8,128)(2,1)}, bf16[128,1664]{1,0:T(8,128)(2,1)S(1)}, u32[]{:S(2)}, u32[]{:S(2)}) collective-permute-start(bf16[128,1664]{1,0:T(8,128)(2,1)} %get-tuple-element.90), channel_id=1, source_target_pairs={{0,16},{1,17},{2,18},{3,19},{4,20},{5,21},{6,22},{7,23},{8,24},{9,... | collective-permute-start | bytes 1277960 | tf_op jit(solution)/shard_map/ppermute | solution.py:48
  144.2 1.9 %copy-done = bf16[1024,1536]{1,0:T(8,128)(2,1)S(1)} copy-done((bf16[1024,1536]{1,0:T(8,128)(2,1)S(1)}, bf16[1024,1536]{1,0:T(8,128)(2,1)}, u32[]{:S(2)}) %copy-start) | copy-done | bytes 3145752
  149.1 7.3 %w_in_grad.1 = bf16[1536,768]{1,0:T(8,128)(2,1)} custom-call(s32[2]{0:T(128)S(1)} %pad_add_fusion.t.at, bf16[1024,1536]{1,0:T(8,128)(2,1)S(1)} %copy-done, bf16[128,1664]{1,0:T(8,128)(2,1)S(1)} %slope.1.m0, bf16[128,1664]{1,0:T(8,128)(2,1)S(1)} %copy-done.8, bf16[128,1664]{1,0:T(8,128)(2,1)S(1)} %copy-done.10, bf16[128,1664]{1,0:T(8,128)(2,1)S(1)} %copy-done.12, ...), custom_call_target="tpu_custom_call" | custom-call | flops 2415919104 | bytes 7995400 | tf_op jit(solution)/shard_map/w_in_grad/pallas_call | solution.py:316
  156.5 6.8 %w_out_grad.1 = bf16[768,1536]{1,0:T(8,128)(2,1)} custom-call(bf16[2,128,768]{2,1,0:T(8,128)(2,1)S(1)} %bitcast.21, bf16[2,128,768]{2,1,0:T(8,128)(2,1)S(1)} %copy-done.14, bf16[2,128,768]{2,1,0:T(8,128)(2,1)} %collective-permute-done.23.r2, bf16[2,128,768]{2,1,0:T(8,128)(2,1)S(1)} %copy-done.16, bf16[512,1536]{1,0:T(8,128)(2,1)S(1)} %bitcast.23, ...), custom_call_target="tpu_custom_call" | custom-call | flops 2415919104 | bytes 7077888 | tf_op jit(solution)/shard_map/w_out_grad/pallas_call | solution.py:316
  163.5 2.6 %collective-permute-start.25 = (bf16[32,1664]{1,0:T(8,128)(2,1)S(1)}, bf16[32,1664]{1,0:T(8,128)(2,1)S(1)}, u32[]{:S(2)}, u32[]{:S(2)}) collective-permute-start(bf16[32,1664]{1,0:T(8,128)(2,1)S(1)} %get-tuple-element.103.mine), channel_id=1, source_target_pairs={{0,2},{1,3},{2,0},{3,1},{4,6},{5,7},{6,4},{7,5},{8,10},{9,11},{10,... | collective-permute-start | bytes 319496 | tf_op jit(solution)/shard_map/ppermute | solution.py:44
  168.4 2.2 %collective-permute-done.26.r2 = bf16[32,1664]{1,0:T(8,128)(2,1)S(1)} collective-permute-done((bf16[32,1664]{1,0:T(8,128)(2,1)S(1)}, bf16[32,1664]{1,0:T(8,128)(2,1)S(1)}, u32[]{:S(2)}, u32[]{:S(2)}) %collective-permute-start.26) | collective-permute-done | bytes 106528 | tf_op jit(solution)/shard_map/ppermute | solution.py:44
  170.7 3.8 %collective-permute-done.27.r3 = bf16[32,1664]{1,0:T(8,128)(2,1)S(1)} collective-permute-done((bf16[32,1664]{1,0:T(8,128)(2,1)S(1)}, bf16[32,1664]{1,0:T(8,128)(2,1)S(1)}, u32[]{:S(2)}, u32[]{:S(2)}) %collective-permute-start.27) | collective-permute-done | bytes 106528 | tf_op jit(solution)/shard_map/ppermute | solution.py:44
  175.2 3.7 %collective-permute-start.28 = (f32[8,128]{1,0:T(8,128)S(1)}, f32[8,128]{1,0:T(8,128)S(1)}, u32[]{:S(2)}, u32[]{:S(2)}) collective-permute-start(f32[8,128]{1,0:T(8,128)S(1)} %get-tuple-element.109), channel_id=1, source_target_pairs={{0,1},{1,0},{2,3},{3,2},{4,5},{5,4},{6,7},{7,6},{8,9},{9,8},{10,11... | collective-permute-start | bytes 12296 | tf_op jit(solution)/shard_map/ppermute | solution.py:40
  (79 shorter events, 24.0 us)
Async XLA Ops:
  7.2 137.0 %all-gather.2.cloned.1.call-start = ((), (), s32[]{:S(2)}) async-start(), calls=%async_computation | async-start | bytes 3244032 | tf_op jit(solution)/shard_map/all_gather | solution.py:344
  7.2 14.4 %collective-permute-start.3 = (bf16[768,1536]{1,0:T(8,128)(2,1)}, bf16[768,1536]{1,0:T(8,128)(2,1)S(1)}, u32[]{:S(2)}, u32[]{:S(2)}) collective-permute-start(bf16[768,1536]{1,0:T(8,128)(2,1)} %wa.2), channel_id=1, source_target_pairs={{0,1},{1,0},{2,3},{3,2},{4,5},{5,4},{6,7},{7,6},{8,9},{9,8},{10,11... | collective-permute-start | bytes 7077896 | tf_op jit(solution)/shard_map/ppermute | solution.py:40
  10.6 6.2 %collective-permute-start = (bf16[32,1536]{1,0:T(8,128)(2,1)}, bf16[32,1536]{1,0:T(8,128)(2,1)S(1)}, u32[]{:S(2)}, u32[]{:S(2)}) collective-permute-start(bf16[32,1536]{1,0:T(8,128)(2,1)} %param.9), channel_id=1, source_target_pairs={{0,2},{1,3},{2,0},{3,1},{4,6},{5,7},{6,4},{7,5},{8,10},{9,11},{10,... | collective-permute-start | bytes 294920 | tf_op jit(solution)/shard_map/ppermute | solution.py:44
  10.6 6.3 %collective-permute-start.1 = (bf16[32,1536]{1,0:T(8,128)(2,1)}, bf16[32,1536]{1,0:T(8,128)(2,1)S(1)}, u32[]{:S(2)}, u32[]{:S(2)}) collective-permute-start(bf16[32,1536]{1,0:T(8,128)(2,1)} %param.9), channel_id=1, source_target_pairs={{0,4},{1,5},{2,6},{3,7},{4,0},{5,1},{6,2},{7,3},{8,12},{9,13},{10,... | collective-permute-start | bytes 294920 | tf_op jit(solution)/shard_map/ppermute | solution.py:44
  13.5 7.1 %collective-permute-start.2 = (bf16[32,1536]{1,0:T(8,128)(2,1)}, bf16[32,1536]{1,0:T(8,128)(2,1)S(1)}, u32[]{:S(2)}, u32[]{:S(2)}) collective-permute-start(bf16[32,1536]{1,0:T(8,128)(2,1)} %param.9), channel_id=1, source_target_pairs={{0,6},{1,7},{2,4},{3,5},{4,2},{5,3},{6,0},{7,1},{8,14},{9,15},{10,... | collective-permute-start | bytes 294920 | tf_op jit(solution)/shard_map/ppermute | solution.py:44
  22.3 26.8 %collective-permute-start.7 = (bf16[1536,768]{1,0:T(8,128)(2,1)}, bf16[1536,768]{1,0:T(8,128)(2,1)S(1)}, u32[]{:S(2)}, u32[]{:S(2)}) collective-permute-start(bf16[1536,768]{1,0:T(8,128)(2,1)} %wa.3), channel_id=1, source_target_pairs={{0,1},{1,0},{2,3},{3,2},{4,5},{5,4},{6,7},{7,6},{8,9},{9,8},{10,11... | collective-permute-start | bytes 7077896 | tf_op jit(solution)/shard_map/ppermute | solution.py:40
  23.9 15.3 %collective-permute-start.4 = (bf16[128,1536]{1,0:T(8,128)(2,1)S(1)}, bf16[128,1536]{1,0:T(8,128)(2,1)S(1)}, u32[]{:S(2)}, u32[]{:S(2)}) collective-permute-start(bf16[128,1536]{1,0:T(8,128)(2,1)S(1)} %bitcast.13), channel_id=1, source_target_pairs={{0,24},{1,25},{2,26},{3,27},{4,28},{5,29},{6,30},{7,31},{8,0},{9,1... | collective-permute-start | bytes 1179656 | tf_op jit(solution)/shard_map/ppermute | solution.py:48
  26.6 14.4 %collective-permute-start.5 = (bf16[128,1536]{1,0:T(8,128)(2,1)S(1)}, bf16[128,1536]{1,0:T(8,128)(2,1)S(1)}, u32[]{:S(2)}, u32[]{:S(2)}) collective-permute-start(bf16[128,1536]{1,0:T(8,128)(2,1)S(1)} %bitcast.14), channel_id=1, source_target_pairs={{0,16},{1,17},{2,18},{3,19},{4,20},{5,21},{6,22},{7,23},{8,24},{9,... | collective-permute-start | bytes 1179656 | tf_op jit(solution)/shard_map/ppermute | solution.py:48
  26.9 22.1 %collective-permute-start.6 = (bf16[128,1536]{1,0:T(8,128)(2,1)S(1)}, bf16[128,1536]{1,0:T(8,128)(2,1)S(1)}, u32[]{:S(2)}, u32[]{:S(2)}) collective-permute-start(bf16[128,1536]{1,0:T(8,128)(2,1)S(1)} %bitcast.15), channel_id=1, source_target_pairs={{0,8},{1,9},{2,10},{3,11},{4,12},{5,13},{6,14},{7,15},{8,16},{9,17... | collective-permute-start | bytes 1179656 | tf_op jit(solution)/shard_map/ppermute | solution.py:48
  27.6 11.5 %collective-permute-start.8 = (bf16[128,768]{1,0:T(8,128)(2,1)}, bf16[128,768]{1,0:T(8,128)(2,1)S(1)}, u32[]{:S(2)}, u32[]{:S(2)}) collective-permute-start(bf16[128,768]{1,0:T(8,128)(2,1)} %here.1), channel_id=1, source_target_pairs={{0,32},{32,0},{64,96},{96,64},{128,160},{160,128},{192,224},{224,1... | collective-permute-start | bytes 589832 | tf_op jit(solution)/shard_map/ppermute | solution.py:56
  58.2 67.4 %copy-start.3 = (bf16[4,128,1536]{2,1,0:T(8,128)(2,1)}, bf16[4,128,1536]{2,1,0:T(8,128)(2,1)S(1)}, u32[]{:S(2)}) copy-start(bf16[4,128,1536]{2,1,0:T(8,128)(2,1)S(1)} %get-tuple-element.82) | copy-start | bytes 4718596
  58.2 67.4 %copy-start.2 = (bf16[1536,768]{1,0:T(8,128)(2,1)S(1)}, bf16[1536,768]{1,0:T(8,128)(2,1)}, u32[]{:S(2)}) copy-start(bf16[1536,768]{1,0:T(8,128)(2,1)} %wa.3) | copy-start | bytes 7077892
  58.2 12.1 %collective-permute-start.10 = (bf16[128,1536]{1,0:T(8,128)(2,1)S(1)}, bf16[128,1536]{1,0:T(8,128)(2,1)S(1)}, u32[]{:S(2)}, u32[]{:S(2)}) collective-permute-start(bf16[128,1536]{1,0:T(8,128)(2,1)S(1)} %get-tuple-element.71), channel_id=1, source_target_pairs={{0,128},{32,160},{64,192},{96,224},{128,0},{160,32},{192,64},{224,... | collective-permute-start | bytes 1179656 | tf_op jit(solution)/shard_map/ppermute | solution.py:52
  61.4 17.3 %collective-permute-start.11 = (bf16[128,1536]{1,0:T(8,128)(2,1)S(1)}, bf16[128,1536]{1,0:T(8,128)(2,1)S(1)}, u32[]{:S(2)}, u32[]{:S(2)}) collective-permute-start(bf16[128,1536]{1,0:T(8,128)(2,1)S(1)} %get-tuple-element.72), channel_id=1, source_target_pairs={{0,192},{32,224},{64,0},{96,32},{128,64},{160,96},{192,128},{224,1... | collective-permute-start | bytes 1179656 | tf_op jit(solution)/shard_map/ppermute | solution.py:52
  62.1 17.3 %collective-permute-start.9 = (bf16[128,1536]{1,0:T(8,128)(2,1)S(1)}, bf16[128,1536]{1,0:T(8,128)(2,1)S(1)}, u32[]{:S(2)}, u32[]{:S(2)}) collective-permute-start(bf16[128,1536]{1,0:T(8,128)(2,1)S(1)} %get-tuple-element.70), channel_id=1, source_target_pairs={{0,64},{32,96},{64,128},{96,160},{128,192},{160,224},{192,0},{224,... | collective-permute-start | bytes 1179656 | tf_op jit(solution)/shard_map/ppermute | solution.py:52
  62.9 2.5 %collective-permute-start.12 = (bf16[128,768]{1,0:T(8,128)(2,1)S(1)}, bf16[128,768]{1,0:T(8,128)(2,1)S(1)}, u32[]{:S(2)}, u32[]{:S(2)}) collective-permute-start(bf16[128,768]{1,0:T(8,128)(2,1)S(1)} %bitcast.24), channel_id=1, source_target_pairs={{0,1},{1,0},{2,3},{3,2},{4,5},{5,4},{6,7},{7,6},{8,9},{9,8},{10,11... | collective-permute-start | bytes 589832 | tf_op jit(solution)/shard_map/ppermute | solution.py:40
  79.7 19.0 %collective-permute-start.13 = (bf16[128,1664]{1,0:T(8,128)(2,1)S(1)}, bf16[128,1664]{1,0:T(8,128)(2,1)S(1)}, u32[]{:S(2)}, u32[]{:S(2)}) collective-permute-start(bf16[128,1664]{1,0:T(8,128)(2,1)S(1)} %back_sum.1.mine), channel_id=1, source_target_pairs={{0,32},{32,0},{64,96},{96,64},{128,160},{160,128},{192,224},{224,1... | collective-permute-start | bytes 1277960 | tf_op jit(solution)/shard_map/ppermute | solution.py:56
  85.4 10.1 %collective-permute-start.14 = (bf16[2,128,768]{2,1,0:T(8,128)(2,1)S(1)}, bf16[2,128,768]{2,1,0:T(8,128)(2,1)S(1)}, u32[]{:S(2)}, u32[]{:S(2)}) collective-permute-start(bf16[2,128,768]{2,1,0:T(8,128)(2,1)S(1)} %bitcast.17), channel_id=1, source_target_pairs={{0,192},{32,224},{64,0},{96,32},{128,64},{160,96},{192,128},{224,1... | collective-permute-start | bytes 1179656 | tf_op jit(solution)/shard_map/ppermute | solution.py:52
  87.9 10.8 %collective-permute-start.15 = (bf16[2,128,768]{2,1,0:T(8,128)(2,1)S(1)}, bf16[2,128,768]{2,1,0:T(8,128)(2,1)S(1)}, u32[]{:S(2)}, u32[]{:S(2)}) collective-permute-start(bf16[2,128,768]{2,1,0:T(8,128)(2,1)S(1)} %bitcast.18), channel_id=1, source_target_pairs={{0,64},{32,96},{64,128},{96,160},{128,192},{160,224},{192,0},{224,... | collective-permute-start | bytes 1179656 | tf_op jit(solution)/shard_map/ppermute | solution.py:52
  99.3 26.2 %collective-permute-start.19 = (bf16[512,1536]{1,0:T(8,128)(2,1)S(1)}, bf16[512,1536]{1,0:T(8,128)(2,1)S(1)}, u32[]{:S(2)}, u32[]{:S(2)}) collective-permute-start(bf16[512,1536]{1,0:T(8,128)(2,1)S(1)} %bitcast.22), channel_id=1, source_target_pairs={{0,1},{1,0},{2,3},{3,2},{4,5},{5,4},{6,7},{7,6},{8,9},{9,8},{10,11... | collective-permute-start | bytes 4718600 | tf_op jit(solution)/shard_map/ppermute | solution.py:40
  101.6 11.4 %collective-permute-start.16 = (bf16[128,1664]{1,0:T(8,128)(2,1)S(1)}, bf16[128,1664]{1,0:T(8,128)(2,1)S(1)}, u32[]{:S(2)}, u32[]{:S(2)}) collective-permute-start(bf16[128,1664]{1,0:T(8,128)(2,1)S(1)} %slope.1.m0), channel_id=1, source_target_pairs={{0,192},{32,224},{64,0},{96,32},{128,64},{160,96},{192,128},{224,1... | collective-permute-start | bytes 1277960 | tf_op jit(solution)/shard_map/ppermute | solution.py:52
  103.2 12.6 %collective-permute-start.17 = (bf16[128,1664]{1,0:T(8,128)(2,1)S(1)}, bf16[128,1664]{1,0:T(8,128)(2,1)S(1)}, u32[]{:S(2)}, u32[]{:S(2)}) collective-permute-start(bf16[128,1664]{1,0:T(8,128)(2,1)S(1)} %slope.1.m0), channel_id=1, source_target_pairs={{0,128},{32,160},{64,192},{96,224},{128,0},{160,32},{192,64},{224,... | collective-permute-start | bytes 1277960 | tf_op jit(solution)/shard_map/ppermute | solution.py:52
  103.5 22.0 %collective-permute-start.18 = (bf16[128,1664]{1,0:T(8,128)(2,1)S(1)}, bf16[128,1664]{1,0:T(8,128)(2,1)S(1)}, u32[]{:S(2)}, u32[]{:S(2)}) collective-permute-start(bf16[128,1664]{1,0:T(8,128)(2,1)S(1)} %slope.1.m0), channel_id=1, source_target_pairs={{0,64},{32,96},{64,128},{96,160},{128,192},{160,224},{192,0},{224,... | collective-permute-start | bytes 1277960 | tf_op jit(solution)/shard_map/ppermute | solution.py:52
  134.3 10.0 %collective-permute-start.24 = (bf16[512,768]{1,0:T(8,128)(2,1)}, bf16[512,768]{1,0:T(8,128)(2,1)}, u32[]{:S(2)}, u32[]{:S(2)}) collective-permute-start(bf16[512,768]{1,0:T(8,128)(2,1)} %get-tuple-element.92), channel_id=1, source_target_pairs={{0,1},{1,0},{2,3},{3,2},{4,5},{5,4},{6,7},{7,6},{8,9},{9,8},{10,11... | collective-permute-start | bytes 2359304 | tf_op jit(solution)/shard_map/ppermute | solution.py:40
  134.8 21.6 %collective-permute-start.23 = (bf16[2,128,768]{2,1,0:T(8,128)(2,1)S(1)}, bf16[2,128,768]{2,1,0:T(8,128)(2,1)}, u32[]{:S(2)}, u32[]{:S(2)}) collective-permute-start(bf16[2,128,768]{2,1,0:T(8,128)(2,1)S(1)} %bitcast.20), channel_id=1, source_target_pairs={{0,128},{32,160},{64,192},{96,224},{128,0},{160,32},{192,64},{224,... | collective-permute-start | bytes 1179656 | tf_op jit(solution)/shard_map/ppermute | solution.py:52
  135.2 28.1 %collective-permute-start.20 = (bf16[128,1664]{1,0:T(8,128)(2,1)S(1)}, bf16[128,1664]{1,0:T(8,128)(2,1)S(1)}, u32[]{:S(2)}, u32[]{:S(2)}) collective-permute-start(bf16[128,1664]{1,0:T(8,128)(2,1)S(1)} %get-tuple-element.89.mine), channel_id=1, source_target_pairs={{0,8},{1,9},{2,10},{3,11},{4,12},{5,13},{6,14},{7,15},{8,16},{9,17... | collective-permute-start | bytes 1277960 | tf_op jit(solution)/shard_map/ppermute | solution.py:48
  136.5 26.8 %collective-permute-start.21 = (bf16[128,1664]{1,0:T(8,128)(2,1)}, bf16[128,1664]{1,0:T(8,128)(2,1)S(1)}, u32[]{:S(2)}, u32[]{:S(2)}) collective-permute-start(bf16[128,1664]{1,0:T(8,128)(2,1)} %get-tuple-element.90), channel_id=1, source_target_pairs={{0,16},{1,17},{2,18},{3,19},{4,20},{5,21},{6,22},{7,23},{8,24},{9,... | collective-permute-start | bytes 1277960 | tf_op jit(solution)/shard_map/ppermute | solution.py:48
  144.2 19.1 %collective-permute-start.22 = (bf16[128,1664]{1,0:T(8,128)(2,1)}, bf16[128,1664]{1,0:T(8,128)(2,1)S(1)}, u32[]{:S(2)}, u32[]{:S(2)}) collective-permute-start(bf16[128,1664]{1,0:T(8,128)(2,1)} %get-tuple-element.91), channel_id=1, source_target_pairs={{0,24},{1,25},{2,26},{3,27},{4,28},{5,29},{6,30},{7,31},{8,0},{9,1... | collective-permute-start | bytes 1277960 | tf_op jit(solution)/shard_map/ppermute | solution.py:48
  163.5 4.9 %collective-permute-start.25 = (bf16[32,1664]{1,0:T(8,128)(2,1)S(1)}, bf16[32,1664]{1,0:T(8,128)(2,1)S(1)}, u32[]{:S(2)}, u32[]{:S(2)}) collective-permute-start(bf16[32,1664]{1,0:T(8,128)(2,1)S(1)} %get-tuple-element.103.mine), channel_id=1, source_target_pairs={{0,2},{1,3},{2,0},{3,1},{4,6},{5,7},{6,4},{7,5},{8,10},{9,11},{10,... | collective-permute-start | bytes 319496 | tf_op jit(solution)/shard_map/ppermute | solution.py:44
  166.1 4.6 %collective-permute-start.26 = (bf16[32,1664]{1,0:T(8,128)(2,1)S(1)}, bf16[32,1664]{1,0:T(8,128)(2,1)S(1)}, u32[]{:S(2)}, u32[]{:S(2)}) collective-permute-start(bf16[32,1664]{1,0:T(8,128)(2,1)S(1)} %get-tuple-element.104), channel_id=1, source_target_pairs={{0,4},{1,5},{2,6},{3,7},{4,0},{5,1},{6,2},{7,3},{8,12},{9,13},{10,... | collective-permute-start | bytes 319496 | tf_op jit(solution)/shard_map/ppermute | solution.py:44
  167.3 7.1 %collective-permute-start.27 = (bf16[32,1664]{1,0:T(8,128)(2,1)S(1)}, bf16[32,1664]{1,0:T(8,128)(2,1)S(1)}, u32[]{:S(2)}, u32[]{:S(2)}) collective-permute-start(bf16[32,1664]{1,0:T(8,128)(2,1)S(1)} %get-tuple-element.105), channel_id=1, source_target_pairs={{0,6},{1,7},{2,4},{3,5},{4,2},{5,3},{6,0},{7,1},{8,14},{9,15},{10,... | collective-permute-start | bytes 319496 | tf_op jit(solution)/shard_map/ppermute | solution.py:44
  175.2 4.5 %collective-permute-start.28 = (f32[8,128]{1,0:T(8,128)S(1)}, f32[8,128]{1,0:T(8,128)S(1)}, u32[]{:S(2)}, u32[]{:S(2)}) collective-permute-start(f32[8,128]{1,0:T(8,128)S(1)} %get-tuple-element.109), channel_id=1, source_target_pairs={{0,1},{1,0},{2,3},{3,2},{4,5},{5,4},{6,7},{7,6},{8,9},{9,8},{10,11... | collective-permute-start | bytes 12296 | tf_op jit(solution)/shard_map/ppermute | solution.py:40
  (16 other events, 168.1 us)
Sparse Core Ops, SparseCore 0:
  14.3 78.0 all-gather.1

commit v4 on v3

--- a/solution.py
+++ b/solution.py
@@ -12,7 +12,7 @@
 barrier = lax.optimization_barrier
 D, FF, T = 1536, 768, 128
 W = 2 * FF
-B = 256
+B, C = 256, 768
 
 
 def gelu_value(pre):
@@ -79,6 +79,16 @@
     return top_h, top_y
 
 
+def stack_kernel(a0, a1, a2, a3, stacked, tops):
+    for m, a in enumerate((a0, a1, a2, a3)):
+        stacked[m * 32 : (m + 1) * 32] = a[...]
+    top = jnp.max(jnp.abs(a0[...].astype(f32)), axis=0, keepdims=True)
+    lanes = top[:, :128]
+    for k in range(1, D // 128):
+        lanes = jnp.maximum(lanes, top[:, 128 * k : 128 * (k + 1)])
+    tops[...] = jnp.broadcast_to(lanes, (8, 128))
+
+
 def place(at):
     row, col = at[0], at[1]
     return row >> 1, row & 1, col >> 3, (col >> 1) & 3, col & 1
@@ -94,11 +104,11 @@
     i = pl.program_id(0)
     x, h, y, l, c = place(t)
     shift = x - y
-    last = FF // B
+    last = FF // C
 
     def weight(k):
         ref, at = (wa, k) if k < last else (wb, k - last)
-        return copy(ref.at[at * B : (at + 1) * B], weights.at[k], wsems.at[k])
+        return copy(ref.at[at * C : (at + 1) * C], weights.at[k], wsems.at[k])
 
     def moves():
         out = []
@@ -117,7 +127,7 @@
     def _():
         for move in blocks_in():
             move.start()
-        for k in range(W // B):
+        for k in range(W // C):
             weight(k).start()
         for move in moves():
             move.start()
@@ -125,10 +135,10 @@
             move.wait()
         copy(blocks, stacked, sems.at[4]).start()
 
-    for k in range(W // B):
+    for k in range(W // C):
         pl.when(i == k)(weight(k).wait)
     out = across(blocks[...].reshape(4 * T, D), weights[i])
-    at = pl.ds(pl.multiple_of(i * B, B), B)
+    at = pl.ds(pl.multiple_of(i * C, C), C)
     own[:, at] = out[:T]
     for k, p in enumerate((p1, p2, p3)):
         p[:, at] = out[(k + 1) * T : (k + 2) * T].astype(bf16)
@@ -176,7 +186,7 @@
     x, _, y, _, _ = place(t)
 
     def weight(k):
-        rows = slice(k * B, (k + 1) * B)
+        rows = slice(k * C, (k + 1) * C)
         return [copy(w.at[rows], weights.at[s, k], wsems.at[s, k]) for s, w in enumerate((wa, wb))]
 
     def blocks_in():
@@ -192,7 +202,7 @@
     def _():
         for move in blocks_in():
             move.start()
-        for k in range(D // B):
+        for k in range(D // C):
             for move in weight(k):
                 move.start()
         for move in blocks_in():
@@ -203,7 +213,7 @@
         for p in (p1, p2, p3):
             put_tops(p, top_h, top_y)
 
-    for k in range(D // B):
+    for k in range(D // C):
 
         @pl.when(i == k)
         def _():
@@ -212,7 +222,7 @@
 
     hq = blocks[:, :, :W].reshape(4 * T, W)
     out = across(hq[:, :FF], weights[0, i]) + across(hq[:, FF:], weights[1, i])
-    at = pl.ds(pl.multiple_of(i * B, B), B)
+    at = pl.ds(pl.multiple_of(i * C, C), C)
     own[:, at] = out[:T]
     for k, p in enumerate((p1, p2, p3)):
         p[:, at] = out[(k + 1) * T : (k + 2) * T].astype(bf16)
@@ -343,14 +353,14 @@
 
     inputs_all = lax.all_gather(inputs, "col", axis=0, tiled=True)
 
-    grad = jnp.stack([out_grad] + [to_l(out_grad, k) for k in (1, 2, 3)]).reshape(T, D)
-    w_out_o = to_core(w_out)
-    top_y = jnp.broadcast_to(jnp.max(jnp.abs(out_grad)).astype(f32), (8, 128))
-    grad, w_out_o, top_y, w_in_late, pre_late = barrier((grad, w_out_o, top_y, w_in, preact))
+    got = [to_l(out_grad, k) for k in (1, 2, 3)]
+    *got, w_out_late, pre_late = barrier((*got, w_out, preact))
+    outs = [like(T, D), like(8, 128, dtype=f32)]
+    grad, top_y = call(stack_kernel, "stack", outs, (out_grad, *got))
     grads = ring(grad, to_y)
-    w_in_o = to_core(w_in_late)
+    w_out_o = to_core(w_out_late)
     there = to_h(pre_late)
-    *grads, w_in_o, there = barrier((*grads, w_in_o, there))
+    *grads, w_out_o, there = barrier((*grads, w_out_o, there))
 
     args = (at, *grads, w_out, w_out_o, preact, there)
     outs = [like(T, W, dtype=f32)] + [like(T, W)] * 3
@@ -364,14 +374,14 @@
         20,
         grid_spec=pltpu.PrefetchScalarGridSpec(
             num_scalar_prefetch=1,
-            grid=(W // B,),
+            grid=(W // C,),
             in_specs=here(args[1:]),
             out_specs=[whole(o) for o in outs] + here(apart),
             scratch_shapes=[
                 pltpu.VMEM((4, T, D), bf16),
-                pltpu.VMEM((W // B, B, D), bf16),
+                pltpu.VMEM((W // C, C, D), bf16),
                 dma((13,)),
-                dma((W // B,)),
+                dma((W // C,)),
             ],
         ),
     )
@@ -381,15 +391,35 @@
 
     (sent,) = call(sum_kernel, "back_sum", [like(T, W + 128)], (own, r1, r2, r3, top_y))
     other = to_h(sent)
-    pre, sent = barrier((pre.reshape(2, T, FF), sent))
-    pre_near, pre_behind = to_x(pre, 3), to_x(pre, 1)
-    other, pre_near, pre_behind = barrier((other, pre_near, pre_behind))
+    pre, sent, w_in_late = barrier((pre.reshape(2, T, FF), sent, w_in))
+    w_in_o = to_core(w_in_late)
+    pre_near, pre_behind, pre_far = to_x(pre, 3), to_x(pre, 1), to_x(pre, 2)
+    other, pre_near, pre_behind, pre_far, w_in_o = barrier((other, pre_near, pre_behind, pre_far, w_in_o))
     pre_a = pre[0]
     (msg,) = call(slope_kernel, "slope", [like(T, W + 128)], (sent, other, pre_a, pre_b))
     msgs = ring(msg, to_x)
     stacked, _ = barrier((stacked.reshape(4 * T, D), msg))
     stacked_o = to_core(stacked)
-    *far, stacked_o = barrier((*msgs[1:], stacked_o))
+    args = (pre, pre_near, pre_far, pre_behind, stacked, stacked_o)
+    (w_out_grad,) = call(
+        w_out_kernel,
+        "w_out_grad",
+        [like(FF, D)],
+        args,
+        big,
+        20,
+        grid=(steps,),
+        in_specs=here(args),
+        out_specs=[pl.BlockSpec((FF, B), lambda i: (0, i))],
+        scratch_shapes=[
+            pltpu.VMEM((4, 2, T, FF), bf16),
+            pltpu.VMEM((2, 4 * T, FF), bf16),
+            pltpu.VMEM((steps, 2, 4 * T, B), bf16),
+            dma((4,)),
+            dma((2, steps)),
+        ],
+    )
+    *far, w_out_grad = barrier((*msgs[1:], w_out_grad))
     msgs = [msgs[0], *far]
 
     args = (at, *msgs, w_in, w_in_o)
@@ -404,21 +434,19 @@
         20,
         grid_spec=pltpu.PrefetchScalarGridSpec(
             num_scalar_prefetch=1,
-            grid=(steps,),
+            grid=(D // C,),
             in_specs=here(args[1:]),
             out_specs=[whole(o) for o in outs] + here(apart),
             scratch_shapes=[
                 pltpu.VMEM((4, T, W + 128), bf16),
-                pltpu.VMEM((2, steps, B, FF), bf16),
+                pltpu.VMEM((2, D // C, C, FF), bf16),
                 dma((8,)),
-                dma((2, steps)),
+                dma((2, D // C)),
             ],
         ),
     )
     r2, r1, r3 = to_y(p2, 2), to_y(p1, 1), to_y(p3, 3)
     hq_o = to_core(hq_b)
-    pre, _ = barrier((pre, hq_b))
-    pre_far = to_x(pre, 2)
     args = (at, inputs_all, *msgs, hq_o)
     (w_in_grad,) = call(
         w_in_kernel,
@@ -440,27 +468,7 @@
             ],
         ),
     )
-    pre_far, w_in_grad = barrier((pre_far, w_in_grad))
-    args = (pre, pre_near, pre_far, pre_behind, stacked, stacked_o)
-    (w_out_grad,) = call(
-        w_out_kernel,
-        "w_out_grad",
-        [like(FF, D)],
-        args,
-        big,
-        20,
-        grid=(steps,),
-        in_specs=here(args),
-        out_specs=[pl.BlockSpec((FF, B), lambda i: (0, i))],
-        scratch_shapes=[
-            pltpu.VMEM((4, 2, T, FF), bf16),
-            pltpu.VMEM((2, 4 * T, FF), bf16),
-            pltpu.VMEM((steps, 2, 4 * T, B), bf16),
-            dma((4,)),
-            dma((2, steps)),
-        ],
-    )
-    r1, r2, r3, w_out_grad = barrier((r1, r2, r3, w_out_grad))
+    r1, r2, r3, w_in_grad = barrier((r1, r2, r3, w_in_grad))
     outs = [like(32, D, dtype=f32)] + [like(32, D + 128)] * 3
     kept, s1, s2, s3 = call(gather_kernel, "y_sum", outs, (own, r1, r2, r3, p1))
     r2, r3, r1 = to_l(s2, 2), to_l(s3, 3), to_l(s1, 1)

time: 188 us -> 182 us (0.968)
  waiting for transfers between devices: 74.5 us -> 81.4 us
  starting transfers between devices: 56 us -> 50.3 us
  Pallas kernels: 31 us -> 27.4 us
  other arithmetic: 3.16 us -> 0.7 us
    ppermute x6, waiting for transfers between devices: 9.86 us -> 17.7 us  [to_y(): return lax.ppermute(v, 'col', [(i, (i + 8 * k) % 32) for i in range(32)])]
    ppermute x6, starting transfers between devices: 12.7 us -> 7.87 us  [to_y(): return lax.ppermute(v, 'col', [(i, (i + 8 * k) % 32) for i in range(32)])]
    pallas_call x8 -> x9, Pallas kernels: 31 us -> 27.4 us  [call(): pl.pallas_call(kernel, out_shape=outs, name=name, compiler_params=pltpu.C...]
    unnamed x36 -> x18, local copies, waits for them, and re-layouts: 7.56 us -> 7.43 us
  transfers between devices with their start and end apart: 30 -> 30, of which waited for: 18 -> 21; matrix products, arithmetic and copies ran while one was open for 2% -> 0% of each run, Pallas kernels for 16% -> 15%
where the time goes in v4:
time: 182 us; the launch traced here: 181 us
  waiting for transfers between devices  81.4 us (45%)
  starting transfers between devices  50.3 us (28%)
  Pallas kernels  27.4 us (15%)
  between operations  14.2 us (8%)
  local copies, waits for them, and re-layouts  7.45 us (4%)
    ppermute x9, waiting for transfers between devices, to_x(): return lax.ppermute(v, 'row', [(i, (i + 2 * k) % 8) for i in range(8)])  45 us
    pallas_call x9, Pallas kernels, call(): pl.pallas_call(kernel, out_shape=outs, name=name, compiler_params=pltpu.C...  27.4 us
    ppermute x6, waiting for transfers between devices, to_y(): return lax.ppermute(v, 'col', [(i, (i + 8 * k) % 32) for i in range(32)])  17.7 us
    ppermute x6, starting transfers between devices, to_core(): return lax.ppermute(v, 'col', [(i, i ^ 1) for i in range(32)])  13.9 us
    ppermute x6, waiting for transfers between devices, to_l(): return lax.ppermute(v, 'col', [(i, i ^ 2 * k) for i in range(32)])  12 us
    ppermute x2, starting transfers between devices, to_h(): return lax.ppermute(v, 'row', [(i, i ^ 1) for i in range(8)])  10.8 us
    ppermute x6, starting transfers between devices, to_l(): return lax.ppermute(v, 'col', [(i, i ^ 2 * k) for i in range(32)])  9.12 us
    ppermute x9, starting transfers between devices, to_x(): return lax.ppermute(v, 'row', [(i, (i + 2 * k) % 8) for i in range(8)])  8.66 us
  transfers between devices with their start and end apart: 30, of which 21 were waited for; matrix products, arithmetic and copies ran while one was open for 0% of the time, Pallas kernels for 15%

profile of v4, /device:TPU:1, one launch (start us, length us, event | category | flops | bytes accessed | tf_op | source)
XLA Modules:
  0.0 181.5 jit_solution(6643522161659676720)
XLA Ops:
  7.3 2.5 %collective-permute-start = (bf16[32,1536]{1,0:T(8,128)(2,1)}, bf16[32,1536]{1,0:T(8,128)(2,1)S(1)}, u32[]{:S(2)}, u32[]{:S(2)}) collective-permute-start(bf16[32,1536]{1,0:T(8,128)(2,1)} %a0), channel_id=1, source_target_pairs={{0,2},{1,3},{2,0},{3,1},{4,6},{5,7},{6,4},{7,5},{8,10},{9,11},{10,... | collective-permute-start | bytes 294920 | tf_op jit(solution)/shard_map/ppermute | solution.py:44
  9.8 3.0 %collective-permute-start.1 = (bf16[32,1536]{1,0:T(8,128)(2,1)}, bf16[32,1536]{1,0:T(8,128)(2,1)S(1)}, u32[]{:S(2)}, u32[]{:S(2)}) collective-permute-start(bf16[32,1536]{1,0:T(8,128)(2,1)} %a0), channel_id=1, source_target_pairs={{0,4},{1,5},{2,6},{3,7},{4,0},{5,1},{6,2},{7,3},{8,12},{9,13},{10,... | collective-permute-start | bytes 294920 | tf_op jit(solution)/shard_map/ppermute | solution.py:44
  12.8 2.8 %collective-permute-done.1.a2 = bf16[32,1536]{1,0:T(8,128)(2,1)S(1)} collective-permute-done((bf16[32,1536]{1,0:T(8,128)(2,1)}, bf16[32,1536]{1,0:T(8,128)(2,1)S(1)}, u32[]{:S(2)}, u32[]{:S(2)}) %collective-permute-start.1) | collective-permute-done | bytes 98336 | tf_op jit(solution)/shard_map/ppermute | solution.py:44
  15.6 3.7 %collective-permute-done.2.a3 = bf16[32,1536]{1,0:T(8,128)(2,1)S(1)} collective-permute-done((bf16[32,1536]{1,0:T(8,128)(2,1)}, bf16[32,1536]{1,0:T(8,128)(2,1)S(1)}, u32[]{:S(2)}, u32[]{:S(2)}) %collective-permute-start.2) | collective-permute-done | bytes 98336 | tf_op jit(solution)/shard_map/ppermute | solution.py:44
  19.3 2.7 %collective-permute-start.6 = (bf16[768,1536]{1,0:T(8,128)(2,1)}, bf16[768,1536]{1,0:T(8,128)(2,1)S(1)}, u32[]{:S(2)}, u32[]{:S(2)}) collective-permute-start(bf16[768,1536]{1,0:T(8,128)(2,1)} %wa.2), channel_id=1, source_target_pairs={{0,1},{1,0},{2,3},{3,2},{4,5},{5,4},{6,7},{7,6},{8,9},{9,8},{10,11... | collective-permute-start | bytes 7077896 | tf_op jit(solution)/shard_map/ppermute | solution.py:40
  22.9 2.8 %collective-permute-start.3 = (bf16[128,1536]{1,0:T(8,128)(2,1)S(1)}, bf16[128,1536]{1,0:T(8,128)(2,1)S(1)}, u32[]{:S(2)}, u32[]{:S(2)}) collective-permute-start(bf16[128,1536]{1,0:T(8,128)(2,1)S(1)} %get-tuple-element.67.g0), channel_id=1, source_target_pairs={{0,24},{1,25},{2,26},{3,27},{4,28},{5,29},{6,30},{7,31},{8,0},{9,1... | collective-permute-start | bytes 1179656 | tf_op jit(solution)/shard_map/ppermute | solution.py:48
  26.8 5.4 %collective-permute-start.7 = (bf16[128,768]{1,0:T(8,128)(2,1)}, bf16[128,768]{1,0:T(8,128)(2,1)S(1)}, u32[]{:S(2)}, u32[]{:S(2)}) collective-permute-start(bf16[128,768]{1,0:T(8,128)(2,1)} %here.1), channel_id=1, source_target_pairs={{0,32},{32,0},{64,96},{96,64},{128,160},{160,128},{192,224},{224,1... | collective-permute-start | bytes 589832 | tf_op jit(solution)/shard_map/ppermute | solution.py:56
  32.2 4.4 %collective-permute-done.7.there = bf16[128,768]{1,0:T(8,128)(2,1)S(1)} collective-permute-done((bf16[128,768]{1,0:T(8,128)(2,1)}, bf16[128,768]{1,0:T(8,128)(2,1)S(1)}, u32[]{:S(2)}, u32[]{:S(2)}) %collective-permute-start.7) | collective-permute-done | bytes 196640 | tf_op jit(solution)/shard_map/ppermute | solution.py:56
  36.6 5.8 %collective-permute-done.3.g1 = bf16[128,1536]{1,0:T(8,128)(2,1)S(1)} collective-permute-done((bf16[128,1536]{1,0:T(8,128)(2,1)S(1)}, bf16[128,1536]{1,0:T(8,128)(2,1)S(1)}, u32[]{:S(2)}, u32[]{:S(2)}) %collective-permute-start.3) | collective-permute-done | bytes 393248 | tf_op jit(solution)/shard_map/ppermute | solution.py:48
  42.3 4.4 %collective-permute-done.5.g3 = bf16[128,1536]{1,0:T(8,128)(2,1)} collective-permute-done((bf16[128,1536]{1,0:T(8,128)(2,1)S(1)}, bf16[128,1536]{1,0:T(8,128)(2,1)}, u32[]{:S(2)}, u32[]{:S(2)}) %collective-permute-start.5) | collective-permute-done | bytes 393248 | tf_op jit(solution)/shard_map/ppermute | solution.py:48
  49.4 5.5 %back.1 = (f32[128,1536]{1,0:T(8,128)S(1)}, bf16[128,1536]{1,0:T(8,128)(2,1)S(1)}, bf16[128,1536]{1,0:T(8,128)(2,1)S(1)}, bf16[128,1536]{1,0:T(8,128)(2,1)S(1)},...) custom-call(s32[2]{0:T(128)S(1)} %pad_add_fusion.t.at, ...), custom_call_target="tpu_custom_call" | custom-call | flops 2415919104 | bytes 10813448 | tf_op jit(solution)/shard_map/back/pallas_call | solution.py:326
  55.0 2.6 %collective-permute-start.10 = (bf16[128,1536]{1,0:T(8,128)(2,1)S(1)}, bf16[128,1536]{1,0:T(8,128)(2,1)S(1)}, u32[]{:S(2)}, u32[]{:S(2)}) collective-permute-start(bf16[128,1536]{1,0:T(8,128)(2,1)S(1)} %get-tuple-element.77), channel_id=1, source_target_pairs={{0,192},{32,224},{64,0},{96,32},{128,64},{160,96},{192,128},{224,1... | collective-permute-start | bytes 1179656 | tf_op jit(solution)/shard_map/ppermute | solution.py:52
  57.5 1.7 collective-permute-start.9
  61.7 4.7 %collective-permute-done.10.r3 = bf16[128,1536]{1,0:T(8,128)(2,1)S(1)} collective-permute-done((bf16[128,1536]{1,0:T(8,128)(2,1)S(1)}, bf16[128,1536]{1,0:T(8,128)(2,1)S(1)}, u32[]{:S(2)}, u32[]{:S(2)}) %collective-permute-start.10) | collective-permute-done | bytes 393248 | tf_op jit(solution)/shard_map/ppermute | solution.py:52
  66.4 3.3 %collective-permute-done.8.r1 = bf16[128,1536]{1,0:T(8,128)(2,1)S(1)} collective-permute-done((bf16[128,1536]{1,0:T(8,128)(2,1)S(1)}, bf16[128,1536]{1,0:T(8,128)(2,1)S(1)}, u32[]{:S(2)}, u32[]{:S(2)}) %collective-permute-start.8) | collective-permute-done | bytes 393248 | tf_op jit(solution)/shard_map/ppermute | solution.py:52
  69.6 6.5 %collective-permute-done.9.r2 = bf16[128,1536]{1,0:T(8,128)(2,1)S(1)} collective-permute-done((bf16[128,1536]{1,0:T(8,128)(2,1)S(1)}, bf16[128,1536]{1,0:T(8,128)(2,1)S(1)}, u32[]{:S(2)}, u32[]{:S(2)}) %collective-permute-start.9) | collective-permute-done | bytes 393248 | tf_op jit(solution)/shard_map/ppermute | solution.py:52
  76.3 2.7 %collective-permute-start.16 = (bf16[1536,768]{1,0:T(8,128)(2,1)S(1)}, bf16[1536,768]{1,0:T(8,128)(2,1)S(1)}, u32[]{:S(2)}, u32[]{:S(2)}) collective-permute-start(bf16[1536,768]{1,0:T(8,128)(2,1)S(1)} %copy-done.3), channel_id=1, source_target_pairs={{0,1},{1,0},{2,3},{3,2},{4,5},{5,4},{6,7},{7,6},{8,9},{9,8},{10,11... | collective-permute-start | bytes 7077896 | tf_op jit(solution)/shard_map/ppermute | solution.py:40
  79.0 5.3 %collective-permute-start.12 = (bf16[128,1664]{1,0:T(8,128)(2,1)S(1)}, bf16[128,1664]{1,0:T(8,128)(2,1)S(1)}, u32[]{:S(2)}, u32[]{:S(2)}) collective-permute-start(bf16[128,1664]{1,0:T(8,128)(2,1)S(1)} %back_sum.1.mine), channel_id=1, source_target_pairs={{0,32},{32,0},{64,96},{96,64},{128,160},{160,128},{192,224},{224,1... | collective-permute-start | bytes 1277960 | tf_op jit(solution)/shard_map/ppermute | solution.py:56
  86.1 8.6 %collective-permute-done.13.r1 = bf16[2,128,768]{2,1,0:T(8,128)(2,1)S(1)} collective-permute-done((bf16[2,128,768]{2,1,0:T(8,128)(2,1)S(1)}, bf16[2,128,768]{2,1,0:T(8,128)(2,1)S(1)}, u32[]{:S(2)}, u32[]{:S(2)}) %collective-permute-start.13) | collective-permute-done | bytes 393248 | tf_op jit(solution)/shard_map/ppermute | solution.py:52
  94.7 1.8 collective-permute-done.14.r3
  96.5 6.6 %collective-permute-done.15.r2 = bf16[2,128,768]{2,1,0:T(8,128)(2,1)S(1)} collective-permute-done((bf16[2,128,768]{2,1,0:T(8,128)(2,1)S(1)}, bf16[2,128,768]{2,1,0:T(8,128)(2,1)S(1)}, u32[]{:S(2)}, u32[]{:S(2)}) %collective-permute-start.15) | collective-permute-done | bytes 393248 | tf_op jit(solution)/shard_map/ppermute | solution.py:52
  103.8 2.5 %collective-permute-start.20 = (bf16[512,1536]{1,0:T(8,128)(2,1)S(1)}, bf16[512,1536]{1,0:T(8,128)(2,1)S(1)}, u32[]{:S(2)}, u32[]{:S(2)}) collective-permute-start(bf16[512,1536]{1,0:T(8,128)(2,1)S(1)} %bitcast.13), channel_id=1, source_target_pairs={{0,1},{1,0},{2,3},{3,2},{4,5},{5,4},{6,7},{7,6},{8,9},{9,8},{10,11... | collective-permute-start | bytes 4718600 | tf_op jit(solution)/shard_map/ppermute | solution.py:40
  109.3 7.0 %w_out_grad.1 = bf16[768,1536]{1,0:T(8,128)(2,1)} custom-call(bf16[2,128,768]{2,1,0:T(8,128)(2,1)S(1)} %bitcast.12, bf16[2,128,768]{2,1,0:T(8,128)(2,1)S(1)} %collective-permute-done.13.r1, bf16[2,128,768]{2,1,0:T(8,128)(2,1)S(1)} %collective-permute-done.15.r2, bf16[2,128,768]{2,1,0:T(8,128)(2,1)S(1)} %collective-permute-done.14.r3, ...), custom_call_target="tpu_custom_call" | custom-call | flops 2415919104 | bytes 7077888 | tf_op jit(solution)/shard_map/w_out_grad/pallas_call | solution.py:326
  117.7 2.4 %collective-permute-done.18.m2 = bf16[128,1664]{1,0:T(8,128)(2,1)S(1)} collective-permute-done((bf16[128,1664]{1,0:T(8,128)(2,1)S(1)}, bf16[128,1664]{1,0:T(8,128)(2,1)S(1)}, u32[]{:S(2)}, u32[]{:S(2)}) %collective-permute-start.18) | collective-permute-done | bytes 426016 | tf_op jit(solution)/shard_map/ppermute | solution.py:52
  120.1 9.8 %collective-permute-done.19.m3 = bf16[128,1664]{1,0:T(8,128)(2,1)S(1)} collective-permute-done((bf16[128,1664]{1,0:T(8,128)(2,1)S(1)}, bf16[128,1664]{1,0:T(8,128)(2,1)S(1)}, u32[]{:S(2)}, u32[]{:S(2)}) %collective-permute-start.19) | collective-permute-done | bytes 426016 | tf_op jit(solution)/shard_map/ppermute | solution.py:52
  129.8 6.3 %input_grad.1 = (f32[128,1536]{1,0:T(8,128)S(1)}, bf16[128,1664]{1,0:T(8,128)(2,1)S(1)}, bf16[128,1664]{1,0:T(8,128)(2,1)}, bf16[128,1664]{1,0:T(8,128)(2,1)}, bf16[512,768]{1,0:T(8,128)(2,1)}) custom-call(s32[2]{0:T(128)S(1)} %pad_add_fusion.t.at, bf16[128,1664]{1,0:T(8,128)(2,1)S(1)} %slope.1.m0, bf16[128,1664]{1,0:T(8,128)(2,1)S(1)} %collective-permute-done.17.m1, ...), custom_call_target="tpu_custom_call" | custom-call | flops 2415919104 | bytes 9273352 | tf_op jit(solution)/shard_map/input_grad/pallas_call | solution.py:326
  136.8 2.7 %collective-permute-start.22 = (bf16[128,1664]{1,0:T(8,128)(2,1)}, bf16[128,1664]{1,0:T(8,128)(2,1)S(1)}, u32[]{:S(2)}, u32[]{:S(2)}) collective-permute-start(bf16[128,1664]{1,0:T(8,128)(2,1)} %get-tuple-element.99), channel_id=1, source_target_pairs={{0,16},{1,17},{2,18},{3,19},{4,20},{5,21},{6,22},{7,23},{8,24},{9,... | collective-permute-start | bytes 1277960 | tf_op jit(solution)/shard_map/ppermute | solution.py:48
  140.8 1.9 %copy-done.1 = bf16[1024,1536]{1,0:T(8,128)(2,1)S(1)} copy-done((bf16[1024,1536]{1,0:T(8,128)(2,1)S(1)}, bf16[1024,1536]{1,0:T(8,128)(2,1)}, u32[]{:S(2)}) %copy-start.1) | copy-done | bytes 3145752
  144.7 6.8 %w_in_grad.1 = bf16[1536,768]{1,0:T(8,128)(2,1)} custom-call(s32[2]{0:T(128)S(1)} %pad_add_fusion.t.at, bf16[1024,1536]{1,0:T(8,128)(2,1)S(1)} %copy-done.1, bf16[128,1664]{1,0:T(8,128)(2,1)S(1)} %slope.1.m0, bf16[128,1664]{1,0:T(8,128)(2,1)S(1)} %collective-permute-done.17.m1, bf16[128,1664]{1,0:T(8,128)(2,1)S(1)} %copy-done.5, ...), custom_call_target="tpu_custom_call" | custom-call | flops 2415919104 | bytes 7995400 | tf_op jit(solution)/shard_map/w_in_grad/pallas_call | solution.py:326
  151.6 7.0 %collective-permute-done.22.r2 = bf16[128,1664]{1,0:T(8,128)(2,1)S(1)} collective-permute-done((bf16[128,1664]{1,0:T(8,128)(2,1)}, bf16[128,1664]{1,0:T(8,128)(2,1)S(1)}, u32[]{:S(2)}, u32[]{:S(2)}) %collective-permute-start.22) | collective-permute-done | bytes 426016 | tf_op jit(solution)/shard_map/ppermute | solution.py:48
  162.8 4.2 %collective-permute-done.26.r2 = bf16[32,1664]{1,0:T(8,128)(2,1)S(1)} collective-permute-done((bf16[32,1664]{1,0:T(8,128)(2,1)S(1)}, bf16[32,1664]{1,0:T(8,128)(2,1)S(1)}, u32[]{:S(2)}, u32[]{:S(2)}) %collective-permute-start.26) | collective-permute-done | bytes 106528 | tf_op jit(solution)/shard_map/ppermute | solution.py:44
  169.1 4.1 %collective-permute-start.28 = (f32[8,128]{1,0:T(8,128)S(1)}, f32[8,128]{1,0:T(8,128)S(1)}, u32[]{:S(2)}, u32[]{:S(2)}) collective-permute-start(f32[8,128]{1,0:T(8,128)S(1)} %get-tuple-element.113), channel_id=1, source_target_pairs={{0,1},{1,0},{2,3},{3,2},{4,5},{5,4},{6,7},{7,6},{8,9},{9,8},{10,11... | collective-permute-start | bytes 12296 | tf_op jit(solution)/shard_map/ppermute | solution.py:40
  (59 shorter events, 25.8 us)
Async XLA Ops:
  7.2 133.6 %all-gather.2.cloned.1.call-start = ((), (), s32[]{:S(2)}) async-start(), calls=%async_computation | async-start | bytes 3244032 | tf_op jit(solution)/shard_map/all_gather | solution.py:354
  7.3 5.5 %collective-permute-start = (bf16[32,1536]{1,0:T(8,128)(2,1)}, bf16[32,1536]{1,0:T(8,128)(2,1)S(1)}, u32[]{:S(2)}, u32[]{:S(2)}) collective-permute-start(bf16[32,1536]{1,0:T(8,128)(2,1)} %a0), channel_id=1, source_target_pairs={{0,2},{1,3},{2,0},{3,1},{4,6},{5,7},{6,4},{7,5},{8,10},{9,11},{10,... | collective-permute-start | bytes 294920 | tf_op jit(solution)/shard_map/ppermute | solution.py:44
  9.8 5.8 %collective-permute-start.1 = (bf16[32,1536]{1,0:T(8,128)(2,1)}, bf16[32,1536]{1,0:T(8,128)(2,1)S(1)}, u32[]{:S(2)}, u32[]{:S(2)}) collective-permute-start(bf16[32,1536]{1,0:T(8,128)(2,1)} %a0), channel_id=1, source_target_pairs={{0,4},{1,5},{2,6},{3,7},{4,0},{5,1},{6,2},{7,3},{8,12},{9,13},{10,... | collective-permute-start | bytes 294920 | tf_op jit(solution)/shard_map/ppermute | solution.py:44
  12.8 6.5 %collective-permute-start.2 = (bf16[32,1536]{1,0:T(8,128)(2,1)}, bf16[32,1536]{1,0:T(8,128)(2,1)S(1)}, u32[]{:S(2)}, u32[]{:S(2)}) collective-permute-start(bf16[32,1536]{1,0:T(8,128)(2,1)} %a0), channel_id=1, source_target_pairs={{0,6},{1,7},{2,4},{3,5},{4,2},{5,3},{6,0},{7,1},{8,14},{9,15},{10,... | collective-permute-start | bytes 294920 | tf_op jit(solution)/shard_map/ppermute | solution.py:44
  19.3 27.5 %collective-permute-start.6 = (bf16[768,1536]{1,0:T(8,128)(2,1)}, bf16[768,1536]{1,0:T(8,128)(2,1)S(1)}, u32[]{:S(2)}, u32[]{:S(2)}) collective-permute-start(bf16[768,1536]{1,0:T(8,128)(2,1)} %wa.2), channel_id=1, source_target_pairs={{0,1},{1,0},{2,3},{3,2},{4,5},{5,4},{6,7},{7,6},{8,9},{9,8},{10,11... | collective-permute-start | bytes 7077896 | tf_op jit(solution)/shard_map/ppermute | solution.py:40
  22.9 19.4 %collective-permute-start.3 = (bf16[128,1536]{1,0:T(8,128)(2,1)S(1)}, bf16[128,1536]{1,0:T(8,128)(2,1)S(1)}, u32[]{:S(2)}, u32[]{:S(2)}) collective-permute-start(bf16[128,1536]{1,0:T(8,128)(2,1)S(1)} %get-tuple-element.67.g0), channel_id=1, source_target_pairs={{0,24},{1,25},{2,26},{3,27},{4,28},{5,29},{6,30},{7,31},{8,0},{9,1... | collective-permute-start | bytes 1179656 | tf_op jit(solution)/shard_map/ppermute | solution.py:48
  25.7 16.6 %collective-permute-start.4 = (bf16[128,1536]{1,0:T(8,128)(2,1)S(1)}, bf16[128,1536]{1,0:T(8,128)(2,1)S(1)}, u32[]{:S(2)}, u32[]{:S(2)}) collective-permute-start(bf16[128,1536]{1,0:T(8,128)(2,1)S(1)} %get-tuple-element.67.g0), channel_id=1, source_target_pairs={{0,16},{1,17},{2,18},{3,19},{4,20},{5,21},{6,22},{7,23},{8,24},{9,... | collective-permute-start | bytes 1179656 | tf_op jit(solution)/shard_map/ppermute | solution.py:48
  26.1 20.7 %collective-permute-start.5 = (bf16[128,1536]{1,0:T(8,128)(2,1)S(1)}, bf16[128,1536]{1,0:T(8,128)(2,1)}, u32[]{:S(2)}, u32[]{:S(2)}) collective-permute-start(bf16[128,1536]{1,0:T(8,128)(2,1)S(1)} %get-tuple-element.67.g0), channel_id=1, source_target_pairs={{0,8},{1,9},{2,10},{3,11},{4,12},{5,13},{6,14},{7,15},{8,16},{9,17... | collective-permute-start | bytes 1179656 | tf_op jit(solution)/shard_map/ppermute | solution.py:48
  26.8 9.8 %collective-permute-start.7 = (bf16[128,768]{1,0:T(8,128)(2,1)}, bf16[128,768]{1,0:T(8,128)(2,1)S(1)}, u32[]{:S(2)}, u32[]{:S(2)}) collective-permute-start(bf16[128,768]{1,0:T(8,128)(2,1)} %here.1), channel_id=1, source_target_pairs={{0,32},{32,0},{64,96},{96,64},{128,160},{160,128},{192,224},{224,1... | collective-permute-start | bytes 589832 | tf_op jit(solution)/shard_map/ppermute | solution.py:56
  55.0 21.3 %copy-start.3 = (bf16[1536,768]{1,0:T(8,128)(2,1)S(1)}, bf16[1536,768]{1,0:T(8,128)(2,1)}, u32[]{:S(2)}) copy-start(bf16[1536,768]{1,0:T(8,128)(2,1)} %wa.3) | copy-start | bytes 7077892
  55.0 11.4 %collective-permute-start.10 = (bf16[128,1536]{1,0:T(8,128)(2,1)S(1)}, bf16[128,1536]{1,0:T(8,128)(2,1)S(1)}, u32[]{:S(2)}, u32[]{:S(2)}) collective-permute-start(bf16[128,1536]{1,0:T(8,128)(2,1)S(1)} %get-tuple-element.77), channel_id=1, source_target_pairs={{0,192},{32,224},{64,0},{96,32},{128,64},{160,96},{192,128},{224,1... | collective-permute-start | bytes 1179656 | tf_op jit(solution)/shard_map/ppermute | solution.py:52
  57.5 12.1 %collective-permute-start.8 = (bf16[128,1536]{1,0:T(8,128)(2,1)S(1)}, bf16[128,1536]{1,0:T(8,128)(2,1)S(1)}, u32[]{:S(2)}, u32[]{:S(2)}) collective-permute-start(bf16[128,1536]{1,0:T(8,128)(2,1)S(1)} %get-tuple-element.75), channel_id=1, source_target_pairs={{0,64},{32,96},{64,128},{96,160},{128,192},{160,224},{192,0},{224,... | collective-permute-start | bytes 1179656 | tf_op jit(solution)/shard_map/ppermute | solution.py:52
  57.5 18.6 %collective-permute-start.9 = (bf16[128,1536]{1,0:T(8,128)(2,1)S(1)}, bf16[128,1536]{1,0:T(8,128)(2,1)S(1)}, u32[]{:S(2)}, u32[]{:S(2)}) collective-permute-start(bf16[128,1536]{1,0:T(8,128)(2,1)S(1)} %get-tuple-element.76), channel_id=1, source_target_pairs={{0,128},{32,160},{64,192},{96,224},{128,0},{160,32},{192,64},{224,... | collective-permute-start | bytes 1179656 | tf_op jit(solution)/shard_map/ppermute | solution.py:52
  59.3 2.4 %collective-permute-start.11 = (bf16[128,768]{1,0:T(8,128)(2,1)S(1)}, bf16[128,768]{1,0:T(8,128)(2,1)S(1)}, u32[]{:S(2)}, u32[]{:S(2)}) collective-permute-start(bf16[128,768]{1,0:T(8,128)(2,1)S(1)} %bitcast.15), channel_id=1, source_target_pairs={{0,1},{1,0},{2,3},{3,2},{4,5},{5,4},{6,7},{7,6},{8,9},{9,8},{10,11... | collective-permute-start | bytes 589832 | tf_op jit(solution)/shard_map/ppermute | solution.py:40
  76.3 26.8 %collective-permute-start.16 = (bf16[1536,768]{1,0:T(8,128)(2,1)S(1)}, bf16[1536,768]{1,0:T(8,128)(2,1)S(1)}, u32[]{:S(2)}, u32[]{:S(2)}) collective-permute-start(bf16[1536,768]{1,0:T(8,128)(2,1)S(1)} %copy-done.3), channel_id=1, source_target_pairs={{0,1},{1,0},{2,3},{3,2},{4,5},{5,4},{6,7},{7,6},{8,9},{9,8},{10,11... | collective-permute-start | bytes 7077896 | tf_op jit(solution)/shard_map/ppermute | solution.py:40
  79.0 24.1 %collective-permute-start.12 = (bf16[128,1664]{1,0:T(8,128)(2,1)S(1)}, bf16[128,1664]{1,0:T(8,128)(2,1)S(1)}, u32[]{:S(2)}, u32[]{:S(2)}) collective-permute-start(bf16[128,1664]{1,0:T(8,128)(2,1)S(1)} %back_sum.1.mine), channel_id=1, source_target_pairs={{0,32},{32,0},{64,96},{96,64},{128,160},{160,128},{192,224},{224,1... | collective-permute-start | bytes 1277960 | tf_op jit(solution)/shard_map/ppermute | solution.py:56
  84.3 10.3 %collective-permute-start.13 = (bf16[2,128,768]{2,1,0:T(8,128)(2,1)S(1)}, bf16[2,128,768]{2,1,0:T(8,128)(2,1)S(1)}, u32[]{:S(2)}, u32[]{:S(2)}) collective-permute-start(bf16[2,128,768]{2,1,0:T(8,128)(2,1)S(1)} %bitcast.8), channel_id=1, source_target_pairs={{0,192},{32,224},{64,0},{96,32},{128,64},{160,96},{192,128},{224,1... | collective-permute-start | bytes 1179656 | tf_op jit(solution)/shard_map/ppermute | solution.py:52
  84.3 12.1 %collective-permute-start.14 = (bf16[2,128,768]{2,1,0:T(8,128)(2,1)S(1)}, bf16[2,128,768]{2,1,0:T(8,128)(2,1)S(1)}, u32[]{:S(2)}, u32[]{:S(2)}) collective-permute-start(bf16[2,128,768]{2,1,0:T(8,128)(2,1)S(1)} %bitcast.9), channel_id=1, source_target_pairs={{0,64},{32,96},{64,128},{96,160},{128,192},{160,224},{192,0},{224,... | collective-permute-start | bytes 1179656 | tf_op jit(solution)/shard_map/ppermute | solution.py:52
  85.8 17.3 %collective-permute-start.15 = (bf16[2,128,768]{2,1,0:T(8,128)(2,1)S(1)}, bf16[2,128,768]{2,1,0:T(8,128)(2,1)S(1)}, u32[]{:S(2)}, u32[]{:S(2)}) collective-permute-start(bf16[2,128,768]{2,1,0:T(8,128)(2,1)S(1)} %bitcast.10), channel_id=1, source_target_pairs={{0,128},{32,160},{64,192},{96,224},{128,0},{160,32},{192,64},{224,... | collective-permute-start | bytes 1179656 | tf_op jit(solution)/shard_map/ppermute | solution.py:52
  103.8 5.5 %collective-permute-start.20 = (bf16[512,1536]{1,0:T(8,128)(2,1)S(1)}, bf16[512,1536]{1,0:T(8,128)(2,1)S(1)}, u32[]{:S(2)}, u32[]{:S(2)}) collective-permute-start(bf16[512,1536]{1,0:T(8,128)(2,1)S(1)} %bitcast.13), channel_id=1, source_target_pairs={{0,1},{1,0},{2,3},{3,2},{4,5},{5,4},{6,7},{7,6},{8,9},{9,8},{10,11... | collective-permute-start | bytes 4718600 | tf_op jit(solution)/shard_map/ppermute | solution.py:40
  106.3 11.4 %collective-permute-start.17 = (bf16[128,1664]{1,0:T(8,128)(2,1)S(1)}, bf16[128,1664]{1,0:T(8,128)(2,1)S(1)}, u32[]{:S(2)}, u32[]{:S(2)}) collective-permute-start(bf16[128,1664]{1,0:T(8,128)(2,1)S(1)} %slope.1.m0), channel_id=1, source_target_pairs={{0,192},{32,224},{64,0},{96,32},{128,64},{160,96},{192,128},{224,1... | collective-permute-start | bytes 1277960 | tf_op jit(solution)/shard_map/ppermute | solution.py:52
  107.5 12.6 %collective-permute-start.18 = (bf16[128,1664]{1,0:T(8,128)(2,1)S(1)}, bf16[128,1664]{1,0:T(8,128)(2,1)S(1)}, u32[]{:S(2)}, u32[]{:S(2)}) collective-permute-start(bf16[128,1664]{1,0:T(8,128)(2,1)S(1)} %slope.1.m0), channel_id=1, source_target_pairs={{0,128},{32,160},{64,192},{96,224},{128,0},{160,32},{192,64},{224,... | collective-permute-start | bytes 1277960 | tf_op jit(solution)/shard_map/ppermute | solution.py:52
  108.0 21.8 %collective-permute-start.19 = (bf16[128,1664]{1,0:T(8,128)(2,1)S(1)}, bf16[128,1664]{1,0:T(8,128)(2,1)S(1)}, u32[]{:S(2)}, u32[]{:S(2)}) collective-permute-start(bf16[128,1664]{1,0:T(8,128)(2,1)S(1)} %slope.1.m0), channel_id=1, source_target_pairs={{0,64},{32,96},{64,128},{96,160},{128,192},{160,224},{192,0},{224,... | collective-permute-start | bytes 1277960 | tf_op jit(solution)/shard_map/ppermute | solution.py:52
  120.1 16.1 %copy-start.4 = (bf16[128,1664]{1,0:T(8,128)(2,1)}, bf16[128,1664]{1,0:T(8,128)(2,1)S(1)}, u32[]{:S(2)}) copy-start(bf16[128,1664]{1,0:T(8,128)(2,1)S(1)} %collective-permute-done.18.m2) | copy-start | bytes 1277956
  136.2 4.6 %collective-permute-start.24 = (bf16[512,768]{1,0:T(8,128)(2,1)}, bf16[512,768]{1,0:T(8,128)(2,1)}, u32[]{:S(2)}, u32[]{:S(2)}) collective-permute-start(bf16[512,768]{1,0:T(8,128)(2,1)} %get-tuple-element.102), channel_id=1, source_target_pairs={{0,1},{1,0},{2,3},{3,2},{4,5},{5,4},{6,7},{7,6},{8,9},{9,8},{10,11... | collective-permute-start | bytes 2359304 | tf_op jit(solution)/shard_map/ppermute | solution.py:40
  136.8 14.8 %collective-permute-start.21 = (bf16[128,1664]{1,0:T(8,128)(2,1)S(1)}, bf16[128,1664]{1,0:T(8,128)(2,1)S(1)}, u32[]{:S(2)}, u32[]{:S(2)}) collective-permute-start(bf16[128,1664]{1,0:T(8,128)(2,1)S(1)} %get-tuple-element.98.mine), channel_id=1, source_target_pairs={{0,8},{1,9},{2,10},{3,11},{4,12},{5,13},{6,14},{7,15},{8,16},{9,17... | collective-permute-start | bytes 1277960 | tf_op jit(solution)/shard_map/ppermute | solution.py:48
  136.8 21.7 %collective-permute-start.22 = (bf16[128,1664]{1,0:T(8,128)(2,1)}, bf16[128,1664]{1,0:T(8,128)(2,1)S(1)}, u32[]{:S(2)}, u32[]{:S(2)}) collective-permute-start(bf16[128,1664]{1,0:T(8,128)(2,1)} %get-tuple-element.99), channel_id=1, source_target_pairs={{0,16},{1,17},{2,18},{3,19},{4,20},{5,21},{6,22},{7,23},{8,24},{9,... | collective-permute-start | bytes 1277960 | tf_op jit(solution)/shard_map/ppermute | solution.py:48
  139.6 19.5 %collective-permute-start.23 = (bf16[128,1664]{1,0:T(8,128)(2,1)}, bf16[128,1664]{1,0:T(8,128)(2,1)S(1)}, u32[]{:S(2)}, u32[]{:S(2)}) collective-permute-start(bf16[128,1664]{1,0:T(8,128)(2,1)} %get-tuple-element.100), channel_id=1, source_target_pairs={{0,24},{1,25},{2,26},{3,27},{4,28},{5,29},{6,30},{7,31},{8,0},{9,1... | collective-permute-start | bytes 1277960 | tf_op jit(solution)/shard_map/ppermute | solution.py:48
  159.2 3.6 %collective-permute-start.25 = (bf16[32,1664]{1,0:T(8,128)(2,1)S(1)}, bf16[32,1664]{1,0:T(8,128)(2,1)S(1)}, u32[]{:S(2)}, u32[]{:S(2)}) collective-permute-start(bf16[32,1664]{1,0:T(8,128)(2,1)S(1)} %get-tuple-element.107.mine), channel_id=1, source_target_pairs={{0,2},{1,3},{2,0},{3,1},{4,6},{5,7},{6,4},{7,5},{8,10},{9,11},{10,... | collective-permute-start | bytes 319496 | tf_op jit(solution)/shard_map/ppermute | solution.py:44
  160.7 6.4 %collective-permute-start.26 = (bf16[32,1664]{1,0:T(8,128)(2,1)S(1)}, bf16[32,1664]{1,0:T(8,128)(2,1)S(1)}, u32[]{:S(2)}, u32[]{:S(2)}) collective-permute-start(bf16[32,1664]{1,0:T(8,128)(2,1)S(1)} %get-tuple-element.108), channel_id=1, source_target_pairs={{0,4},{1,5},{2,6},{3,7},{4,0},{5,1},{6,2},{7,3},{8,12},{9,13},{10,... | collective-permute-start | bytes 319496 | tf_op jit(solution)/shard_map/ppermute | solution.py:44
  161.2 7.2 %collective-permute-start.27 = (bf16[32,1664]{1,0:T(8,128)(2,1)S(1)}, bf16[32,1664]{1,0:T(8,128)(2,1)S(1)}, u32[]{:S(2)}, u32[]{:S(2)}) collective-permute-start(bf16[32,1664]{1,0:T(8,128)(2,1)S(1)} %get-tuple-element.109), channel_id=1, source_target_pairs={{0,6},{1,7},{2,4},{3,5},{4,2},{5,3},{6,0},{7,1},{8,14},{9,15},{10,... | collective-permute-start | bytes 319496 | tf_op jit(solution)/shard_map/ppermute | solution.py:44
  169.1 4.9 %collective-permute-start.28 = (f32[8,128]{1,0:T(8,128)S(1)}, f32[8,128]{1,0:T(8,128)S(1)}, u32[]{:S(2)}, u32[]{:S(2)}) collective-permute-start(f32[8,128]{1,0:T(8,128)S(1)} %get-tuple-element.113), channel_id=1, source_target_pairs={{0,1},{1,0},{2,3},{3,2},{4,5},{5,4},{6,7},{7,6},{8,9},{9,8},{10,11... | collective-permute-start | bytes 12296 | tf_op jit(solution)/shard_map/ppermute | solution.py:40
  (7 other events, 13.8 us)
Sparse Core Ops, SparseCore 0:
  26.9 67.1 all-gather.1

commit v5 on v4

--- a/solution.py
+++ b/solution.py
@@ -61,22 +61,34 @@
     return [v, near, far, behind]
 
 
+def message(rows):
+    return like(W // 128 * rows + 16, 128)
+
+
+def tile(c, rows, first=0, count=None):
+    return slice(c * rows + first, c * rows + first + (count or rows))
+
+
 def put_tops(ref, top_h, top_y):
-    row = lax.broadcasted_iota(jnp.int32, (ref.shape[0], 128), 0)
+    row = lax.broadcasted_iota(jnp.int32, (16, 128), 0)
     high = top_h.astype(bf16).astype(f32)
     mid = (top_h - high).astype(bf16).astype(f32)
     low = top_h - high - mid
     extra = jnp.where(row == 0, high, jnp.where(row == 1, mid, jnp.where(row == 2, low, 0.0)))
-    ref[:, D : D + 128] = jnp.where(row == 3, top_y, extra).astype(bf16)
+    ref[ref.shape[0] - 16 :] = jnp.where(row == 3, top_y, extra).astype(bf16)
 
 
 def get_tops(refs):
     top_h = top_y = jnp.zeros((1, 128), f32)
     for ref in refs:
-        extra = ref[0:16, D : D + 128].astype(f32)
+        extra = ref[ref.shape[0] - 16 :].astype(f32)
         top_h = jnp.maximum(top_h, extra[0:1] + extra[1:2] + extra[2:3])
         top_y = jnp.maximum(top_y, extra[3:4])
     return top_h, top_y
+
+
+def columns(c):
+    return slice(c * 128, (c + 1) * 128)
 
 
 def stack_kernel(a0, a1, a2, a3, stacked, tops):
@@ -87,6 +99,14 @@
     for k in range(1, D // 128):
         lanes = jnp.maximum(lanes, top[:, 128 * k : 128 * (k + 1)])
     tops[...] = jnp.broadcast_to(lanes, (8, 128))
+
+
+def join_kernel(a0, a1, a2, a3, out, sems):
+    moves = [copy(a, out.at[k], sems.at[k]) for k, a in enumerate((a0, a1, a2, a3))]
+    for move in moves:
+        move.start()
+    for move in moves:
+        move.wait()
 
 
 def place(at):
@@ -156,34 +176,29 @@
 
 
 def sum_kernel(own, r1, r2, r3, tops, msg):
-    for k in range(T // 16):
-        at = slice(16 * k, 16 * (k + 1))
+    for c in range(W // 128):
+        at = (slice(None), columns(c))
         total = own[at] + r1[at].astype(f32) + r2[at].astype(f32) + r3[at].astype(f32)
-        msg[at, :W] = total.astype(bf16)
+        msg[tile(c, T)] = total.astype(bf16)
     put_tops(msg, jnp.zeros((1, 128), f32), tops[0:1])
 
 
 def slope_kernel(mine, other, pre_a, pre_b, msg):
     _, top_y = get_tops((mine, other))
-    top = jnp.zeros((16, FF), f32)
-    for k in range(T // 16):
-        at = slice(16 * k, 16 * (k + 1))
-        for half, pre in enumerate((pre_a, pre_b)):
-            cols = slice(half * FF, (half + 1) * FF)
-            back = mine[at, cols].astype(f32) + other[at, cols].astype(f32)
-            hidden_grad = back * gelu_slope(pre[at].astype(f32))
-            top = jnp.maximum(top, jnp.abs(hidden_grad))
-            msg[at, cols] = hidden_grad.astype(bf16)
-    top = jnp.max(top, axis=0, keepdims=True)
-    top_h = top[:, :128]
-    for k in range(1, FF // 128):
-        top_h = jnp.maximum(top_h, top[:, 128 * k : 128 * (k + 1)])
+    top_h = jnp.zeros((1, 128), f32)
+    for c in range(W // 128):
+        pre, k = (pre_a, c) if c < FF // 128 else (pre_b, c - FF // 128)
+        back = mine[tile(c, T)].astype(f32) + other[tile(c, T)].astype(f32)
+        hidden_grad = back * gelu_slope(pre[:, columns(k)].astype(f32))
+        top_h = jnp.maximum(top_h, jnp.max(jnp.abs(hidden_grad), axis=0, keepdims=True))
+        msg[tile(c, T)] = hidden_grad.astype(bf16)
     put_tops(msg, top_h, top_y)
 
 
-def grad_kernel(t, m0, m1, m2, m3, wa, wb, own, p1, p2, p3, hq_b, blocks, weights, sems, wsems):
+def grad_kernel(t, m0, m1, m2, m3, wa, wb, own, p1, p2, p3, hq_a, hq_b, blocks, weights, sems, wsems):
     i = pl.program_id(0)
     x, _, y, _, _ = place(t)
+    half = FF // 128
 
     def weight(k):
         rows = slice(k * C, (k + 1) * C)
@@ -194,8 +209,14 @@
 
     def blocks_out():
         return [
-            copy(blocks.at[(s - y + x) & 3, :, FF:W], hq_b.at[s * T : (s + 1) * T], sems.at[4 + s])
+            copy(
+                blocks.at[(s - y + x) & 3, tile(k * half + c, T)],
+                out.at[s * T : (s + 1) * T, columns(c)],
+                sems.at[4 + (k * 4 + s) * half + c],
+            )
+            for k, out in enumerate((hq_a, hq_b))
             for s in range(4)
+            for c in range(half)
         ]
 
     @pl.when(i == 0)
@@ -220,12 +241,14 @@
             for move in weight(k):
                 move.wait()
 
-    hq = blocks[:, :, :W].reshape(4 * T, W)
-    out = across(hq[:, :FF], weights[0, i]) + across(hq[:, FF:], weights[1, i])
-    at = pl.ds(pl.multiple_of(i * C, C), C)
-    own[:, at] = out[:T]
+    tiles = [blocks[:, tile(c, T)].reshape(4 * T, 128) for c in range(2 * half)]
+    hq = [jnp.concatenate(part, axis=1) for part in (tiles[:half], tiles[half:])]
+    out = across(hq[0], weights[0, i]) + across(hq[1], weights[1, i])
+    own[:, pl.ds(pl.multiple_of(i * C, C), C)] = out[:T]
     for k, p in enumerate((p1, p2, p3)):
-        p[:, at] = out[(k + 1) * T : (k + 2) * T].astype(bf16)
+        for c in range(C // 128):
+            rows = pl.ds(pl.multiple_of((i * (C // 128) + c) * T, T), T)
+            p[rows] = out[(k + 1) * T : (k + 2) * T, columns(c)].astype(bf16)
 
     @pl.when(i == pl.num_programs(0) - 1)
     def _():
@@ -236,17 +259,24 @@
 def gather_kernel(own, r1, r2, r3, mine, kept, s1, s2, s3):
     top_h, top_y = get_tops((r1, r2, r3, mine))
     for m, out in enumerate((kept, s1, s2, s3)):
-        at = slice(32 * m, 32 * (m + 1))
-        total = own[at] + r1[at, :D].astype(f32) + r2[at, :D].astype(f32) + r3[at, :D].astype(f32)
-        out[:, :D] = total.astype(out.dtype)
+        for c in range(D // 128):
+            at = tile(c, T, 32 * m, 32)
+            total = own[32 * m : 32 * (m + 1), columns(c)]
+            total = total + r1[at].astype(f32) + r2[at].astype(f32) + r3[at].astype(f32)
+            if m:
+                out[tile(c, 32)] = total.astype(bf16)
+            else:
+                out[:, columns(c)] = total
     for out in (s1, s2, s3):
         put_tops(out, top_h, top_y)
 
 
 def last_kernel(kept, r1, r2, r3, mine, out, tops):
     top_h, top_y = get_tops((r1, r2, r3, mine))
-    total = kept[...] + r1[:, :D].astype(f32) + r2[:, :D].astype(f32) + r3[:, :D].astype(f32)
-    out[...] = total.astype(bf16)
+    for c in range(D // 128):
+        at = tile(c, 32)
+        total = kept[:, columns(c)] + r1[at].astype(f32) + r2[at].astype(f32) + r3[at].astype(f32)
+        out[:, columns(c)] = total.astype(bf16)
     row = lax.broadcasted_iota(jnp.int32, (8, 128), 0)
     tops[...] = jnp.where(row == 0, top_y, jnp.where(row == 1, top_h, 0.0))
 
@@ -284,36 +314,39 @@
     out[...] = (over_tokens(hidden[0], half[0]) + over_tokens(hidden[1], half[1])).astype(bf16)
 
 
-def w_in_kernel(at, inputs, m0, m1, m2, m3, other, out, hq, cols, sems, csems):
+def w_in_kernel(t, inputs, inputs_o, mine, other, out, hq, cols, sems, csems):
     i = pl.program_id(0)
-    x, _, _, l, c = place(at)
-
-    def part(k):
-        return copy(inputs.at[:, k * B : (k + 1) * B], cols.at[k], csems.at[k])
+    x, _, y, _, _ = place(t)
+
+    def parts(k):
+        at = slice(k * B, (k + 1) * B)
+        return [copy(a.at[:, :, at], cols.at[k, s], csems.at[s, k]) for s, a in enumerate((inputs, inputs_o))]
 
     def blocks_in():
-        out = []
-        for k, m in enumerate((m0, m1, m2, m3)):
-            for s in range(4):
-                to = ((x + k) & 3) * 4 + (s ^ l)
-                rows = slice(s * 32, (s + 1) * 32)
-                out.append(copy(m.at[rows, 0:FF], hq.at[to, c], sems.at[len(out)]))
-                rows = slice(k * T + s * 32, k * T + (s + 1) * 32)
-                out.append(copy(other.at[rows], hq.at[to, 1 - c], sems.at[len(out)]))
-        return out
+        return [
+            copy(ref.at[k * T : (k + 1) * T], hq.at[s, (k + x - y) & 3], sems.at[4 * s + k])
+            for s, ref in enumerate((mine, other))
+            for k in range(4)
+        ]
 
     @pl.when(i == 0)
     def _():
         for move in blocks_in():
             move.start()
         for k in range(D // B):
-            part(k).start()
+            for move in parts(k):
+                move.start()
         for move in blocks_in():
             move.wait()
 
     for k in range(D // B):
-        pl.when(i == k)(part(k).wait)
-    out[...] = over_tokens(cols[i], hq[...].reshape(8 * T, FF)).astype(bf16)
+
+        @pl.when(i == k)
+        def _():
+            for move in parts(k):
+                move.wait()
+
+    out[...] = over_tokens(cols[i].reshape(8 * T, B), hq[...].reshape(8 * T, FF)).astype(bf16)
 
 
 def like(*shape, dtype=bf16):
@@ -351,16 +384,15 @@
     steps = D // B
     big = 2 * 4 * T * D * W
 
-    inputs_all = lax.all_gather(inputs, "col", axis=0, tiled=True)
-
     got = [to_l(out_grad, k) for k in (1, 2, 3)]
-    *got, w_out_late, pre_late = barrier((*got, w_out, preact))
+    w_out_o = to_core(w_out)
+    *got, w_out_o, pre_late, w_in_late = barrier((*got, w_out_o, preact, w_in))
     outs = [like(T, D), like(8, 128, dtype=f32)]
     grad, top_y = call(stack_kernel, "stack", outs, (out_grad, *got))
     grads = ring(grad, to_y)
-    w_out_o = to_core(w_out_late)
+    w_in_o = to_core(w_in_late)
     there = to_h(pre_late)
-    *grads, w_out_o, there = barrier((*grads, w_out_o, there))
+    *grads, w_in_o, there = barrier((*grads, w_in_o, there))
 
     args = (at, *grads, w_out, w_out_o, preact, there)
     outs = [like(T, W, dtype=f32)] + [like(T, W)] * 3
@@ -387,19 +419,58 @@
     )
     r2, r1, r3 = to_x(p2, 2), to_x(p1, 1), to_x(p3, 3)
     pre_b = to_core(pre_other.reshape(T, FF))
-    r1, r2, r3, pre_b = barrier((r1, r2, r3, pre_b))
-
-    (sent,) = call(sum_kernel, "back_sum", [like(T, W + 128)], (own, r1, r2, r3, top_y))
+    r3, inputs = barrier((r3, inputs))
+    got = [to_l(inputs, k) for k in (1, 2, 3)]
+    r1, r2, r3, pre_b, *got = barrier((r1, r2, r3, pre_b, *got))
+
+    (sent,) = call(sum_kernel, "back_sum", [message(T)], (own, r1, r2, r3, top_y))
     other = to_h(sent)
-    pre, sent, w_in_late = barrier((pre.reshape(2, T, FF), sent, w_in))
-    w_in_o = to_core(w_in_late)
-    pre_near, pre_behind, pre_far = to_x(pre, 3), to_x(pre, 1), to_x(pre, 2)
-    other, pre_near, pre_behind, pre_far, w_in_o = barrier((other, pre_near, pre_behind, pre_far, w_in_o))
+    pre, sent, *got = barrier((pre.reshape(2, T, FF), sent, *got))
+    pre_far = to_x(pre, 2)
+    outs = [like(T, D), like(8, 128, dtype=f32)]
+    token_inputs, _ = call(stack_kernel, "stack_inputs", outs, (inputs, *got))
+    token_inputs = ring(token_inputs, to_y)
+    outs = [like(4, T, D)]
+    (inputs_all,) = call(
+        join_kernel, "join_inputs", outs, token_inputs, in_specs=here(token_inputs), out_specs=here(outs), scratch_shapes=[dma((4,))]
+    )
+    other, pre_far, inputs_all = barrier((other, pre_far, inputs_all))
     pre_a = pre[0]
-    (msg,) = call(slope_kernel, "slope", [like(T, W + 128)], (sent, other, pre_a, pre_b))
+    (msg,) = call(slope_kernel, "slope", [message(T)], (sent, other, pre_a, pre_b))
     msgs = ring(msg, to_x)
     stacked, _ = barrier((stacked.reshape(4 * T, D), msg))
     stacked_o = to_core(stacked)
+    inputs_all, _ = barrier((inputs_all, msg))
+    inputs_o = to_core(inputs_all)
+    *far, stacked_o, inputs_o = barrier((*msgs[1:], stacked_o, inputs_o))
+    msgs = [msgs[0], *far]
+
+    args = (at, *msgs, w_in, w_in_o)
+    outs = [like(T, D, dtype=f32)] + [message(T)] * 3
+    apart = [like(4 * T, FF)] * 2
+    own, p1, p2, p3, hq_a, hq_b = call(
+        grad_kernel,
+        "input_grad",
+        outs + apart,
+        args,
+        big,
+        20,
+        grid_spec=pltpu.PrefetchScalarGridSpec(
+            num_scalar_prefetch=1,
+            grid=(D // C,),
+            in_specs=here(args[1:]),
+            out_specs=[whole(o) for o in outs] + here(apart),
+            scratch_shapes=[
+                pltpu.VMEM((4, *message(T).shape), bf16),
+                pltpu.VMEM((2, D // C, C, FF), bf16),
+                dma((52,)),
+                dma((2, D // C)),
+            ],
+        ),
+    )
+    r2, r1, r3 = to_y(p2, 2), to_y(p1, 1), to_y(p3, 3)
+    pre, hq_b = barrier((pre, hq_b))
+    pre_near, pre_behind = to_x(pre, 3), to_x(pre, 1)
     args = (pre, pre_near, pre_far, pre_behind, stacked, stacked_o)
     (w_out_grad,) = call(
         w_out_kernel,
@@ -419,35 +490,12 @@
             dma((2, steps)),
         ],
     )
-    *far, w_out_grad = barrier((*msgs[1:], w_out_grad))
-    msgs = [msgs[0], *far]
-
-    args = (at, *msgs, w_in, w_in_o)
-    outs = [like(T, D, dtype=f32)] + [like(T, D + 128)] * 3
-    apart = [like(4 * T, FF)]
-    own, p1, p2, p3, hq_b = call(
-        grad_kernel,
-        "input_grad",
-        outs + apart,
-        args,
-        big,
-        20,
-        grid_spec=pltpu.PrefetchScalarGridSpec(
-            num_scalar_prefetch=1,
-            grid=(D // C,),
-            in_specs=here(args[1:]),
-            out_specs=[whole(o) for o in outs] + here(apart),
-            scratch_shapes=[
-                pltpu.VMEM((4, T, W + 128), bf16),
-                pltpu.VMEM((2, D // C, C, FF), bf16),
-                dma((8,)),
-                dma((2, D // C)),
-            ],
-        ),
-    )
-    r2, r1, r3 = to_y(p2, 2), to_y(p1, 1), to_y(p3, 3)
+    r1, r2, r3, w_out_grad, hq_b = barrier((r1, r2, r3, w_out_grad, hq_b))
+    outs = [like(32, D, dtype=f32)] + [message(32)] * 3
+    kept, s1, s2, s3 = call(gather_kernel, "y_sum", outs, (own, r1, r2, r3, p1))
+    r2, r3, r1 = to_l(s2, 2), to_l(s3, 3), to_l(s1, 1)
     hq_o = to_core(hq_b)
-    args = (at, inputs_all, *msgs, hq_o)
+    args = (at, inputs_all, inputs_o, hq_a, hq_o)
     (w_in_grad,) = call(
         w_in_kernel,
         "w_in_grad",
@@ -461,17 +509,14 @@
             in_specs=here(args[1:]),
             out_specs=[pl.BlockSpec((B, FF), lambda i, t: (i, 0))],
             scratch_shapes=[
-                pltpu.VMEM((16, 2, 32, FF), bf16),
-                pltpu.VMEM((steps, 8 * T, B), bf16),
-                dma((32,)),
-                dma((steps,)),
+                pltpu.VMEM((2, 4, T, FF), bf16),
+                pltpu.VMEM((steps, 2, 4, T, B), bf16),
+                dma((8,)),
+                dma((2, steps)),
             ],
         ),
     )
     r1, r2, r3, w_in_grad = barrier((r1, r2, r3, w_in_grad))
-    outs = [like(32, D, dtype=f32)] + [like(32, D + 128)] * 3
-    kept, s1, s2, s3 = call(gather_kernel, "y_sum", outs, (own, r1, r2, r3, p1))
-    r2, r3, r1 = to_l(s2, 2), to_l(s3, 3), to_l(s1, 1)
     outs = [like(32, D), like(8, 128, dtype=f32)]
     input_grad, tops = call(last_kernel, "l_sum", outs, (kept, r1, r2, r3, s1))
     amaxes = jnp.max(jnp.maximum(tops, to_core(tops)), axis=1)[:2]

time: 182 us -> 173 us (0.951)
  starting transfers between devices: 50.3 us -> 71.5 us
  waiting for transfers between devices: 81.4 us -> 66.6 us
  between operations: 14.2 us -> 0.81 us
  local copies, waits for them, and re-layouts: 7.45 us -> 3.51 us
  Pallas kernels: 27.4 us -> 29.6 us
    ppermute x9, waiting for transfers between devices: 45 us -> 34.5 us  [to_x(): return lax.ppermute(v, 'row', [(i, (i + 2 * k) % 8) for i in range(8)])]
    ppermute x6 -> x7, starting transfers between devices: 13.9 us -> 23.6 us  [to_core(): return lax.ppermute(v, 'col', [(i, i ^ 1) for i in range(32)])]
    ppermute x9, starting transfers between devices: 8.66 us -> 15.4 us  [to_x(): return lax.ppermute(v, 'row', [(i, (i + 2 * k) % 8) for i in range(8)])]
    ppermute x6 -> x9, waiting for transfers between devices: 12 us -> 7.55 us  [to_l(): return lax.ppermute(v, 'col', [(i, i ^ 2 * k) for i in range(32)])]
    unnamed x18 -> x10, local copies, waits for them, and re-layouts: 7.43 us -> 3.5 us
    ppermute x6 -> x9, starting transfers between devices: 7.87 us -> 11 us  [to_y(): return lax.ppermute(v, 'col', [(i, (i + 8 * k) % 32) for i in range(32)])]
    ppermute x2, waiting for transfers between devices: 4.37 us -> 7.25 us  [to_h(): return lax.ppermute(v, 'row', [(i, i ^ 1) for i in range(8)])]
    pallas_call x9 -> x11, Pallas kernels: 27.4 us -> 29.6 us  [call(): pl.pallas_call(kernel, out_shape=outs, name=name, compiler_params=pltpu.C...]
  transfers between devices with their start and end apart: 30 -> 36, of which waited for: 21 -> 14; matrix products, arithmetic and copies ran while one was open for 0% -> 0% of each run, Pallas kernels for 15% -> 9%
where the time goes in v5:
time: 173 us
  starting transfers between devices  71.5 us (41%)
  waiting for transfers between devices  66.6 us (38%)
  Pallas kernels  29.6 us (17%)
  local copies, waits for them, and re-layouts  3.51 us (2%)
    ppermute x9, waiting for transfers between devices, to_x(): return lax.ppermute(v, 'row', [(i, (i + 2 * k) % 8) for i in range(8)])  34.5 us
    pallas_call x11, Pallas kernels, call(): pl.pallas_call(kernel, out_shape=outs, name=name, compiler_params=pltpu.C...  29.6 us
    ppermute x7, starting transfers between devices, to_core(): return lax.ppermute(v, 'col', [(i, i ^ 1) for i in range(32)])  23.6 us
    ppermute x9, waiting for transfers between devices, to_y(): return lax.ppermute(v, 'col', [(i, (i + 8 * k) % 32) for i in range(32)])  16.4 us
    ppermute x9, starting transfers between devices, to_x(): return lax.ppermute(v, 'row', [(i, (i + 2 * k) % 8) for i in range(8)])  15.4 us
    ppermute x2, starting transfers between devices, to_h(): return lax.ppermute(v, 'row', [(i, i ^ 1) for i in range(8)])  11.7 us
    ppermute x9, starting transfers between devices, to_y(): return lax.ppermute(v, 'col', [(i, (i + 8 * k) % 32) for i in range(32)])  11 us
    ppermute x9, starting transfers between devices, to_l(): return lax.ppermute(v, 'col', [(i, i ^ 2 * k) for i in range(32)])  9.84 us
  transfers between devices with their start and end apart: 36, of which 14 were waited for; matrix products, arithmetic and copies ran while one was open for 0% of the time, Pallas kernels for 9%

profile of v5, /device:TPU:1, one launch (start us, length us, event | category | flops | bytes accessed | tf_op | source)
XLA Modules:
  0.0 172.7 jit_solution(18404602234880654397)
XLA Ops:
  0.6 3.3 %collective-permute-start.3 = (bf16[768,1536]{1,0:T(8,128)(2,1)}, bf16[768,1536]{1,0:T(8,128)(2,1)S(1)}, u32[]{:S(2)}, u32[]{:S(2)}) collective-permute-start(bf16[768,1536]{1,0:T(8,128)(2,1)} %wa.2), channel_id=1, source_target_pairs={{0,1},{1,0},{2,3},{3,2},{4,5},{5,4},{6,7},{7,6},{8,9},{9,8},{10,11... | collective-permute-start | bytes 7077896 | tf_op jit(solution)/shard_map/ppermute | solution.py:40
  4.0 2.6 %collective-permute-start.2 = (bf16[32,1536]{1,0:T(8,128)(2,1)}, bf16[32,1536]{1,0:T(8,128)(2,1)S(1)}, u32[]{:S(2)}, u32[]{:S(2)}) collective-permute-start(bf16[32,1536]{1,0:T(8,128)(2,1)} %a0), channel_id=1, source_target_pairs={{0,6},{1,7},{2,4},{3,5},{4,2},{5,3},{6,0},{7,1},{8,14},{9,15},{10,... | collective-permute-start | bytes 294920 | tf_op jit(solution)/shard_map/ppermute | solution.py:44
  7.6 2.9 %collective-permute-done.2.a3 = bf16[32,1536]{1,0:T(8,128)(2,1)S(1)} collective-permute-done((bf16[32,1536]{1,0:T(8,128)(2,1)}, bf16[32,1536]{1,0:T(8,128)(2,1)S(1)}, u32[]{:S(2)}, u32[]{:S(2)}) %collective-permute-start.2) | collective-permute-done | bytes 98336 | tf_op jit(solution)/shard_map/ppermute | solution.py:44
  10.5 4.6 %collective-permute-done.1.a2 = bf16[32,1536]{1,0:T(8,128)(2,1)S(1)} collective-permute-done((bf16[32,1536]{1,0:T(8,128)(2,1)}, bf16[32,1536]{1,0:T(8,128)(2,1)S(1)}, u32[]{:S(2)}, u32[]{:S(2)}) %collective-permute-start.1) | collective-permute-done | bytes 98336 | tf_op jit(solution)/shard_map/ppermute | solution.py:44
  17.9 2.6 %collective-permute-start.5 = (bf16[128,1536]{1,0:T(8,128)(2,1)S(1)}, bf16[128,1536]{1,0:T(8,128)(2,1)S(1)}, u32[]{:S(2)}, u32[]{:S(2)}) collective-permute-start(bf16[128,1536]{1,0:T(8,128)(2,1)S(1)} %get-tuple-element.84.g0), channel_id=1, source_target_pairs={{0,16},{1,17},{2,18},{3,19},{4,20},{5,21},{6,22},{7,23},{8,24},{9,... | collective-permute-start | bytes 1179656 | tf_op jit(solution)/shard_map/ppermute | solution.py:48
  21.6 5.8 %collective-permute-start.8 = (bf16[128,768]{1,0:T(8,128)(2,1)}, bf16[128,768]{1,0:T(8,128)(2,1)S(1)}, u32[]{:S(2)}, u32[]{:S(2)}) collective-permute-start(bf16[128,768]{1,0:T(8,128)(2,1)} %here.1), channel_id=1, source_target_pairs={{0,32},{32,0},{64,96},{96,64},{128,160},{160,128},{192,224},{224,1... | collective-permute-start | bytes 589832 | tf_op jit(solution)/shard_map/ppermute | solution.py:56
  27.4 7.2 %collective-permute-done.8.there = bf16[128,768]{1,0:T(8,128)(2,1)S(1)} collective-permute-done((bf16[128,768]{1,0:T(8,128)(2,1)}, bf16[128,768]{1,0:T(8,128)(2,1)S(1)}, u32[]{:S(2)}, u32[]{:S(2)}) %collective-permute-start.8) | collective-permute-done | bytes 196640 | tf_op jit(solution)/shard_map/ppermute | solution.py:56
  34.7 3.5 %collective-permute-done.5.g2 = bf16[128,1536]{1,0:T(8,128)(2,1)S(1)} collective-permute-done((bf16[128,1536]{1,0:T(8,128)(2,1)S(1)}, bf16[128,1536]{1,0:T(8,128)(2,1)S(1)}, u32[]{:S(2)}, u32[]{:S(2)}) %collective-permute-start.5) | collective-permute-done | bytes 393248 | tf_op jit(solution)/shard_map/ppermute | solution.py:48
  38.2 1.7 copy-done.2
  40.8 5.6 %back.1 = (f32[128,1536]{1,0:T(8,128)S(1)}, bf16[128,1536]{1,0:T(8,128)(2,1)S(1)}, bf16[128,1536]{1,0:T(8,128)(2,1)S(1)}, bf16[128,1536]{1,0:T(8,128)(2,1)S(1)},...) custom-call(s32[2]{0:T(128)S(1)} %pad_add_fusion.t, ...), custom_call_target="tpu_custom_call" | custom-call | flops 2415919104 | bytes 10813448 | tf_op jit(solution)/shard_map/back/pallas_call | solution.py:359
  46.4 2.5 %collective-permute-start.11 = (bf16[128,1536]{1,0:T(8,128)(2,1)S(1)}, bf16[128,1536]{1,0:T(8,128)(2,1)S(1)}, u32[]{:S(2)}, u32[]{:S(2)}) collective-permute-start(bf16[128,1536]{1,0:T(8,128)(2,1)S(1)} %get-tuple-element.94), channel_id=1, source_target_pairs={{0,192},{32,224},{64,0},{96,32},{128,64},{160,96},{192,128},{224,1... | collective-permute-start | bytes 1179656 | tf_op jit(solution)/shard_map/ppermute | solution.py:52
  49.0 1.7 %collective-permute-start.10 = (bf16[128,1536]{1,0:T(8,128)(2,1)S(1)}, bf16[128,1536]{1,0:T(8,128)(2,1)S(1)}, u32[]{:S(2)}, u32[]{:S(2)}) collective-permute-start(bf16[128,1536]{1,0:T(8,128)(2,1)S(1)} %get-tuple-element.93), channel_id=1, source_target_pairs={{0,128},{32,160},{64,192},{96,224},{128,0},{160,32},{192,64},{224,... | collective-permute-start | bytes 1179656 | tf_op jit(solution)/shard_map/ppermute | solution.py:52
  50.7 1.6 collective-permute-start.12
  52.3 5.1 %collective-permute-done.11.r3 = bf16[128,1536]{1,0:T(8,128)(2,1)S(1)} collective-permute-done((bf16[128,1536]{1,0:T(8,128)(2,1)S(1)}, bf16[128,1536]{1,0:T(8,128)(2,1)S(1)}, u32[]{:S(2)}, u32[]{:S(2)}) %collective-permute-start.11) | collective-permute-done | bytes 393248 | tf_op jit(solution)/shard_map/ppermute | solution.py:52
  57.4 2.4 %collective-permute-start.15 = (bf16[32,1536]{1,0:T(8,128)(2,1)S(1)}, bf16[32,1536]{1,0:T(8,128)(2,1)S(1)}, u32[]{:S(2)}, u32[]{:S(2)}) collective-permute-start(bf16[32,1536]{1,0:T(8,128)(2,1)S(1)} %copy-done.1), channel_id=1, source_target_pairs={{0,6},{1,7},{2,4},{3,5},{4,2},{5,3},{6,0},{7,1},{8,14},{9,15},{10,... | collective-permute-start | bytes 294920 | tf_op jit(solution)/shard_map/ppermute | solution.py:44
  60.9 6.3 %collective-permute-done.10.r2 = bf16[128,1536]{1,0:T(8,128)(2,1)S(1)} collective-permute-done((bf16[128,1536]{1,0:T(8,128)(2,1)S(1)}, bf16[128,1536]{1,0:T(8,128)(2,1)S(1)}, u32[]{:S(2)}, u32[]{:S(2)}) %collective-permute-start.10) | collective-permute-done | bytes 393248 | tf_op jit(solution)/shard_map/ppermute | solution.py:52
  67.4 5.9 %collective-permute-start.16 = (bf16[1552,128]{1,0:T(8,128)(2,1)S(1)}, bf16[1552,128]{1,0:T(8,128)(2,1)S(1)}, u32[]{:S(2)}, u32[]{:S(2)}) collective-permute-start(bf16[1552,128]{1,0:T(8,128)(2,1)S(1)} %back_sum.1.mine), channel_id=1, source_target_pairs={{0,32},{32,0},{64,96},{96,64},{128,160},{160,128},{192,224},{224,1... | collective-permute-start | bytes 1191944 | tf_op jit(solution)/shard_map/ppermute | solution.py:56
  74.2 3.5 %collective-permute-start.19 = (bf16[128,1536]{1,0:T(8,128)(2,1)S(1)}, bf16[128,1536]{1,0:T(8,128)(2,1)S(1)}, u32[]{:S(2)}, u32[]{:S(2)}) collective-permute-start(bf16[128,1536]{1,0:T(8,128)(2,1)S(1)} %get-tuple-element.111.a0), channel_id=1, source_target_pairs={{0,16},{1,17},{2,18},{3,19},{4,20},{5,21},{6,22},{7,23},{8,24},{9,... | collective-permute-start | bytes 1179656 | tf_op jit(solution)/shard_map/ppermute | solution.py:48
  77.7 2.8 %collective-permute-start.17 = (bf16[2,128,768]{2,1,0:T(8,128)(2,1)S(1)}, bf16[2,128,768]{2,1,0:T(8,128)(2,1)S(1)}, u32[]{:S(2)}, u32[]{:S(2)}) collective-permute-start(bf16[2,128,768]{2,1,0:T(8,128)(2,1)S(1)} %bitcast.8), channel_id=1, source_target_pairs={{0,128},{32,160},{64,192},{96,224},{128,0},{160,32},{192,64},{224,... | collective-permute-start | bytes 1179656 | tf_op jit(solution)/shard_map/ppermute | solution.py:52
  81.8 5.3 %collective-permute-done.19.a2 = bf16[128,1536]{1,0:T(8,128)(2,1)S(1)} collective-permute-done((bf16[128,1536]{1,0:T(8,128)(2,1)S(1)}, bf16[128,1536]{1,0:T(8,128)(2,1)S(1)}, u32[]{:S(2)}, u32[]{:S(2)}) %collective-permute-start.19) | collective-permute-done | bytes 393248 | tf_op jit(solution)/shard_map/ppermute | solution.py:48
  88.5 16.8 %collective-permute-start.24 = (bf16[512,1536]{1,0:T(8,128)(2,1)S(1)}, bf16[512,1536]{1,0:T(8,128)(2,1)S(1)}, u32[]{:S(2)}, u32[]{:S(2)}) collective-permute-start(bf16[512,1536]{1,0:T(8,128)(2,1)S(1)} %bitcast.13), channel_id=1, source_target_pairs={{0,1},{1,0},{2,3},{3,2},{4,5},{5,4},{6,7},{7,6},{8,9},{9,8},{10,11... | collective-permute-start | bytes 4718600 | tf_op jit(solution)/shard_map/ppermute | solution.py:40
  105.4 5.5 %collective-permute-start.22 = (bf16[1552,128]{1,0:T(8,128)(2,1)S(1)}, bf16[1552,128]{1,0:T(8,128)(2,1)S(1)}, u32[]{:S(2)}, u32[]{:S(2)}) collective-permute-start(bf16[1552,128]{1,0:T(8,128)(2,1)S(1)} %slope.1.m0), channel_id=1, source_target_pairs={{0,128},{32,160},{64,192},{96,224},{128,0},{160,32},{192,64},{224,... | collective-permute-start | bytes 1191944 | tf_op jit(solution)/shard_map/ppermute | solution.py:52
  111.0 8.0 %collective-permute-done.23.m3 = bf16[1552,128]{1,0:T(8,128)(2,1)S(1)} collective-permute-done((bf16[1552,128]{1,0:T(8,128)(2,1)S(1)}, bf16[1552,128]{1,0:T(8,128)(2,1)S(1)}, u32[]{:S(2)}, u32[]{:S(2)}) %collective-permute-start.23) | collective-permute-done | bytes 397344 | tf_op jit(solution)/shard_map/ppermute | solution.py:52
  119.0 9.4 %collective-permute-done.22.m2 = bf16[1552,128]{1,0:T(8,128)(2,1)S(1)} collective-permute-done((bf16[1552,128]{1,0:T(8,128)(2,1)S(1)}, bf16[1552,128]{1,0:T(8,128)(2,1)S(1)}, u32[]{:S(2)}, u32[]{:S(2)}) %collective-permute-start.22) | collective-permute-done | bytes 397344 | tf_op jit(solution)/shard_map/ppermute | solution.py:52
  128.4 6.1 %input_grad.1 = (f32[128,1536]{1,0:T(8,128)S(1)}, bf16[1552,128]{1,0:T(8,128)(2,1)S(1)}, bf16[1552,128]{1,0:T(8,128)(2,1)S(1)}, bf16[1552,128]{1,0:T(8,128)(2,1)...) custom-call(s32[2]{0:T(128)S(1)} %pad_add_fusion.t, bf16[1552,128]{1,0:T(8,128)(2,1)S(1)} %slope.1.m0, ...), custom_call_target="tpu_custom_call" | custom-call | flops 2415919104 | bytes 9859080 | tf_op jit(solution)/shard_map/input_grad/pallas_call | solution.py:359
  134.8 2.5 %collective-permute-start.29 = (bf16[2,128,768]{2,1,0:T(8,128)(2,1)S(1)}, bf16[2,128,768]{2,1,0:T(8,128)(2,1)S(1)}, u32[]{:S(2)}, u32[]{:S(2)}) collective-permute-start(bf16[2,128,768]{2,1,0:T(8,128)(2,1)S(1)} %bitcast.11), channel_id=1, source_target_pairs={{0,192},{32,224},{64,0},{96,32},{128,64},{160,96},{192,128},{224,1... | collective-permute-start | bytes 1179656 | tf_op jit(solution)/shard_map/ppermute | solution.py:52
  137.3 1.6 collective-permute-start.28
  139.4 5.7 %collective-permute-done.30.r3 = bf16[2,128,768]{2,1,0:T(8,128)(2,1)S(1)} collective-permute-done((bf16[2,128,768]{2,1,0:T(8,128)(2,1)S(1)}, bf16[2,128,768]{2,1,0:T(8,128)(2,1)S(1)}, u32[]{:S(2)}, u32[]{:S(2)}) %collective-permute-start.30) | collective-permute-done | bytes 393248 | tf_op jit(solution)/shard_map/ppermute | solution.py:52
  145.2 7.0 %w_out_grad.1 = bf16[768,1536]{1,0:T(8,128)(2,1)} custom-call(bf16[2,128,768]{2,1,0:T(8,128)(2,1)S(1)} %bitcast.12, bf16[2,128,768]{2,1,0:T(8,128)(2,1)S(1)} %collective-permute-done.29.r1, bf16[2,128,768]{2,1,0:T(8,128)(2,1)S(1)} %collective-permute-done.17.r2, bf16[2,128,768]{2,1,0:T(8,128)(2,1)S(1)} %collective-permute-done.30.r3, ...), custom_call_target="tpu_custom_call" | custom-call | flops 2415919104 | bytes 7077888 | tf_op jit(solution)/shard_map/w_out_grad/pallas_call | solution.py:359
  152.2 3.8 %collective-permute-done.28.r3 = bf16[1552,128]{1,0:T(8,128)(2,1)S(1)} collective-permute-done((bf16[1552,128]{1,0:T(8,128)(2,1)S(1)}, bf16[1552,128]{1,0:T(8,128)(2,1)S(1)}, u32[]{:S(2)}, u32[]{:S(2)}) %collective-permute-start.28) | collective-permute-done | bytes 397344 | tf_op jit(solution)/shard_map/ppermute | solution.py:48
  156.0 2.5 %collective-permute-done.26.r1 = bf16[1552,128]{1,0:T(8,128)(2,1)S(1)} collective-permute-done((bf16[1552,128]{1,0:T(8,128)(2,1)S(1)}, bf16[1552,128]{1,0:T(8,128)(2,1)S(1)}, u32[]{:S(2)}, u32[]{:S(2)}) %collective-permute-start.26) | collective-permute-done | bytes 397344 | tf_op jit(solution)/shard_map/ppermute | solution.py:48
  161.9 7.8 %w_in_grad.1 = bf16[1536,768]{1,0:T(8,128)(2,1)} custom-call(s32[2]{0:T(128)S(1)} %pad_add_fusion.t, bf16[4,128,1536]{2,1,0:T(8,128)(2,1)S(1)} %join_inputs.1.inputs, bf16[4,128,1536]{2,1,0:T(8,128)(2,1)S(1)} %collective-permute-done.25.inputs_o, bf16[512,768]{1,0:T(8,128)(2,1)S(1)} %get-tuple-element.139.mine, ...), custom_call_target="tpu_custom_call" | custom-call | flops 2415919104 | bytes 7077896 | tf_op jit(solution)/shard_map/w_in_grad/pallas_call | solution.py:359
  (64 shorter events, 18.1 us)
Async XLA Ops:
  0.6 14.5 %collective-permute-start.3 = (bf16[768,1536]{1,0:T(8,128)(2,1)}, bf16[768,1536]{1,0:T(8,128)(2,1)S(1)}, u32[]{:S(2)}, u32[]{:S(2)}) collective-permute-start(bf16[768,1536]{1,0:T(8,128)(2,1)} %wa.2), channel_id=1, source_target_pairs={{0,1},{1,0},{2,3},{3,2},{4,5},{5,4},{6,7},{7,6},{8,9},{9,8},{10,11... | collective-permute-start | bytes 7077896 | tf_op jit(solution)/shard_map/ppermute | solution.py:40
  6.7 8.5 %collective-permute-start.1 = (bf16[32,1536]{1,0:T(8,128)(2,1)}, bf16[32,1536]{1,0:T(8,128)(2,1)S(1)}, u32[]{:S(2)}, u32[]{:S(2)}) collective-permute-start(bf16[32,1536]{1,0:T(8,128)(2,1)} %a0), channel_id=1, source_target_pairs={{0,4},{1,5},{2,6},{3,7},{4,0},{5,1},{6,2},{7,3},{8,12},{9,13},{10,... | collective-permute-start | bytes 294920 | tf_op jit(solution)/shard_map/ppermute | solution.py:44
  6.7 8.5 %collective-permute-start = (bf16[32,1536]{1,0:T(8,128)(2,1)}, bf16[32,1536]{1,0:T(8,128)(2,1)S(1)}, u32[]{:S(2)}, u32[]{:S(2)}) collective-permute-start(bf16[32,1536]{1,0:T(8,128)(2,1)} %a0), channel_id=1, source_target_pairs={{0,2},{1,3},{2,0},{3,1},{4,6},{5,7},{6,4},{7,5},{8,10},{9,11},{10,... | collective-permute-start | bytes 294920 | tf_op jit(solution)/shard_map/ppermute | solution.py:44
  15.1 23.1 %collective-permute-start.7 = (bf16[1536,768]{1,0:T(8,128)(2,1)}, bf16[1536,768]{1,0:T(8,128)(2,1)S(1)}, u32[]{:S(2)}, u32[]{:S(2)}) collective-permute-start(bf16[1536,768]{1,0:T(8,128)(2,1)} %wa.3), channel_id=1, source_target_pairs={{0,1},{1,0},{2,3},{3,2},{4,5},{5,4},{6,7},{7,6},{8,9},{9,8},{10,11... | collective-permute-start | bytes 7077896 | tf_op jit(solution)/shard_map/ppermute | solution.py:40
  16.5 18.2 %collective-permute-start.6 = (bf16[128,1536]{1,0:T(8,128)(2,1)S(1)}, bf16[128,1536]{1,0:T(8,128)(2,1)S(1)}, u32[]{:S(2)}, u32[]{:S(2)}) collective-permute-start(bf16[128,1536]{1,0:T(8,128)(2,1)S(1)} %get-tuple-element.84.g0), channel_id=1, source_target_pairs={{0,8},{1,9},{2,10},{3,11},{4,12},{5,13},{6,14},{7,15},{8,16},{9,17... | collective-permute-start | bytes 1179656 | tf_op jit(solution)/shard_map/ppermute | solution.py:48
  17.9 20.3 %collective-permute-start.5 = (bf16[128,1536]{1,0:T(8,128)(2,1)S(1)}, bf16[128,1536]{1,0:T(8,128)(2,1)S(1)}, u32[]{:S(2)}, u32[]{:S(2)}) collective-permute-start(bf16[128,1536]{1,0:T(8,128)(2,1)S(1)} %get-tuple-element.84.g0), channel_id=1, source_target_pairs={{0,16},{1,17},{2,18},{3,19},{4,20},{5,21},{6,22},{7,23},{8,24},{9,... | collective-permute-start | bytes 1179656 | tf_op jit(solution)/shard_map/ppermute | solution.py:48
  20.5 17.7 %collective-permute-start.4 = (bf16[128,1536]{1,0:T(8,128)(2,1)S(1)}, bf16[128,1536]{1,0:T(8,128)(2,1)S(1)}, u32[]{:S(2)}, u32[]{:S(2)}) collective-permute-start(bf16[128,1536]{1,0:T(8,128)(2,1)S(1)} %get-tuple-element.84.g0), channel_id=1, source_target_pairs={{0,24},{1,25},{2,26},{3,27},{4,28},{5,29},{6,30},{7,31},{8,0},{9,1... | collective-permute-start | bytes 1179656 | tf_op jit(solution)/shard_map/ppermute | solution.py:48
  21.6 13.1 %collective-permute-start.8 = (bf16[128,768]{1,0:T(8,128)(2,1)}, bf16[128,768]{1,0:T(8,128)(2,1)S(1)}, u32[]{:S(2)}, u32[]{:S(2)}) collective-permute-start(bf16[128,768]{1,0:T(8,128)(2,1)} %here.1), channel_id=1, source_target_pairs={{0,32},{32,0},{64,96},{96,64},{128,160},{160,128},{192,224},{224,1... | collective-permute-start | bytes 589832 | tf_op jit(solution)/shard_map/ppermute | solution.py:56
  46.4 11.0 %collective-permute-start.11 = (bf16[128,1536]{1,0:T(8,128)(2,1)S(1)}, bf16[128,1536]{1,0:T(8,128)(2,1)S(1)}, u32[]{:S(2)}, u32[]{:S(2)}) collective-permute-start(bf16[128,1536]{1,0:T(8,128)(2,1)S(1)} %get-tuple-element.94), channel_id=1, source_target_pairs={{0,192},{32,224},{64,0},{96,32},{128,64},{160,96},{192,128},{224,1... | collective-permute-start | bytes 1179656 | tf_op jit(solution)/shard_map/ppermute | solution.py:52
  49.0 12.0 %collective-permute-start.9 = (bf16[128,1536]{1,0:T(8,128)(2,1)S(1)}, bf16[128,1536]{1,0:T(8,128)(2,1)S(1)}, u32[]{:S(2)}, u32[]{:S(2)}) collective-permute-start(bf16[128,1536]{1,0:T(8,128)(2,1)S(1)} %get-tuple-element.92), channel_id=1, source_target_pairs={{0,64},{32,96},{64,128},{96,160},{128,192},{160,224},{192,0},{224,... | collective-permute-start | bytes 1179656 | tf_op jit(solution)/shard_map/ppermute | solution.py:52
  49.0 18.3 %collective-permute-start.10 = (bf16[128,1536]{1,0:T(8,128)(2,1)S(1)}, bf16[128,1536]{1,0:T(8,128)(2,1)S(1)}, u32[]{:S(2)}, u32[]{:S(2)}) collective-permute-start(bf16[128,1536]{1,0:T(8,128)(2,1)S(1)} %get-tuple-element.93), channel_id=1, source_target_pairs={{0,128},{32,160},{64,192},{96,224},{128,0},{160,32},{192,64},{224,... | collective-permute-start | bytes 1179656 | tf_op jit(solution)/shard_map/ppermute | solution.py:52
  50.7 9.0 %collective-permute-start.12 = (bf16[128,768]{1,0:T(8,128)(2,1)S(1)}, bf16[128,768]{1,0:T(8,128)(2,1)S(1)}, u32[]{:S(2)}, u32[]{:S(2)}) collective-permute-start(bf16[128,768]{1,0:T(8,128)(2,1)S(1)} %bitcast.15), channel_id=1, source_target_pairs={{0,1},{1,0},{2,3},{3,2},{4,5},{5,4},{6,7},{7,6},{8,9},{9,8},{10,11... | collective-permute-start | bytes 589832 | tf_op jit(solution)/shard_map/ppermute | solution.py:40
  57.4 9.9 %collective-permute-start.15 = (bf16[32,1536]{1,0:T(8,128)(2,1)S(1)}, bf16[32,1536]{1,0:T(8,128)(2,1)S(1)}, u32[]{:S(2)}, u32[]{:S(2)}) collective-permute-start(bf16[32,1536]{1,0:T(8,128)(2,1)S(1)} %copy-done.1), channel_id=1, source_target_pairs={{0,6},{1,7},{2,4},{3,5},{4,2},{5,3},{6,0},{7,1},{8,14},{9,15},{10,... | collective-permute-start | bytes 294920 | tf_op jit(solution)/shard_map/ppermute | solution.py:44
  59.7 7.5 %collective-permute-start.14 = (bf16[32,1536]{1,0:T(8,128)(2,1)S(1)}, bf16[32,1536]{1,0:T(8,128)(2,1)S(1)}, u32[]{:S(2)}, u32[]{:S(2)}) collective-permute-start(bf16[32,1536]{1,0:T(8,128)(2,1)S(1)} %copy-done.1), channel_id=1, source_target_pairs={{0,4},{1,5},{2,6},{3,7},{4,0},{5,1},{6,2},{7,3},{8,12},{9,13},{10,... | collective-permute-start | bytes 294920 | tf_op jit(solution)/shard_map/ppermute | solution.py:44
  67.4 20.5 %collective-permute-start.16 = (bf16[1552,128]{1,0:T(8,128)(2,1)S(1)}, bf16[1552,128]{1,0:T(8,128)(2,1)S(1)}, u32[]{:S(2)}, u32[]{:S(2)}) collective-permute-start(bf16[1552,128]{1,0:T(8,128)(2,1)S(1)} %back_sum.1.mine), channel_id=1, source_target_pairs={{0,32},{32,0},{64,96},{96,64},{128,160},{160,128},{192,224},{224,1... | collective-permute-start | bytes 1191944 | tf_op jit(solution)/shard_map/ppermute | solution.py:56
  74.0 7.8 %collective-permute-start.20 = (bf16[128,1536]{1,0:T(8,128)(2,1)S(1)}, bf16[128,1536]{1,0:T(8,128)(2,1)S(1)}, u32[]{:S(2)}, u32[]{:S(2)}) collective-permute-start(bf16[128,1536]{1,0:T(8,128)(2,1)S(1)} %get-tuple-element.111.a0), channel_id=1, source_target_pairs={{0,8},{1,9},{2,10},{3,11},{4,12},{5,13},{6,14},{7,15},{8,16},{9,17... | collective-permute-start | bytes 1179656 | tf_op jit(solution)/shard_map/ppermute | solution.py:48
  74.2 12.9 %collective-permute-start.19 = (bf16[128,1536]{1,0:T(8,128)(2,1)S(1)}, bf16[128,1536]{1,0:T(8,128)(2,1)S(1)}, u32[]{:S(2)}, u32[]{:S(2)}) collective-permute-start(bf16[128,1536]{1,0:T(8,128)(2,1)S(1)} %get-tuple-element.111.a0), channel_id=1, source_target_pairs={{0,16},{1,17},{2,18},{3,19},{4,20},{5,21},{6,22},{7,23},{8,24},{9,... | collective-permute-start | bytes 1179656 | tf_op jit(solution)/shard_map/ppermute | solution.py:48
  77.7 9.4 %collective-permute-start.18 = (bf16[128,1536]{1,0:T(8,128)(2,1)S(1)}, bf16[128,1536]{1,0:T(8,128)(2,1)S(1)}, u32[]{:S(2)}, u32[]{:S(2)}) collective-permute-start(bf16[128,1536]{1,0:T(8,128)(2,1)S(1)} %get-tuple-element.111.a0), channel_id=1, source_target_pairs={{0,24},{1,25},{2,26},{3,27},{4,28},{5,29},{6,30},{7,31},{8,0},{9,1... | collective-permute-start | bytes 1179656 | tf_op jit(solution)/shard_map/ppermute | solution.py:48
  77.7 10.2 %collective-permute-start.17 = (bf16[2,128,768]{2,1,0:T(8,128)(2,1)S(1)}, bf16[2,128,768]{2,1,0:T(8,128)(2,1)S(1)}, u32[]{:S(2)}, u32[]{:S(2)}) collective-permute-start(bf16[2,128,768]{2,1,0:T(8,128)(2,1)S(1)} %bitcast.8), channel_id=1, source_target_pairs={{0,128},{32,160},{64,192},{96,224},{128,0},{160,32},{192,64},{224,... | collective-permute-start | bytes 1179656 | tf_op jit(solution)/shard_map/ppermute | solution.py:52
  88.5 39.9 %collective-permute-start.24 = (bf16[512,1536]{1,0:T(8,128)(2,1)S(1)}, bf16[512,1536]{1,0:T(8,128)(2,1)S(1)}, u32[]{:S(2)}, u32[]{:S(2)}) collective-permute-start(bf16[512,1536]{1,0:T(8,128)(2,1)S(1)} %bitcast.13), channel_id=1, source_target_pairs={{0,1},{1,0},{2,3},{3,2},{4,5},{5,4},{6,7},{7,6},{8,9},{9,8},{10,11... | collective-permute-start | bytes 4718600 | tf_op jit(solution)/shard_map/ppermute | solution.py:40
  105.3 23.1 %collective-permute-start.25 = (bf16[4,128,1536]{2,1,0:T(8,128)(2,1)S(1)}, bf16[4,128,1536]{2,1,0:T(8,128)(2,1)S(1)}, u32[]{:S(2)}, u32[]{:S(2)}) collective-permute-start(bf16[4,128,1536]{2,1,0:T(8,128)(2,1)S(1)} %join_inputs.1.inputs), channel_id=1, source_target_pairs={{0,1},{1,0},{2,3},{3,2},{4,5},{5,4},{6,7},{7,6},{8,9},{9,8},{10,11... | collective-permute-start | bytes 4718600 | tf_op jit(solution)/shard_map/ppermute | solution.py:40
  105.4 13.6 %collective-permute-start.23 = (bf16[1552,128]{1,0:T(8,128)(2,1)S(1)}, bf16[1552,128]{1,0:T(8,128)(2,1)S(1)}, u32[]{:S(2)}, u32[]{:S(2)}) collective-permute-start(bf16[1552,128]{1,0:T(8,128)(2,1)S(1)} %slope.1.m0), channel_id=1, source_target_pairs={{0,64},{32,96},{64,128},{96,160},{128,192},{160,224},{192,0},{224,... | collective-permute-start | bytes 1191944 | tf_op jit(solution)/shard_map/ppermute | solution.py:52
  105.4 23.0 %collective-permute-start.22 = (bf16[1552,128]{1,0:T(8,128)(2,1)S(1)}, bf16[1552,128]{1,0:T(8,128)(2,1)S(1)}, u32[]{:S(2)}, u32[]{:S(2)}) collective-permute-start(bf16[1552,128]{1,0:T(8,128)(2,1)S(1)} %slope.1.m0), channel_id=1, source_target_pairs={{0,128},{32,160},{64,192},{96,224},{128,0},{160,32},{192,64},{224,... | collective-permute-start | bytes 1191944 | tf_op jit(solution)/shard_map/ppermute | solution.py:52
  111.0 17.4 %collective-permute-start.21 = (bf16[1552,128]{1,0:T(8,128)(2,1)S(1)}, bf16[1552,128]{1,0:T(8,128)(2,1)S(1)}, u32[]{:S(2)}, u32[]{:S(2)}) collective-permute-start(bf16[1552,128]{1,0:T(8,128)(2,1)S(1)} %slope.1.m0), channel_id=1, source_target_pairs={{0,192},{32,224},{64,0},{96,32},{128,64},{160,96},{192,128},{224,1... | collective-permute-start | bytes 1191944 | tf_op jit(solution)/shard_map/ppermute | solution.py:52
  134.5 10.6 %collective-permute-start.30 = (bf16[2,128,768]{2,1,0:T(8,128)(2,1)S(1)}, bf16[2,128,768]{2,1,0:T(8,128)(2,1)S(1)}, u32[]{:S(2)}, u32[]{:S(2)}) collective-permute-start(bf16[2,128,768]{2,1,0:T(8,128)(2,1)S(1)} %bitcast.10), channel_id=1, source_target_pairs={{0,64},{32,96},{64,128},{96,160},{128,192},{160,224},{192,0},{224,... | collective-permute-start | bytes 1179656 | tf_op jit(solution)/shard_map/ppermute | solution.py:52
  134.8 10.4 %collective-permute-start.29 = (bf16[2,128,768]{2,1,0:T(8,128)(2,1)S(1)}, bf16[2,128,768]{2,1,0:T(8,128)(2,1)S(1)}, u32[]{:S(2)}, u32[]{:S(2)}) collective-permute-start(bf16[2,128,768]{2,1,0:T(8,128)(2,1)S(1)} %bitcast.11), channel_id=1, source_target_pairs={{0,192},{32,224},{64,0},{96,32},{128,64},{160,96},{192,128},{224,1... | collective-permute-start | bytes 1179656 | tf_op jit(solution)/shard_map/ppermute | solution.py:52
  137.3 14.9 %collective-permute-start.27 = (bf16[1552,128]{1,0:T(8,128)(2,1)S(1)}, bf16[1552,128]{1,0:T(8,128)(2,1)S(1)}, u32[]{:S(2)}, u32[]{:S(2)}) collective-permute-start(bf16[1552,128]{1,0:T(8,128)(2,1)S(1)} %get-tuple-element.124), channel_id=1, source_target_pairs={{0,16},{1,17},{2,18},{3,19},{4,20},{5,21},{6,22},{7,23},{8,24},{9,... | collective-permute-start | bytes 1191944 | tf_op jit(solution)/shard_map/ppermute | solution.py:48
  137.3 18.7 %collective-permute-start.28 = (bf16[1552,128]{1,0:T(8,128)(2,1)S(1)}, bf16[1552,128]{1,0:T(8,128)(2,1)S(1)}, u32[]{:S(2)}, u32[]{:S(2)}) collective-permute-start(bf16[1552,128]{1,0:T(8,128)(2,1)S(1)} %get-tuple-element.125), channel_id=1, source_target_pairs={{0,24},{1,25},{2,26},{3,27},{4,28},{5,29},{6,30},{7,31},{8,0},{9,1... | collective-permute-start | bytes 1191944 | tf_op jit(solution)/shard_map/ppermute | solution.py:48
  138.9 19.6 %collective-permute-start.26 = (bf16[1552,128]{1,0:T(8,128)(2,1)S(1)}, bf16[1552,128]{1,0:T(8,128)(2,1)S(1)}, u32[]{:S(2)}, u32[]{:S(2)}) collective-permute-start(bf16[1552,128]{1,0:T(8,128)(2,1)S(1)} %get-tuple-element.123.mine), channel_id=1, source_target_pairs={{0,8},{1,9},{2,10},{3,11},{4,12},{5,13},{6,14},{7,15},{8,16},{9,17... | collective-permute-start | bytes 1191944 | tf_op jit(solution)/shard_map/ppermute | solution.py:48
  159.1 10.5 %collective-permute-start.32 = (bf16[400,128]{1,0:T(8,128)(2,1)S(1)}, bf16[400,128]{1,0:T(8,128)(2,1)S(1)}, u32[]{:S(2)}, u32[]{:S(2)}) collective-permute-start(bf16[400,128]{1,0:T(8,128)(2,1)S(1)} %get-tuple-element.136), channel_id=1, source_target_pairs={{0,4},{1,5},{2,6},{3,7},{4,0},{5,1},{6,2},{7,3},{8,12},{9,13},{10,... | collective-permute-start | bytes 307208 | tf_op jit(solution)/shard_map/ppermute | solution.py:44
  159.2 10.4 %collective-permute-start.33 = (bf16[400,128]{1,0:T(8,128)(2,1)S(1)}, bf16[400,128]{1,0:T(8,128)(2,1)S(1)}, u32[]{:S(2)}, u32[]{:S(2)}) collective-permute-start(bf16[400,128]{1,0:T(8,128)(2,1)S(1)} %get-tuple-element.137), channel_id=1, source_target_pairs={{0,6},{1,7},{2,4},{3,5},{4,2},{5,3},{6,0},{7,1},{8,14},{9,15},{10,... | collective-permute-start | bytes 307208 | tf_op jit(solution)/shard_map/ppermute | solution.py:44
  160.8 8.9 %collective-permute-start.31 = (bf16[400,128]{1,0:T(8,128)(2,1)S(1)}, bf16[400,128]{1,0:T(8,128)(2,1)S(1)}, u32[]{:S(2)}, u32[]{:S(2)}) collective-permute-start(bf16[400,128]{1,0:T(8,128)(2,1)S(1)} %get-tuple-element.135.mine), channel_id=1, source_target_pairs={{0,2},{1,3},{2,0},{3,1},{4,6},{5,7},{6,4},{7,5},{8,10},{9,11},{10,... | collective-permute-start | bytes 307208 | tf_op jit(solution)/shard_map/ppermute | solution.py:44
  (9 other events, 111.4 us)

commit v6 on v5

--- a/solution.py
+++ b/solution.py
@@ -12,7 +12,7 @@
 barrier = lax.optimization_barrier
 D, FF, T = 1536, 768, 128
 W = 2 * FF
-B, C = 256, 768
+B, C = 512, 768
 
 
 def gelu_value(pre):
@@ -353,7 +353,7 @@
     return jax.ShapeDtypeStruct(shape, dtype)
 
 
-def call(kernel, name, outs, args, flops=0, mib=8, **spec):
+def call(kernel, name, outs, args, flops=0, mib=8, light=False, **spec):
     outs = list(outs)
     size = sum(math.prod(a.shape) * a.dtype.itemsize for a in list(args) + outs)
     return pl.pallas_call(
@@ -361,7 +361,7 @@
         out_shape=outs,
         name=name,
         compiler_params=pltpu.CompilerParams(vmem_limit_bytes=mib * 2**20),
-        cost_estimate=pl.CostEstimate(flops=flops, bytes_accessed=size, transcendentals=0),
+        cost_estimate=pl.CostEstimate(flops=flops, bytes_accessed=1 if light else size, transcendentals=0),
         **spec,
     )(*args)
 
@@ -477,8 +477,9 @@
         "w_out_grad",
         [like(FF, D)],
         args,
-        big,
+        1,
         20,
+        True,
         grid=(steps,),
         in_specs=here(args),
         out_specs=[pl.BlockSpec((FF, B), lambda i: (0, i))],

time: 173 us -> 170 us (0.983)
    ppermute x9, waiting for transfers between devices: 16.4 us -> 13 us  [to_y(): return lax.ppermute(v, 'col', [(i, (i + 8 * k) % 32) for i in range(32)])]
  transfers between devices with their start and end apart: 36 -> 36, of which waited for: 14 -> 15; matrix products, arithmetic and copies ran while one was open for 0% -> 0% of each run, Pallas kernels for 9% -> 9%
where the time goes in v6:
time: 170 us
  starting transfers between devices  71.6 us (42%)
  waiting for transfers between devices  65.4 us (38%)
  Pallas kernels  27.9 us (16%)
  local copies, waits for them, and re-layouts  3.51 us (2%)
    ppermute x9, waiting for transfers between devices, to_x(): return lax.ppermute(v, 'row', [(i, (i + 2 * k) % 8) for i in range(8)])  36.1 us
    pallas_call x11, Pallas kernels, call(): pl.pallas_call(kernel, out_shape=outs, name=name, compiler_params=pltpu.C...  27.9 us
    ppermute x7, starting transfers between devices, to_core(): return lax.ppermute(v, 'col', [(i, i ^ 1) for i in range(32)])  23.7 us
    ppermute x9, starting transfers between devices, to_x(): return lax.ppermute(v, 'row', [(i, (i + 2 * k) % 8) for i in range(8)])  15.3 us
    ppermute x9, waiting for transfers between devices, to_y(): return lax.ppermute(v, 'col', [(i, (i + 8 * k) % 32) for i in range(32)])  13 us
    ppermute x2, starting transfers between devices, to_h(): return lax.ppermute(v, 'row', [(i, i ^ 1) for i in range(8)])  11.7 us
    ppermute x9, starting transfers between devices, to_y(): return lax.ppermute(v, 'col', [(i, (i + 8 * k) % 32) for i in range(32)])  11.1 us
    ppermute x9, starting transfers between devices, to_l(): return lax.ppermute(v, 'col', [(i, i ^ 2 * k) for i in range(32)])  9.84 us
  transfers between devices with their start and end apart: 36, of which 15 were waited for; matrix products, arithmetic and copies ran while one was open for 0% of the time, Pallas kernels for 9%

profile of v6, /device:TPU:1, one launch (start us, length us, event | category | flops | bytes accessed | tf_op | source)
XLA Modules:
  0.0 169.9 jit_solution(2924428903381317182)
XLA Ops:
  0.6 3.3 %collective-permute-start.3 = (bf16[768,1536]{1,0:T(8,128)(2,1)}, bf16[768,1536]{1,0:T(8,128)(2,1)S(1)}, u32[]{:S(2)}, u32[]{:S(2)}) collective-permute-start(bf16[768,1536]{1,0:T(8,128)(2,1)} %wa.2), channel_id=1, source_target_pairs={{0,1},{1,0},{2,3},{3,2},{4,5},{5,4},{6,7},{7,6},{8,9},{9,8},{10,11... | collective-permute-start | bytes 7077896 | tf_op jit(solution)/shard_map/ppermute | solution.py:40
  4.0 2.6 %collective-permute-start.2 = (bf16[32,1536]{1,0:T(8,128)(2,1)}, bf16[32,1536]{1,0:T(8,128)(2,1)S(1)}, u32[]{:S(2)}, u32[]{:S(2)}) collective-permute-start(bf16[32,1536]{1,0:T(8,128)(2,1)} %a0), channel_id=1, source_target_pairs={{0,6},{1,7},{2,4},{3,5},{4,2},{5,3},{6,0},{7,1},{8,14},{9,15},{10,... | collective-permute-start | bytes 294920 | tf_op jit(solution)/shard_map/ppermute | solution.py:44
  7.6 2.9 %collective-permute-done.2.a3 = bf16[32,1536]{1,0:T(8,128)(2,1)S(1)} collective-permute-done((bf16[32,1536]{1,0:T(8,128)(2,1)}, bf16[32,1536]{1,0:T(8,128)(2,1)S(1)}, u32[]{:S(2)}, u32[]{:S(2)}) %collective-permute-start.2) | collective-permute-done | bytes 98336 | tf_op jit(solution)/shard_map/ppermute | solution.py:44
  10.5 4.6 %collective-permute-done.1.a2 = bf16[32,1536]{1,0:T(8,128)(2,1)S(1)} collective-permute-done((bf16[32,1536]{1,0:T(8,128)(2,1)}, bf16[32,1536]{1,0:T(8,128)(2,1)S(1)}, u32[]{:S(2)}, u32[]{:S(2)}) %collective-permute-start.1) | collective-permute-done | bytes 98336 | tf_op jit(solution)/shard_map/ppermute | solution.py:44
  17.9 2.6 %collective-permute-start.5 = (bf16[128,1536]{1,0:T(8,128)(2,1)S(1)}, bf16[128,1536]{1,0:T(8,128)(2,1)S(1)}, u32[]{:S(2)}, u32[]{:S(2)}) collective-permute-start(bf16[128,1536]{1,0:T(8,128)(2,1)S(1)} %get-tuple-element.84.g0), channel_id=1, source_target_pairs={{0,16},{1,17},{2,18},{3,19},{4,20},{5,21},{6,22},{7,23},{8,24},{9,... | collective-permute-start | bytes 1179656 | tf_op jit(solution)/shard_map/ppermute | solution.py:48
  21.6 5.8 %collective-permute-start.8 = (bf16[128,768]{1,0:T(8,128)(2,1)}, bf16[128,768]{1,0:T(8,128)(2,1)S(1)}, u32[]{:S(2)}, u32[]{:S(2)}) collective-permute-start(bf16[128,768]{1,0:T(8,128)(2,1)} %here.1), channel_id=1, source_target_pairs={{0,32},{32,0},{64,96},{96,64},{128,160},{160,128},{192,224},{224,1... | collective-permute-start | bytes 589832 | tf_op jit(solution)/shard_map/ppermute | solution.py:56
  27.4 7.2 %collective-permute-done.8.there = bf16[128,768]{1,0:T(8,128)(2,1)S(1)} collective-permute-done((bf16[128,768]{1,0:T(8,128)(2,1)}, bf16[128,768]{1,0:T(8,128)(2,1)S(1)}, u32[]{:S(2)}, u32[]{:S(2)}) %collective-permute-start.8) | collective-permute-done | bytes 196640 | tf_op jit(solution)/shard_map/ppermute | solution.py:56
  34.7 3.5 %collective-permute-done.5.g2 = bf16[128,1536]{1,0:T(8,128)(2,1)S(1)} collective-permute-done((bf16[128,1536]{1,0:T(8,128)(2,1)S(1)}, bf16[128,1536]{1,0:T(8,128)(2,1)S(1)}, u32[]{:S(2)}, u32[]{:S(2)}) %collective-permute-start.5) | collective-permute-done | bytes 393248 | tf_op jit(solution)/shard_map/ppermute | solution.py:48
  38.2 1.7 copy-done.2
  40.8 5.6 %back.1 = (f32[128,1536]{1,0:T(8,128)S(1)}, bf16[128,1536]{1,0:T(8,128)(2,1)S(1)}, bf16[128,1536]{1,0:T(8,128)(2,1)S(1)}, bf16[128,1536]{1,0:T(8,128)(2,1)S(1)},...) custom-call(s32[2]{0:T(128)S(1)} %pad_add_fusion.t, ...), custom_call_target="tpu_custom_call" | custom-call | flops 2415919104 | bytes 10813448 | tf_op jit(solution)/shard_map/back/pallas_call | solution.py:359
  46.4 2.5 %collective-permute-start.11 = (bf16[128,1536]{1,0:T(8,128)(2,1)S(1)}, bf16[128,1536]{1,0:T(8,128)(2,1)S(1)}, u32[]{:S(2)}, u32[]{:S(2)}) collective-permute-start(bf16[128,1536]{1,0:T(8,128)(2,1)S(1)} %get-tuple-element.94), channel_id=1, source_target_pairs={{0,192},{32,224},{64,0},{96,32},{128,64},{160,96},{192,128},{224,1... | collective-permute-start | bytes 1179656 | tf_op jit(solution)/shard_map/ppermute | solution.py:52
  49.0 1.7 %collective-permute-start.10 = (bf16[128,1536]{1,0:T(8,128)(2,1)S(1)}, bf16[128,1536]{1,0:T(8,128)(2,1)S(1)}, u32[]{:S(2)}, u32[]{:S(2)}) collective-permute-start(bf16[128,1536]{1,0:T(8,128)(2,1)S(1)} %get-tuple-element.93), channel_id=1, source_target_pairs={{0,128},{32,160},{64,192},{96,224},{128,0},{160,32},{192,64},{224,... | collective-permute-start | bytes 1179656 | tf_op jit(solution)/shard_map/ppermute | solution.py:52
  50.7 1.6 collective-permute-start.12
  52.3 5.1 %collective-permute-done.11.r3 = bf16[128,1536]{1,0:T(8,128)(2,1)S(1)} collective-permute-done((bf16[128,1536]{1,0:T(8,128)(2,1)S(1)}, bf16[128,1536]{1,0:T(8,128)(2,1)S(1)}, u32[]{:S(2)}, u32[]{:S(2)}) %collective-permute-start.11) | collective-permute-done | bytes 393248 | tf_op jit(solution)/shard_map/ppermute | solution.py:52
  57.4 2.4 %collective-permute-start.15 = (bf16[32,1536]{1,0:T(8,128)(2,1)S(1)}, bf16[32,1536]{1,0:T(8,128)(2,1)S(1)}, u32[]{:S(2)}, u32[]{:S(2)}) collective-permute-start(bf16[32,1536]{1,0:T(8,128)(2,1)S(1)} %copy-done.1), channel_id=1, source_target_pairs={{0,6},{1,7},{2,4},{3,5},{4,2},{5,3},{6,0},{7,1},{8,14},{9,15},{10,... | collective-permute-start | bytes 294920 | tf_op jit(solution)/shard_map/ppermute | solution.py:44
  60.9 6.3 %collective-permute-done.10.r2 = bf16[128,1536]{1,0:T(8,128)(2,1)S(1)} collective-permute-done((bf16[128,1536]{1,0:T(8,128)(2,1)S(1)}, bf16[128,1536]{1,0:T(8,128)(2,1)S(1)}, u32[]{:S(2)}, u32[]{:S(2)}) %collective-permute-start.10) | collective-permute-done | bytes 393248 | tf_op jit(solution)/shard_map/ppermute | solution.py:52
  67.4 5.9 %collective-permute-start.16 = (bf16[1552,128]{1,0:T(8,128)(2,1)S(1)}, bf16[1552,128]{1,0:T(8,128)(2,1)S(1)}, u32[]{:S(2)}, u32[]{:S(2)}) collective-permute-start(bf16[1552,128]{1,0:T(8,128)(2,1)S(1)} %back_sum.1.mine), channel_id=1, source_target_pairs={{0,32},{32,0},{64,96},{96,64},{128,160},{160,128},{192,224},{224,1... | collective-permute-start | bytes 1191944 | tf_op jit(solution)/shard_map/ppermute | solution.py:56
  74.2 3.5 %collective-permute-start.19 = (bf16[128,1536]{1,0:T(8,128)(2,1)S(1)}, bf16[128,1536]{1,0:T(8,128)(2,1)S(1)}, u32[]{:S(2)}, u32[]{:S(2)}) collective-permute-start(bf16[128,1536]{1,0:T(8,128)(2,1)S(1)} %get-tuple-element.111.a0), channel_id=1, source_target_pairs={{0,16},{1,17},{2,18},{3,19},{4,20},{5,21},{6,22},{7,23},{8,24},{9,... | collective-permute-start | bytes 1179656 | tf_op jit(solution)/shard_map/ppermute | solution.py:48
  77.7 2.8 %collective-permute-start.17 = (bf16[2,128,768]{2,1,0:T(8,128)(2,1)S(1)}, bf16[2,128,768]{2,1,0:T(8,128)(2,1)S(1)}, u32[]{:S(2)}, u32[]{:S(2)}) collective-permute-start(bf16[2,128,768]{2,1,0:T(8,128)(2,1)S(1)} %bitcast.10), channel_id=1, source_target_pairs={{0,128},{32,160},{64,192},{96,224},{128,0},{160,32},{192,64},{224,... | collective-permute-start | bytes 1179656 | tf_op jit(solution)/shard_map/ppermute | solution.py:52
  81.8 5.3 %collective-permute-done.19.a2 = bf16[128,1536]{1,0:T(8,128)(2,1)S(1)} collective-permute-done((bf16[128,1536]{1,0:T(8,128)(2,1)S(1)}, bf16[128,1536]{1,0:T(8,128)(2,1)S(1)}, u32[]{:S(2)}, u32[]{:S(2)}) %collective-permute-start.19) | collective-permute-done | bytes 393248 | tf_op jit(solution)/shard_map/ppermute | solution.py:48
  88.6 16.8 %collective-permute-start.24 = (bf16[512,1536]{1,0:T(8,128)(2,1)S(1)}, bf16[512,1536]{1,0:T(8,128)(2,1)S(1)}, u32[]{:S(2)}, u32[]{:S(2)}) collective-permute-start(bf16[512,1536]{1,0:T(8,128)(2,1)S(1)} %bitcast.8), channel_id=1, source_target_pairs={{0,1},{1,0},{2,3},{3,2},{4,5},{5,4},{6,7},{7,6},{8,9},{9,8},{10,11... | collective-permute-start | bytes 4718600 | tf_op jit(solution)/shard_map/ppermute | solution.py:40
  105.4 5.5 %collective-permute-start.22 = (bf16[1552,128]{1,0:T(8,128)(2,1)S(1)}, bf16[1552,128]{1,0:T(8,128)(2,1)S(1)}, u32[]{:S(2)}, u32[]{:S(2)}) collective-permute-start(bf16[1552,128]{1,0:T(8,128)(2,1)S(1)} %slope.1.m0), channel_id=1, source_target_pairs={{0,128},{32,160},{64,192},{96,224},{128,0},{160,32},{192,64},{224,... | collective-permute-start | bytes 1191944 | tf_op jit(solution)/shard_map/ppermute | solution.py:52
  111.0 8.0 %collective-permute-done.23.m3 = bf16[1552,128]{1,0:T(8,128)(2,1)S(1)} collective-permute-done((bf16[1552,128]{1,0:T(8,128)(2,1)S(1)}, bf16[1552,128]{1,0:T(8,128)(2,1)S(1)}, u32[]{:S(2)}, u32[]{:S(2)}) %collective-permute-start.23) | collective-permute-done | bytes 397344 | tf_op jit(solution)/shard_map/ppermute | solution.py:52
  119.0 9.4 %collective-permute-done.22.m2 = bf16[1552,128]{1,0:T(8,128)(2,1)S(1)} collective-permute-done((bf16[1552,128]{1,0:T(8,128)(2,1)S(1)}, bf16[1552,128]{1,0:T(8,128)(2,1)S(1)}, u32[]{:S(2)}, u32[]{:S(2)}) %collective-permute-start.22) | collective-permute-done | bytes 397344 | tf_op jit(solution)/shard_map/ppermute | solution.py:52
  128.4 6.1 %input_grad.1 = (f32[128,1536]{1,0:T(8,128)S(1)}, bf16[1552,128]{1,0:T(8,128)(2,1)S(1)}, bf16[1552,128]{1,0:T(8,128)(2,1)S(1)}, bf16[1552,128]{1,0:T(8,128)(2,1)...) custom-call(s32[2]{0:T(128)S(1)} %pad_add_fusion.t, bf16[1552,128]{1,0:T(8,128)(2,1)S(1)} %slope.1.m0, ...), custom_call_target="tpu_custom_call" | custom-call | flops 2415919104 | bytes 9859080 | tf_op jit(solution)/shard_map/input_grad/pallas_call | solution.py:359
  134.6 1.6 collective-permute-start.28
  136.9 2.5 %collective-permute-start.29 = (bf16[2,128,768]{2,1,0:T(8,128)(2,1)S(1)}, bf16[2,128,768]{2,1,0:T(8,128)(2,1)S(1)}, u32[]{:S(2)}, u32[]{:S(2)}) collective-permute-start(bf16[2,128,768]{2,1,0:T(8,128)(2,1)S(1)} %bitcast.13), channel_id=1, source_target_pairs={{0,192},{32,224},{64,0},{96,32},{128,64},{160,96},{192,128},{224,1... | collective-permute-start | bytes 1179656 | tf_op jit(solution)/shard_map/ppermute | solution.py:52
  139.5 7.3 %collective-permute-done.30.r3 = bf16[2,128,768]{2,1,0:T(8,128)(2,1)S(1)} collective-permute-done((bf16[2,128,768]{2,1,0:T(8,128)(2,1)S(1)}, bf16[2,128,768]{2,1,0:T(8,128)(2,1)S(1)}, u32[]{:S(2)}, u32[]{:S(2)}) %collective-permute-start.30) | collective-permute-done | bytes 393248 | tf_op jit(solution)/shard_map/ppermute | solution.py:52
  146.8 6.1 %w_out_grad.1 = bf16[768,1536]{1,0:T(8,128)(2,1)} custom-call(bf16[2,128,768]{2,1,0:T(8,128)(2,1)S(1)} %bitcast.14, bf16[2,128,768]{2,1,0:T(8,128)(2,1)S(1)} %collective-permute-done.29.r1, bf16[2,128,768]{2,1,0:T(8,128)(2,1)S(1)} %collective-permute-done.17.r2, bf16[2,128,768]{2,1,0:T(8,128)(2,1)S(1)} %collective-permute-done.30.r3, ...), custom_call_target="tpu_custom_call" | custom-call | flops 1 | bytes 1 | tf_op jit(solution)/shard_map/w_out_grad/pallas_call | solution.py:359
  153.5 2.2 %collective-permute-done.26.r1 = bf16[1552,128]{1,0:T(8,128)(2,1)S(1)} collective-permute-done((bf16[1552,128]{1,0:T(8,128)(2,1)S(1)}, bf16[1552,128]{1,0:T(8,128)(2,1)S(1)}, u32[]{:S(2)}, u32[]{:S(2)}) %collective-permute-start.26) | collective-permute-done | bytes 397344 | tf_op jit(solution)/shard_map/ppermute | solution.py:48
  156.6 1.5 collective-permute-start.33
  159.2 6.9 %w_in_grad.1 = bf16[1536,768]{1,0:T(8,128)(2,1)} custom-call(s32[2]{0:T(128)S(1)} %pad_add_fusion.t, bf16[4,128,1536]{2,1,0:T(8,128)(2,1)S(1)} %join_inputs.1.inputs, bf16[4,128,1536]{2,1,0:T(8,128)(2,1)S(1)} %collective-permute-done.25.inputs_o, bf16[512,768]{1,0:T(8,128)(2,1)S(1)} %get-tuple-element.139.mine, ...), custom_call_target="tpu_custom_call" | custom-call | flops 2415919104 | bytes 7077896 | tf_op jit(solution)/shard_map/w_in_grad/pallas_call | solution.py:359
  (64 shorter events, 17.9 us)
Async XLA Ops:
  0.6 14.5 %collective-permute-start.3 = (bf16[768,1536]{1,0:T(8,128)(2,1)}, bf16[768,1536]{1,0:T(8,128)(2,1)S(1)}, u32[]{:S(2)}, u32[]{:S(2)}) collective-permute-start(bf16[768,1536]{1,0:T(8,128)(2,1)} %wa.2), channel_id=1, source_target_pairs={{0,1},{1,0},{2,3},{3,2},{4,5},{5,4},{6,7},{7,6},{8,9},{9,8},{10,11... | collective-permute-start | bytes 7077896 | tf_op jit(solution)/shard_map/ppermute | solution.py:40
  6.7 8.5 %collective-permute-start.1 = (bf16[32,1536]{1,0:T(8,128)(2,1)}, bf16[32,1536]{1,0:T(8,128)(2,1)S(1)}, u32[]{:S(2)}, u32[]{:S(2)}) collective-permute-start(bf16[32,1536]{1,0:T(8,128)(2,1)} %a0), channel_id=1, source_target_pairs={{0,4},{1,5},{2,6},{3,7},{4,0},{5,1},{6,2},{7,3},{8,12},{9,13},{10,... | collective-permute-start | bytes 294920 | tf_op jit(solution)/shard_map/ppermute | solution.py:44
  6.7 8.5 %collective-permute-start = (bf16[32,1536]{1,0:T(8,128)(2,1)}, bf16[32,1536]{1,0:T(8,128)(2,1)S(1)}, u32[]{:S(2)}, u32[]{:S(2)}) collective-permute-start(bf16[32,1536]{1,0:T(8,128)(2,1)} %a0), channel_id=1, source_target_pairs={{0,2},{1,3},{2,0},{3,1},{4,6},{5,7},{6,4},{7,5},{8,10},{9,11},{10,... | collective-permute-start | bytes 294920 | tf_op jit(solution)/shard_map/ppermute | solution.py:44
  15.1 23.1 %collective-permute-start.7 = (bf16[1536,768]{1,0:T(8,128)(2,1)}, bf16[1536,768]{1,0:T(8,128)(2,1)S(1)}, u32[]{:S(2)}, u32[]{:S(2)}) collective-permute-start(bf16[1536,768]{1,0:T(8,128)(2,1)} %wa.3), channel_id=1, source_target_pairs={{0,1},{1,0},{2,3},{3,2},{4,5},{5,4},{6,7},{7,6},{8,9},{9,8},{10,11... | collective-permute-start | bytes 7077896 | tf_op jit(solution)/shard_map/ppermute | solution.py:40
  16.5 18.2 %collective-permute-start.6 = (bf16[128,1536]{1,0:T(8,128)(2,1)S(1)}, bf16[128,1536]{1,0:T(8,128)(2,1)S(1)}, u32[]{:S(2)}, u32[]{:S(2)}) collective-permute-start(bf16[128,1536]{1,0:T(8,128)(2,1)S(1)} %get-tuple-element.84.g0), channel_id=1, source_target_pairs={{0,8},{1,9},{2,10},{3,11},{4,12},{5,13},{6,14},{7,15},{8,16},{9,17... | collective-permute-start | bytes 1179656 | tf_op jit(solution)/shard_map/ppermute | solution.py:48
  17.9 20.3 %collective-permute-start.5 = (bf16[128,1536]{1,0:T(8,128)(2,1)S(1)}, bf16[128,1536]{1,0:T(8,128)(2,1)S(1)}, u32[]{:S(2)}, u32[]{:S(2)}) collective-permute-start(bf16[128,1536]{1,0:T(8,128)(2,1)S(1)} %get-tuple-element.84.g0), channel_id=1, source_target_pairs={{0,16},{1,17},{2,18},{3,19},{4,20},{5,21},{6,22},{7,23},{8,24},{9,... | collective-permute-start | bytes 1179656 | tf_op jit(solution)/shard_map/ppermute | solution.py:48
  20.5 17.7 %collective-permute-start.4 = (bf16[128,1536]{1,0:T(8,128)(2,1)S(1)}, bf16[128,1536]{1,0:T(8,128)(2,1)S(1)}, u32[]{:S(2)}, u32[]{:S(2)}) collective-permute-start(bf16[128,1536]{1,0:T(8,128)(2,1)S(1)} %get-tuple-element.84.g0), channel_id=1, source_target_pairs={{0,24},{1,25},{2,26},{3,27},{4,28},{5,29},{6,30},{7,31},{8,0},{9,1... | collective-permute-start | bytes 1179656 | tf_op jit(solution)/shard_map/ppermute | solution.py:48
  21.6 13.1 %collective-permute-start.8 = (bf16[128,768]{1,0:T(8,128)(2,1)}, bf16[128,768]{1,0:T(8,128)(2,1)S(1)}, u32[]{:S(2)}, u32[]{:S(2)}) collective-permute-start(bf16[128,768]{1,0:T(8,128)(2,1)} %here.1), channel_id=1, source_target_pairs={{0,32},{32,0},{64,96},{96,64},{128,160},{160,128},{192,224},{224,1... | collective-permute-start | bytes 589832 | tf_op jit(solution)/shard_map/ppermute | solution.py:56
  46.4 11.0 %collective-permute-start.11 = (bf16[128,1536]{1,0:T(8,128)(2,1)S(1)}, bf16[128,1536]{1,0:T(8,128)(2,1)S(1)}, u32[]{:S(2)}, u32[]{:S(2)}) collective-permute-start(bf16[128,1536]{1,0:T(8,128)(2,1)S(1)} %get-tuple-element.94), channel_id=1, source_target_pairs={{0,192},{32,224},{64,0},{96,32},{128,64},{160,96},{192,128},{224,1... | collective-permute-start | bytes 1179656 | tf_op jit(solution)/shard_map/ppermute | solution.py:52
  49.0 12.0 %collective-permute-start.9 = (bf16[128,1536]{1,0:T(8,128)(2,1)S(1)}, bf16[128,1536]{1,0:T(8,128)(2,1)S(1)}, u32[]{:S(2)}, u32[]{:S(2)}) collective-permute-start(bf16[128,1536]{1,0:T(8,128)(2,1)S(1)} %get-tuple-element.92), channel_id=1, source_target_pairs={{0,64},{32,96},{64,128},{96,160},{128,192},{160,224},{192,0},{224,... | collective-permute-start | bytes 1179656 | tf_op jit(solution)/shard_map/ppermute | solution.py:52
  49.0 18.3 %collective-permute-start.10 = (bf16[128,1536]{1,0:T(8,128)(2,1)S(1)}, bf16[128,1536]{1,0:T(8,128)(2,1)S(1)}, u32[]{:S(2)}, u32[]{:S(2)}) collective-permute-start(bf16[128,1536]{1,0:T(8,128)(2,1)S(1)} %get-tuple-element.93), channel_id=1, source_target_pairs={{0,128},{32,160},{64,192},{96,224},{128,0},{160,32},{192,64},{224,... | collective-permute-start | bytes 1179656 | tf_op jit(solution)/shard_map/ppermute | solution.py:52
  50.7 9.0 %collective-permute-start.12 = (bf16[128,768]{1,0:T(8,128)(2,1)S(1)}, bf16[128,768]{1,0:T(8,128)(2,1)S(1)}, u32[]{:S(2)}, u32[]{:S(2)}) collective-permute-start(bf16[128,768]{1,0:T(8,128)(2,1)S(1)} %bitcast.15), channel_id=1, source_target_pairs={{0,1},{1,0},{2,3},{3,2},{4,5},{5,4},{6,7},{7,6},{8,9},{9,8},{10,11... | collective-permute-start | bytes 589832 | tf_op jit(solution)/shard_map/ppermute | solution.py:40
  57.4 9.9 %collective-permute-start.15 = (bf16[32,1536]{1,0:T(8,128)(2,1)S(1)}, bf16[32,1536]{1,0:T(8,128)(2,1)S(1)}, u32[]{:S(2)}, u32[]{:S(2)}) collective-permute-start(bf16[32,1536]{1,0:T(8,128)(2,1)S(1)} %copy-done.1), channel_id=1, source_target_pairs={{0,6},{1,7},{2,4},{3,5},{4,2},{5,3},{6,0},{7,1},{8,14},{9,15},{10,... | collective-permute-start | bytes 294920 | tf_op jit(solution)/shard_map/ppermute | solution.py:44
  59.7 7.5 %collective-permute-start.14 = (bf16[32,1536]{1,0:T(8,128)(2,1)S(1)}, bf16[32,1536]{1,0:T(8,128)(2,1)S(1)}, u32[]{:S(2)}, u32[]{:S(2)}) collective-permute-start(bf16[32,1536]{1,0:T(8,128)(2,1)S(1)} %copy-done.1), channel_id=1, source_target_pairs={{0,4},{1,5},{2,6},{3,7},{4,0},{5,1},{6,2},{7,3},{8,12},{9,13},{10,... | collective-permute-start | bytes 294920 | tf_op jit(solution)/shard_map/ppermute | solution.py:44
  67.4 20.5 %collective-permute-start.16 = (bf16[1552,128]{1,0:T(8,128)(2,1)S(1)}, bf16[1552,128]{1,0:T(8,128)(2,1)S(1)}, u32[]{:S(2)}, u32[]{:S(2)}) collective-permute-start(bf16[1552,128]{1,0:T(8,128)(2,1)S(1)} %back_sum.1.mine), channel_id=1, source_target_pairs={{0,32},{32,0},{64,96},{96,64},{128,160},{160,128},{192,224},{224,1... | collective-permute-start | bytes 1191944 | tf_op jit(solution)/shard_map/ppermute | solution.py:56
  74.0 7.8 %collective-permute-start.20 = (bf16[128,1536]{1,0:T(8,128)(2,1)S(1)}, bf16[128,1536]{1,0:T(8,128)(2,1)S(1)}, u32[]{:S(2)}, u32[]{:S(2)}) collective-permute-start(bf16[128,1536]{1,0:T(8,128)(2,1)S(1)} %get-tuple-element.111.a0), channel_id=1, source_target_pairs={{0,8},{1,9},{2,10},{3,11},{4,12},{5,13},{6,14},{7,15},{8,16},{9,17... | collective-permute-start | bytes 1179656 | tf_op jit(solution)/shard_map/ppermute | solution.py:48
  74.2 12.9 %collective-permute-start.19 = (bf16[128,1536]{1,0:T(8,128)(2,1)S(1)}, bf16[128,1536]{1,0:T(8,128)(2,1)S(1)}, u32[]{:S(2)}, u32[]{:S(2)}) collective-permute-start(bf16[128,1536]{1,0:T(8,128)(2,1)S(1)} %get-tuple-element.111.a0), channel_id=1, source_target_pairs={{0,16},{1,17},{2,18},{3,19},{4,20},{5,21},{6,22},{7,23},{8,24},{9,... | collective-permute-start | bytes 1179656 | tf_op jit(solution)/shard_map/ppermute | solution.py:48
  77.7 9.4 %collective-permute-start.18 = (bf16[128,1536]{1,0:T(8,128)(2,1)S(1)}, bf16[128,1536]{1,0:T(8,128)(2,1)S(1)}, u32[]{:S(2)}, u32[]{:S(2)}) collective-permute-start(bf16[128,1536]{1,0:T(8,128)(2,1)S(1)} %get-tuple-element.111.a0), channel_id=1, source_target_pairs={{0,24},{1,25},{2,26},{3,27},{4,28},{5,29},{6,30},{7,31},{8,0},{9,1... | collective-permute-start | bytes 1179656 | tf_op jit(solution)/shard_map/ppermute | solution.py:48
  77.7 10.2 %collective-permute-start.17 = (bf16[2,128,768]{2,1,0:T(8,128)(2,1)S(1)}, bf16[2,128,768]{2,1,0:T(8,128)(2,1)S(1)}, u32[]{:S(2)}, u32[]{:S(2)}) collective-permute-start(bf16[2,128,768]{2,1,0:T(8,128)(2,1)S(1)} %bitcast.10), channel_id=1, source_target_pairs={{0,128},{32,160},{64,192},{96,224},{128,0},{160,32},{192,64},{224,... | collective-permute-start | bytes 1179656 | tf_op jit(solution)/shard_map/ppermute | solution.py:52
  88.6 39.9 %collective-permute-start.24 = (bf16[512,1536]{1,0:T(8,128)(2,1)S(1)}, bf16[512,1536]{1,0:T(8,128)(2,1)S(1)}, u32[]{:S(2)}, u32[]{:S(2)}) collective-permute-start(bf16[512,1536]{1,0:T(8,128)(2,1)S(1)} %bitcast.8), channel_id=1, source_target_pairs={{0,1},{1,0},{2,3},{3,2},{4,5},{5,4},{6,7},{7,6},{8,9},{9,8},{10,11... | collective-permute-start | bytes 4718600 | tf_op jit(solution)/shard_map/ppermute | solution.py:40
  105.3 23.1 %collective-permute-start.25 = (bf16[4,128,1536]{2,1,0:T(8,128)(2,1)S(1)}, bf16[4,128,1536]{2,1,0:T(8,128)(2,1)S(1)}, u32[]{:S(2)}, u32[]{:S(2)}) collective-permute-start(bf16[4,128,1536]{2,1,0:T(8,128)(2,1)S(1)} %join_inputs.1.inputs), channel_id=1, source_target_pairs={{0,1},{1,0},{2,3},{3,2},{4,5},{5,4},{6,7},{7,6},{8,9},{9,8},{10,11... | collective-permute-start | bytes 4718600 | tf_op jit(solution)/shard_map/ppermute | solution.py:40
  105.4 13.6 %collective-permute-start.23 = (bf16[1552,128]{1,0:T(8,128)(2,1)S(1)}, bf16[1552,128]{1,0:T(8,128)(2,1)S(1)}, u32[]{:S(2)}, u32[]{:S(2)}) collective-permute-start(bf16[1552,128]{1,0:T(8,128)(2,1)S(1)} %slope.1.m0), channel_id=1, source_target_pairs={{0,64},{32,96},{64,128},{96,160},{128,192},{160,224},{192,0},{224,... | collective-permute-start | bytes 1191944 | tf_op jit(solution)/shard_map/ppermute | solution.py:52
  105.4 23.0 %collective-permute-start.22 = (bf16[1552,128]{1,0:T(8,128)(2,1)S(1)}, bf16[1552,128]{1,0:T(8,128)(2,1)S(1)}, u32[]{:S(2)}, u32[]{:S(2)}) collective-permute-start(bf16[1552,128]{1,0:T(8,128)(2,1)S(1)} %slope.1.m0), channel_id=1, source_target_pairs={{0,128},{32,160},{64,192},{96,224},{128,0},{160,32},{192,64},{224,... | collective-permute-start | bytes 1191944 | tf_op jit(solution)/shard_map/ppermute | solution.py:52
  111.0 17.4 %collective-permute-start.21 = (bf16[1552,128]{1,0:T(8,128)(2,1)S(1)}, bf16[1552,128]{1,0:T(8,128)(2,1)S(1)}, u32[]{:S(2)}, u32[]{:S(2)}) collective-permute-start(bf16[1552,128]{1,0:T(8,128)(2,1)S(1)} %slope.1.m0), channel_id=1, source_target_pairs={{0,192},{32,224},{64,0},{96,32},{128,64},{160,96},{192,128},{224,1... | collective-permute-start | bytes 1191944 | tf_op jit(solution)/shard_map/ppermute | solution.py:52
  134.5 18.4 %collective-permute-start.27 = (bf16[1552,128]{1,0:T(8,128)(2,1)S(1)}, bf16[1552,128]{1,0:T(8,128)(2,1)S(1)}, u32[]{:S(2)}, u32[]{:S(2)}) collective-permute-start(bf16[1552,128]{1,0:T(8,128)(2,1)S(1)} %get-tuple-element.124), channel_id=1, source_target_pairs={{0,16},{1,17},{2,18},{3,19},{4,20},{5,21},{6,22},{7,23},{8,24},{9,... | collective-permute-start | bytes 1191944 | tf_op jit(solution)/shard_map/ppermute | solution.py:48
  134.6 18.9 %collective-permute-start.28 = (bf16[1552,128]{1,0:T(8,128)(2,1)S(1)}, bf16[1552,128]{1,0:T(8,128)(2,1)S(1)}, u32[]{:S(2)}, u32[]{:S(2)}) collective-permute-start(bf16[1552,128]{1,0:T(8,128)(2,1)S(1)} %get-tuple-element.125), channel_id=1, source_target_pairs={{0,24},{1,25},{2,26},{3,27},{4,28},{5,29},{6,30},{7,31},{8,0},{9,1... | collective-permute-start | bytes 1191944 | tf_op jit(solution)/shard_map/ppermute | solution.py:48
  136.3 19.5 %collective-permute-start.26 = (bf16[1552,128]{1,0:T(8,128)(2,1)S(1)}, bf16[1552,128]{1,0:T(8,128)(2,1)S(1)}, u32[]{:S(2)}, u32[]{:S(2)}) collective-permute-start(bf16[1552,128]{1,0:T(8,128)(2,1)S(1)} %get-tuple-element.123.mine), channel_id=1, source_target_pairs={{0,8},{1,9},{2,10},{3,11},{4,12},{5,13},{6,14},{7,15},{8,16},{9,17... | collective-permute-start | bytes 1191944 | tf_op jit(solution)/shard_map/ppermute | solution.py:48
  136.8 10.0 %collective-permute-start.30 = (bf16[2,128,768]{2,1,0:T(8,128)(2,1)S(1)}, bf16[2,128,768]{2,1,0:T(8,128)(2,1)S(1)}, u32[]{:S(2)}, u32[]{:S(2)}) collective-permute-start(bf16[2,128,768]{2,1,0:T(8,128)(2,1)S(1)} %bitcast.12), channel_id=1, source_target_pairs={{0,64},{32,96},{64,128},{96,160},{128,192},{160,224},{192,0},{224,... | collective-permute-start | bytes 1179656 | tf_op jit(solution)/shard_map/ppermute | solution.py:52
  136.9 9.9 %collective-permute-start.29 = (bf16[2,128,768]{2,1,0:T(8,128)(2,1)S(1)}, bf16[2,128,768]{2,1,0:T(8,128)(2,1)S(1)}, u32[]{:S(2)}, u32[]{:S(2)}) collective-permute-start(bf16[2,128,768]{2,1,0:T(8,128)(2,1)S(1)} %bitcast.13), channel_id=1, source_target_pairs={{0,192},{32,224},{64,0},{96,32},{128,64},{160,96},{192,128},{224,1... | collective-permute-start | bytes 1179656 | tf_op jit(solution)/shard_map/ppermute | solution.py:52
  156.5 9.7 %collective-permute-start.32 = (bf16[400,128]{1,0:T(8,128)(2,1)S(1)}, bf16[400,128]{1,0:T(8,128)(2,1)S(1)}, u32[]{:S(2)}, u32[]{:S(2)}) collective-permute-start(bf16[400,128]{1,0:T(8,128)(2,1)S(1)} %get-tuple-element.136), channel_id=1, source_target_pairs={{0,4},{1,5},{2,6},{3,7},{4,0},{5,1},{6,2},{7,3},{8,12},{9,13},{10,... | collective-permute-start | bytes 307208 | tf_op jit(solution)/shard_map/ppermute | solution.py:44
  156.6 9.6 %collective-permute-start.33 = (bf16[400,128]{1,0:T(8,128)(2,1)S(1)}, bf16[400,128]{1,0:T(8,128)(2,1)S(1)}, u32[]{:S(2)}, u32[]{:S(2)}) collective-permute-start(bf16[400,128]{1,0:T(8,128)(2,1)S(1)} %get-tuple-element.137), channel_id=1, source_target_pairs={{0,6},{1,7},{2,4},{3,5},{4,2},{5,3},{6,0},{7,1},{8,14},{9,15},{10,... | collective-permute-start | bytes 307208 | tf_op jit(solution)/shard_map/ppermute | solution.py:44
  158.1 8.7 %collective-permute-start.31 = (bf16[400,128]{1,0:T(8,128)(2,1)S(1)}, bf16[400,128]{1,0:T(8,128)(2,1)S(1)}, u32[]{:S(2)}, u32[]{:S(2)}) collective-permute-start(bf16[400,128]{1,0:T(8,128)(2,1)S(1)} %get-tuple-element.135.mine), channel_id=1, source_target_pairs={{0,2},{1,3},{2,0},{3,1},{4,6},{5,7},{6,4},{7,5},{8,10},{9,11},{10,... | collective-permute-start | bytes 307208 | tf_op jit(solution)/shard_map/ppermute | solution.py:44
  (9 other events, 111.5 us)

commit v7 on v6

--- a/solution.py
+++ b/solution.py
@@ -12,7 +12,7 @@
 barrier = lax.optimization_barrier
 D, FF, T = 1536, 768, 128
 W = 2 * FF
-B, C = 512, 768
+B, C = 768, 768
 
 
 def gelu_value(pre):
@@ -91,14 +91,19 @@
     return slice(c * 128, (c + 1) * 128)
 
 
-def stack_kernel(a0, a1, a2, a3, stacked, tops):
-    for m, a in enumerate((a0, a1, a2, a3)):
-        stacked[m * 32 : (m + 1) * 32] = a[...]
-    top = jnp.max(jnp.abs(a0[...].astype(f32)), axis=0, keepdims=True)
+def first_kernel(a, stacked, tops):
+    stacked[:32] = a[...]
+    top = jnp.max(jnp.abs(a[...].astype(f32)), axis=0, keepdims=True)
     lanes = top[:, :128]
     for k in range(1, D // 128):
         lanes = jnp.maximum(lanes, top[:, 128 * k : 128 * (k + 1)])
     tops[...] = jnp.broadcast_to(lanes, (8, 128))
+
+
+def stack_kernel(so_far, a1, a2, a3, stacked):
+    stacked[:32] = so_far[:32]
+    for m, a in enumerate((a1, a2, a3)):
+        stacked[(m + 1) * 32 : (m + 2) * 32] = a[...]
 
 
 def join_kernel(a0, a1, a2, a3, out, sems):
@@ -386,9 +391,10 @@
 
     got = [to_l(out_grad, k) for k in (1, 2, 3)]
     w_out_o = to_core(w_out)
-    *got, w_out_o, pre_late, w_in_late = barrier((*got, w_out_o, preact, w_in))
     outs = [like(T, D), like(8, 128, dtype=f32)]
-    grad, top_y = call(stack_kernel, "stack", outs, (out_grad, *got))
+    grad, top_y = call(first_kernel, "first", outs, (out_grad,))
+    *got, grad, top_y, w_out_o, pre_late, w_in_late = barrier((*got, grad, top_y, w_out_o, preact, w_in))
+    (grad,) = call(stack_kernel, "stack", outs[:1], (grad, *got), input_output_aliases={0: 0})
     grads = ring(grad, to_y)
     w_in_o = to_core(w_in_late)
     there = to_h(pre_late)
@@ -421,14 +427,15 @@
     pre_b = to_core(pre_other.reshape(T, FF))
     r3, inputs = barrier((r3, inputs))
     got = [to_l(inputs, k) for k in (1, 2, 3)]
-    r1, r2, r3, pre_b, *got = barrier((r1, r2, r3, pre_b, *got))
+    outs = [like(T, D), like(8, 128, dtype=f32)]
+    token_inputs, _ = call(first_kernel, "first_inputs", outs, (inputs,))
+    r1, r2, r3, pre_b, token_inputs, *got = barrier((r1, r2, r3, pre_b, token_inputs, *got))
 
     (sent,) = call(sum_kernel, "back_sum", [message(T)], (own, r1, r2, r3, top_y))
     other = to_h(sent)
     pre, sent, *got = barrier((pre.reshape(2, T, FF), sent, *got))
     pre_far = to_x(pre, 2)
-    outs = [like(T, D), like(8, 128, dtype=f32)]
-    token_inputs, _ = call(stack_kernel, "stack_inputs", outs, (inputs, *got))
+    (token_inputs,) = call(stack_kernel, "stack_inputs", [like(T, D)], (token_inputs, *got), input_output_aliases={0: 0})
     token_inputs = ring(token_inputs, to_y)
     outs = [like(4, T, D)]
     (inputs_all,) = call(

time: 170 us -> 169 us (level)
    pallas_call x11 -> x13, Pallas kernels: 27.9 us -> 27.7 us  [call(): pl.pallas_call(kernel, out_shape=outs, name=name, compiler_params=pltpu.C...]
where the time goes in v7:
time: 169 us
  starting transfers between devices  72 us (43%)
  waiting for transfers between devices  63.8 us (38%)
  Pallas kernels  27.7 us (16%)
  local copies, waits for them, and re-layouts  3.54 us (2%)
    ppermute x9, waiting for transfers between devices, to_x(): return lax.ppermute(v, 'row', [(i, (i + 2 * k) % 8) for i in range(8)])  35.5 us
    pallas_call x13, Pallas kernels, call(): pl.pallas_call(kernel, out_shape=outs, name=name, compiler_params=pltpu.C...  27.7 us
    ppermute x7, starting transfers between devices, to_core(): return lax.ppermute(v, 'col', [(i, i ^ 1) for i in range(32)])  23.7 us
    ppermute x9, starting transfers between devices, to_x(): return lax.ppermute(v, 'row', [(i, (i + 2 * k) % 8) for i in range(8)])  15.2 us
    ppermute x9, waiting for transfers between devices, to_y(): return lax.ppermute(v, 'col', [(i, (i + 8 * k) % 32) for i in range(32)])  12.9 us
    ppermute x2, starting transfers between devices, to_h(): return lax.ppermute(v, 'row', [(i, i ^ 1) for i in range(8)])  11.7 us
    ppermute x9, starting transfers between devices, to_y(): return lax.ppermute(v, 'col', [(i, (i + 8 * k) % 32) for i in range(32)])  11.5 us
    ppermute x9, starting transfers between devices, to_l(): return lax.ppermute(v, 'col', [(i, i ^ 2 * k) for i in range(32)])  9.84 us
  transfers between devices with their start and end apart: 36, of which 15 were waited for; matrix products, arithmetic and copies ran while one was open for 0% of the time, Pallas kernels for 9%

profile of v7, /device:TPU:1, one launch (start us, length us, event | category | flops | bytes accessed | tf_op | source)
XLA Modules:
  0.0 168.6 jit_solution(6283050713992145472)
XLA Ops:
  0.6 3.3 %collective-permute-start.3 = (bf16[768,1536]{1,0:T(8,128)(2,1)}, bf16[768,1536]{1,0:T(8,128)(2,1)S(1)}, u32[]{:S(2)}, u32[]{:S(2)}) collective-permute-start(bf16[768,1536]{1,0:T(8,128)(2,1)} %wa.2), channel_id=1, source_target_pairs={{0,1},{1,0},{2,3},{3,2},{4,5},{5,4},{6,7},{7,6},{8,9},{9,8},{10,11... | collective-permute-start | bytes 7077896 | tf_op jit(solution)/shard_map/ppermute | solution.py:40
  4.0 2.6 %collective-permute-start.2 = (bf16[32,1536]{1,0:T(8,128)(2,1)}, bf16[32,1536]{1,0:T(8,128)(2,1)S(1)}, u32[]{:S(2)}, u32[]{:S(2)}) collective-permute-start(bf16[32,1536]{1,0:T(8,128)(2,1)} %a), channel_id=1, source_target_pairs={{0,6},{1,7},{2,4},{3,5},{4,2},{5,3},{6,0},{7,1},{8,14},{9,15},{10,... | collective-permute-start | bytes 294920 | tf_op jit(solution)/shard_map/ppermute | solution.py:44
  8.6 1.9 %collective-permute-done.2.a3 = bf16[32,1536]{1,0:T(8,128)(2,1)S(1)} collective-permute-done((bf16[32,1536]{1,0:T(8,128)(2,1)}, bf16[32,1536]{1,0:T(8,128)(2,1)S(1)}, u32[]{:S(2)}, u32[]{:S(2)}) %collective-permute-start.2) | collective-permute-done | bytes 98336 | tf_op jit(solution)/shard_map/ppermute | solution.py:44
  10.5 4.6 %collective-permute-done.1.a2 = bf16[32,1536]{1,0:T(8,128)(2,1)S(1)} collective-permute-done((bf16[32,1536]{1,0:T(8,128)(2,1)}, bf16[32,1536]{1,0:T(8,128)(2,1)S(1)}, u32[]{:S(2)}, u32[]{:S(2)}) %collective-permute-start.1) | collective-permute-done | bytes 98336 | tf_op jit(solution)/shard_map/ppermute | solution.py:44
  17.0 2.6 %collective-permute-start.5 = (bf16[128,1536]{1,0:T(8,128)(2,1)S(1)}, bf16[128,1536]{1,0:T(8,128)(2,1)S(1)}, u32[]{:S(2)}, u32[]{:S(2)}) collective-permute-start(bf16[128,1536]{1,0:T(8,128)(2,1)S(1)} %stack.13.g0), channel_id=1, source_target_pairs={{0,16},{1,17},{2,18},{3,19},{4,20},{5,21},{6,22},{7,23},{8,24},{9,... | collective-permute-start | bytes 1179656 | tf_op jit(solution)/shard_map/ppermute | solution.py:48
  20.7 5.8 %collective-permute-start.8 = (bf16[128,768]{1,0:T(8,128)(2,1)}, bf16[128,768]{1,0:T(8,128)(2,1)S(1)}, u32[]{:S(2)}, u32[]{:S(2)}) collective-permute-start(bf16[128,768]{1,0:T(8,128)(2,1)} %here.1), channel_id=1, source_target_pairs={{0,32},{32,0},{64,96},{96,64},{128,160},{160,128},{192,224},{224,1... | collective-permute-start | bytes 589832 | tf_op jit(solution)/shard_map/ppermute | solution.py:56
  26.5 7.2 %collective-permute-done.8.there = bf16[128,768]{1,0:T(8,128)(2,1)S(1)} collective-permute-done((bf16[128,768]{1,0:T(8,128)(2,1)}, bf16[128,768]{1,0:T(8,128)(2,1)S(1)}, u32[]{:S(2)}, u32[]{:S(2)}) %collective-permute-start.8) | collective-permute-done | bytes 196640 | tf_op jit(solution)/shard_map/ppermute | solution.py:56
  33.8 3.5 %collective-permute-done.5.g2 = bf16[128,1536]{1,0:T(8,128)(2,1)S(1)} collective-permute-done((bf16[128,1536]{1,0:T(8,128)(2,1)S(1)}, bf16[128,1536]{1,0:T(8,128)(2,1)S(1)}, u32[]{:S(2)}, u32[]{:S(2)}) %collective-permute-start.5) | collective-permute-done | bytes 393248 | tf_op jit(solution)/shard_map/ppermute | solution.py:48
  37.3 1.7 copy-done.2
  39.9 5.6 %back.1 = (f32[128,1536]{1,0:T(8,128)S(1)}, bf16[128,1536]{1,0:T(8,128)(2,1)S(1)}, bf16[128,1536]{1,0:T(8,128)(2,1)S(1)}, bf16[128,1536]{1,0:T(8,128)(2,1)S(1)},...) custom-call(s32[2]{0:T(128)S(1)} %pad_add_fusion.t, ...), custom_call_target="tpu_custom_call" | custom-call | flops 2415919104 | bytes 10813448 | tf_op jit(solution)/shard_map/back/pallas_call | solution.py:364
  45.5 2.6 %collective-permute-start.11 = (bf16[128,1536]{1,0:T(8,128)(2,1)S(1)}, bf16[128,1536]{1,0:T(8,128)(2,1)S(1)}, u32[]{:S(2)}, u32[]{:S(2)}) collective-permute-start(bf16[128,1536]{1,0:T(8,128)(2,1)S(1)} %get-tuple-element.99), channel_id=1, source_target_pairs={{0,192},{32,224},{64,0},{96,32},{128,64},{160,96},{192,128},{224,1... | collective-permute-start | bytes 1179656 | tf_op jit(solution)/shard_map/ppermute | solution.py:52
  48.1 1.7 %collective-permute-start.10 = (bf16[128,1536]{1,0:T(8,128)(2,1)S(1)}, bf16[128,1536]{1,0:T(8,128)(2,1)S(1)}, u32[]{:S(2)}, u32[]{:S(2)}) collective-permute-start(bf16[128,1536]{1,0:T(8,128)(2,1)S(1)} %get-tuple-element.98), channel_id=1, source_target_pairs={{0,128},{32,160},{64,192},{96,224},{128,0},{160,32},{192,64},{224,... | collective-permute-start | bytes 1179656 | tf_op jit(solution)/shard_map/ppermute | solution.py:52
  49.8 1.6 collective-permute-start.12
  51.4 5.1 %collective-permute-done.11.r3 = bf16[128,1536]{1,0:T(8,128)(2,1)S(1)} collective-permute-done((bf16[128,1536]{1,0:T(8,128)(2,1)S(1)}, bf16[128,1536]{1,0:T(8,128)(2,1)S(1)}, u32[]{:S(2)}, u32[]{:S(2)}) %collective-permute-start.11) | collective-permute-done | bytes 393248 | tf_op jit(solution)/shard_map/ppermute | solution.py:52
  56.5 2.4 %collective-permute-start.15 = (bf16[32,1536]{1,0:T(8,128)(2,1)S(1)}, bf16[32,1536]{1,0:T(8,128)(2,1)S(1)}, u32[]{:S(2)}, u32[]{:S(2)}) collective-permute-start(bf16[32,1536]{1,0:T(8,128)(2,1)S(1)} %copy-done.1), channel_id=1, source_target_pairs={{0,6},{1,7},{2,4},{3,5},{4,2},{5,3},{6,0},{7,1},{8,14},{9,15},{10,... | collective-permute-start | bytes 294920 | tf_op jit(solution)/shard_map/ppermute | solution.py:44
  60.7 5.7 %collective-permute-done.10.r2 = bf16[128,1536]{1,0:T(8,128)(2,1)S(1)} collective-permute-done((bf16[128,1536]{1,0:T(8,128)(2,1)S(1)}, bf16[128,1536]{1,0:T(8,128)(2,1)S(1)}, u32[]{:S(2)}, u32[]{:S(2)}) %collective-permute-start.10) | collective-permute-done | bytes 393248 | tf_op jit(solution)/shard_map/ppermute | solution.py:52
  66.6 5.9 %collective-permute-start.16 = (bf16[1552,128]{1,0:T(8,128)(2,1)S(1)}, bf16[1552,128]{1,0:T(8,128)(2,1)S(1)}, u32[]{:S(2)}, u32[]{:S(2)}) collective-permute-start(bf16[1552,128]{1,0:T(8,128)(2,1)S(1)} %back_sum.1.mine), channel_id=1, source_target_pairs={{0,32},{32,0},{64,96},{96,64},{128,160},{160,128},{192,224},{224,1... | collective-permute-start | bytes 1191944 | tf_op jit(solution)/shard_map/ppermute | solution.py:56
  73.0 3.5 %collective-permute-start.19 = (bf16[128,1536]{1,0:T(8,128)(2,1)S(1)}, bf16[128,1536]{1,0:T(8,128)(2,1)S(1)}, u32[]{:S(2)}, u32[]{:S(2)}) collective-permute-start(bf16[128,1536]{1,0:T(8,128)(2,1)S(1)} %stack_inputs.1.a0), channel_id=1, source_target_pairs={{0,16},{1,17},{2,18},{3,19},{4,20},{5,21},{6,22},{7,23},{8,24},{9,... | collective-permute-start | bytes 1179656 | tf_op jit(solution)/shard_map/ppermute | solution.py:48
  76.5 2.7 %collective-permute-start.17 = (bf16[2,128,768]{2,1,0:T(8,128)(2,1)S(1)}, bf16[2,128,768]{2,1,0:T(8,128)(2,1)S(1)}, u32[]{:S(2)}, u32[]{:S(2)}) collective-permute-start(bf16[2,128,768]{2,1,0:T(8,128)(2,1)S(1)} %bitcast.10), channel_id=1, source_target_pairs={{0,128},{32,160},{64,192},{96,224},{128,0},{160,32},{192,64},{224,... | collective-permute-start | bytes 1179656 | tf_op jit(solution)/shard_map/ppermute | solution.py:52
  80.6 5.3 %collective-permute-done.19.a2 = bf16[128,1536]{1,0:T(8,128)(2,1)S(1)} collective-permute-done((bf16[128,1536]{1,0:T(8,128)(2,1)S(1)}, bf16[128,1536]{1,0:T(8,128)(2,1)S(1)}, u32[]{:S(2)}, u32[]{:S(2)}) %collective-permute-start.19) | collective-permute-done | bytes 393248 | tf_op jit(solution)/shard_map/ppermute | solution.py:48
  87.3 16.8 %collective-permute-start.24 = (bf16[512,1536]{1,0:T(8,128)(2,1)S(1)}, bf16[512,1536]{1,0:T(8,128)(2,1)S(1)}, u32[]{:S(2)}, u32[]{:S(2)}) collective-permute-start(bf16[512,1536]{1,0:T(8,128)(2,1)S(1)} %bitcast.8), channel_id=1, source_target_pairs={{0,1},{1,0},{2,3},{3,2},{4,5},{5,4},{6,7},{7,6},{8,9},{9,8},{10,11... | collective-permute-start | bytes 4718600 | tf_op jit(solution)/shard_map/ppermute | solution.py:40
  104.2 5.5 %collective-permute-start.22 = (bf16[1552,128]{1,0:T(8,128)(2,1)S(1)}, bf16[1552,128]{1,0:T(8,128)(2,1)S(1)}, u32[]{:S(2)}, u32[]{:S(2)}) collective-permute-start(bf16[1552,128]{1,0:T(8,128)(2,1)S(1)} %slope.1.m0), channel_id=1, source_target_pairs={{0,128},{32,160},{64,192},{96,224},{128,0},{160,32},{192,64},{224,... | collective-permute-start | bytes 1191944 | tf_op jit(solution)/shard_map/ppermute | solution.py:52
  109.7 8.0 %collective-permute-done.23.m3 = bf16[1552,128]{1,0:T(8,128)(2,1)S(1)} collective-permute-done((bf16[1552,128]{1,0:T(8,128)(2,1)S(1)}, bf16[1552,128]{1,0:T(8,128)(2,1)S(1)}, u32[]{:S(2)}, u32[]{:S(2)}) %collective-permute-start.23) | collective-permute-done | bytes 397344 | tf_op jit(solution)/shard_map/ppermute | solution.py:52
  117.8 9.4 %collective-permute-done.22.m2 = bf16[1552,128]{1,0:T(8,128)(2,1)S(1)} collective-permute-done((bf16[1552,128]{1,0:T(8,128)(2,1)S(1)}, bf16[1552,128]{1,0:T(8,128)(2,1)S(1)}, u32[]{:S(2)}, u32[]{:S(2)}) %collective-permute-start.22) | collective-permute-done | bytes 397344 | tf_op jit(solution)/shard_map/ppermute | solution.py:52
  127.2 6.1 %input_grad.1 = (f32[128,1536]{1,0:T(8,128)S(1)}, bf16[1552,128]{1,0:T(8,128)(2,1)S(1)}, bf16[1552,128]{1,0:T(8,128)(2,1)S(1)}, bf16[1552,128]{1,0:T(8,128)(2,1)...) custom-call(s32[2]{0:T(128)S(1)} %pad_add_fusion.t, bf16[1552,128]{1,0:T(8,128)(2,1)S(1)} %slope.1.m0, ...), custom_call_target="tpu_custom_call" | custom-call | flops 2415919104 | bytes 9859080 | tf_op jit(solution)/shard_map/input_grad/pallas_call | solution.py:364
  133.4 1.8 %collective-permute-start.28 = (bf16[1552,128]{1,0:T(8,128)(2,1)S(1)}, bf16[1552,128]{1,0:T(8,128)(2,1)S(1)}, u32[]{:S(2)}, u32[]{:S(2)}) collective-permute-start(bf16[1552,128]{1,0:T(8,128)(2,1)S(1)} %get-tuple-element.131), channel_id=1, source_target_pairs={{0,24},{1,25},{2,26},{3,27},{4,28},{5,29},{6,30},{7,31},{8,0},{9,1... | collective-permute-start | bytes 1191944 | tf_op jit(solution)/shard_map/ppermute | solution.py:48
  135.9 2.5 %collective-permute-start.29 = (bf16[2,128,768]{2,1,0:T(8,128)(2,1)S(1)}, bf16[2,128,768]{2,1,0:T(8,128)(2,1)S(1)}, u32[]{:S(2)}, u32[]{:S(2)}) collective-permute-start(bf16[2,128,768]{2,1,0:T(8,128)(2,1)S(1)} %bitcast.13), channel_id=1, source_target_pairs={{0,192},{32,224},{64,0},{96,32},{128,64},{160,96},{192,128},{224,1... | collective-permute-start | bytes 1179656 | tf_op jit(solution)/shard_map/ppermute | solution.py:52
  138.4 7.3 %collective-permute-done.30.r3 = bf16[2,128,768]{2,1,0:T(8,128)(2,1)S(1)} collective-permute-done((bf16[2,128,768]{2,1,0:T(8,128)(2,1)S(1)}, bf16[2,128,768]{2,1,0:T(8,128)(2,1)S(1)}, u32[]{:S(2)}, u32[]{:S(2)}) %collective-permute-start.30) | collective-permute-done | bytes 393248 | tf_op jit(solution)/shard_map/ppermute | solution.py:52
  145.7 6.0 %w_out_grad.1 = bf16[768,1536]{1,0:T(8,128)(2,1)} custom-call(bf16[2,128,768]{2,1,0:T(8,128)(2,1)S(1)} %bitcast.14, bf16[2,128,768]{2,1,0:T(8,128)(2,1)S(1)} %collective-permute-done.29.r1, bf16[2,128,768]{2,1,0:T(8,128)(2,1)S(1)} %collective-permute-done.17.r2, bf16[2,128,768]{2,1,0:T(8,128)(2,1)S(1)} %collective-permute-done.30.r3, ...), custom_call_target="tpu_custom_call" | custom-call | flops 1 | bytes 1 | tf_op jit(solution)/shard_map/w_out_grad/pallas_call | solution.py:364
  152.5 2.1 %collective-permute-done.26.r1 = bf16[1552,128]{1,0:T(8,128)(2,1)S(1)} collective-permute-done((bf16[1552,128]{1,0:T(8,128)(2,1)S(1)}, bf16[1552,128]{1,0:T(8,128)(2,1)S(1)}, u32[]{:S(2)}, u32[]{:S(2)}) %collective-permute-start.26) | collective-permute-done | bytes 397344 | tf_op jit(solution)/shard_map/ppermute | solution.py:48
  155.3 1.5 collective-permute-start.33
  158.0 6.8 %w_in_grad.1 = bf16[1536,768]{1,0:T(8,128)(2,1)} custom-call(s32[2]{0:T(128)S(1)} %pad_add_fusion.t, bf16[4,128,1536]{2,1,0:T(8,128)(2,1)S(1)} %join_inputs.1.inputs, bf16[4,128,1536]{2,1,0:T(8,128)(2,1)S(1)} %collective-permute-done.25.inputs_o, bf16[512,768]{1,0:T(8,128)(2,1)S(1)} %get-tuple-element.145.mine, ...), custom_call_target="tpu_custom_call" | custom-call | flops 2415919104 | bytes 7077896 | tf_op jit(solution)/shard_map/w_in_grad/pallas_call | solution.py:364
  (66 shorter events, 18.5 us)
Async XLA Ops:
  0.6 14.5 %collective-permute-start.3 = (bf16[768,1536]{1,0:T(8,128)(2,1)}, bf16[768,1536]{1,0:T(8,128)(2,1)S(1)}, u32[]{:S(2)}, u32[]{:S(2)}) collective-permute-start(bf16[768,1536]{1,0:T(8,128)(2,1)} %wa.2), channel_id=1, source_target_pairs={{0,1},{1,0},{2,3},{3,2},{4,5},{5,4},{6,7},{7,6},{8,9},{9,8},{10,11... | collective-permute-start | bytes 7077896 | tf_op jit(solution)/shard_map/ppermute | solution.py:40
  6.7 8.5 %collective-permute-start.1 = (bf16[32,1536]{1,0:T(8,128)(2,1)}, bf16[32,1536]{1,0:T(8,128)(2,1)S(1)}, u32[]{:S(2)}, u32[]{:S(2)}) collective-permute-start(bf16[32,1536]{1,0:T(8,128)(2,1)} %a), channel_id=1, source_target_pairs={{0,4},{1,5},{2,6},{3,7},{4,0},{5,1},{6,2},{7,3},{8,12},{9,13},{10,... | collective-permute-start | bytes 294920 | tf_op jit(solution)/shard_map/ppermute | solution.py:44
  6.7 8.5 %collective-permute-start = (bf16[32,1536]{1,0:T(8,128)(2,1)}, bf16[32,1536]{1,0:T(8,128)(2,1)S(1)}, u32[]{:S(2)}, u32[]{:S(2)}) collective-permute-start(bf16[32,1536]{1,0:T(8,128)(2,1)} %a), channel_id=1, source_target_pairs={{0,2},{1,3},{2,0},{3,1},{4,6},{5,7},{6,4},{7,5},{8,10},{9,11},{10,... | collective-permute-start | bytes 294920 | tf_op jit(solution)/shard_map/ppermute | solution.py:44
  15.1 22.2 %collective-permute-start.7 = (bf16[1536,768]{1,0:T(8,128)(2,1)}, bf16[1536,768]{1,0:T(8,128)(2,1)S(1)}, u32[]{:S(2)}, u32[]{:S(2)}) collective-permute-start(bf16[1536,768]{1,0:T(8,128)(2,1)} %wa.3), channel_id=1, source_target_pairs={{0,1},{1,0},{2,3},{3,2},{4,5},{5,4},{6,7},{7,6},{8,9},{9,8},{10,11... | collective-permute-start | bytes 7077896 | tf_op jit(solution)/shard_map/ppermute | solution.py:40
  15.6 18.2 %collective-permute-start.6 = (bf16[128,1536]{1,0:T(8,128)(2,1)S(1)}, bf16[128,1536]{1,0:T(8,128)(2,1)S(1)}, u32[]{:S(2)}, u32[]{:S(2)}) collective-permute-start(bf16[128,1536]{1,0:T(8,128)(2,1)S(1)} %stack.13.g0), channel_id=1, source_target_pairs={{0,8},{1,9},{2,10},{3,11},{4,12},{5,13},{6,14},{7,15},{8,16},{9,17... | collective-permute-start | bytes 1179656 | tf_op jit(solution)/shard_map/ppermute | solution.py:48
  17.0 20.3 %collective-permute-start.5 = (bf16[128,1536]{1,0:T(8,128)(2,1)S(1)}, bf16[128,1536]{1,0:T(8,128)(2,1)S(1)}, u32[]{:S(2)}, u32[]{:S(2)}) collective-permute-start(bf16[128,1536]{1,0:T(8,128)(2,1)S(1)} %stack.13.g0), channel_id=1, source_target_pairs={{0,16},{1,17},{2,18},{3,19},{4,20},{5,21},{6,22},{7,23},{8,24},{9,... | collective-permute-start | bytes 1179656 | tf_op jit(solution)/shard_map/ppermute | solution.py:48
  19.6 17.7 %collective-permute-start.4 = (bf16[128,1536]{1,0:T(8,128)(2,1)S(1)}, bf16[128,1536]{1,0:T(8,128)(2,1)S(1)}, u32[]{:S(2)}, u32[]{:S(2)}) collective-permute-start(bf16[128,1536]{1,0:T(8,128)(2,1)S(1)} %stack.13.g0), channel_id=1, source_target_pairs={{0,24},{1,25},{2,26},{3,27},{4,28},{5,29},{6,30},{7,31},{8,0},{9,1... | collective-permute-start | bytes 1179656 | tf_op jit(solution)/shard_map/ppermute | solution.py:48
  20.7 13.1 %collective-permute-start.8 = (bf16[128,768]{1,0:T(8,128)(2,1)}, bf16[128,768]{1,0:T(8,128)(2,1)S(1)}, u32[]{:S(2)}, u32[]{:S(2)}) collective-permute-start(bf16[128,768]{1,0:T(8,128)(2,1)} %here.1), channel_id=1, source_target_pairs={{0,32},{32,0},{64,96},{96,64},{128,160},{160,128},{192,224},{224,1... | collective-permute-start | bytes 589832 | tf_op jit(solution)/shard_map/ppermute | solution.py:56
  45.5 11.0 %collective-permute-start.11 = (bf16[128,1536]{1,0:T(8,128)(2,1)S(1)}, bf16[128,1536]{1,0:T(8,128)(2,1)S(1)}, u32[]{:S(2)}, u32[]{:S(2)}) collective-permute-start(bf16[128,1536]{1,0:T(8,128)(2,1)S(1)} %get-tuple-element.99), channel_id=1, source_target_pairs={{0,192},{32,224},{64,0},{96,32},{128,64},{160,96},{192,128},{224,1... | collective-permute-start | bytes 1179656 | tf_op jit(solution)/shard_map/ppermute | solution.py:52
  48.1 12.6 %collective-permute-start.9 = (bf16[128,1536]{1,0:T(8,128)(2,1)S(1)}, bf16[128,1536]{1,0:T(8,128)(2,1)S(1)}, u32[]{:S(2)}, u32[]{:S(2)}) collective-permute-start(bf16[128,1536]{1,0:T(8,128)(2,1)S(1)} %get-tuple-element.97), channel_id=1, source_target_pairs={{0,64},{32,96},{64,128},{96,160},{128,192},{160,224},{192,0},{224,... | collective-permute-start | bytes 1179656 | tf_op jit(solution)/shard_map/ppermute | solution.py:52
  48.1 18.3 %collective-permute-start.10 = (bf16[128,1536]{1,0:T(8,128)(2,1)S(1)}, bf16[128,1536]{1,0:T(8,128)(2,1)S(1)}, u32[]{:S(2)}, u32[]{:S(2)}) collective-permute-start(bf16[128,1536]{1,0:T(8,128)(2,1)S(1)} %get-tuple-element.98), channel_id=1, source_target_pairs={{0,128},{32,160},{64,192},{96,224},{128,0},{160,32},{192,64},{224,... | collective-permute-start | bytes 1179656 | tf_op jit(solution)/shard_map/ppermute | solution.py:52
  49.8 9.1 %collective-permute-start.12 = (bf16[128,768]{1,0:T(8,128)(2,1)S(1)}, bf16[128,768]{1,0:T(8,128)(2,1)S(1)}, u32[]{:S(2)}, u32[]{:S(2)}) collective-permute-start(bf16[128,768]{1,0:T(8,128)(2,1)S(1)} %bitcast.15), channel_id=1, source_target_pairs={{0,1},{1,0},{2,3},{3,2},{4,5},{5,4},{6,7},{7,6},{8,9},{9,8},{10,11... | collective-permute-start | bytes 589832 | tf_op jit(solution)/shard_map/ppermute | solution.py:40
  56.5 9.9 %collective-permute-start.15 = (bf16[32,1536]{1,0:T(8,128)(2,1)S(1)}, bf16[32,1536]{1,0:T(8,128)(2,1)S(1)}, u32[]{:S(2)}, u32[]{:S(2)}) collective-permute-start(bf16[32,1536]{1,0:T(8,128)(2,1)S(1)} %copy-done.1), channel_id=1, source_target_pairs={{0,6},{1,7},{2,4},{3,5},{4,2},{5,3},{6,0},{7,1},{8,14},{9,15},{10,... | collective-permute-start | bytes 294920 | tf_op jit(solution)/shard_map/ppermute | solution.py:44
  58.9 7.5 %collective-permute-start.14 = (bf16[32,1536]{1,0:T(8,128)(2,1)S(1)}, bf16[32,1536]{1,0:T(8,128)(2,1)S(1)}, u32[]{:S(2)}, u32[]{:S(2)}) collective-permute-start(bf16[32,1536]{1,0:T(8,128)(2,1)S(1)} %copy-done.1), channel_id=1, source_target_pairs={{0,4},{1,5},{2,6},{3,7},{4,0},{5,1},{6,2},{7,3},{8,12},{9,13},{10,... | collective-permute-start | bytes 294920 | tf_op jit(solution)/shard_map/ppermute | solution.py:44
  66.6 20.1 %collective-permute-start.16 = (bf16[1552,128]{1,0:T(8,128)(2,1)S(1)}, bf16[1552,128]{1,0:T(8,128)(2,1)S(1)}, u32[]{:S(2)}, u32[]{:S(2)}) collective-permute-start(bf16[1552,128]{1,0:T(8,128)(2,1)S(1)} %back_sum.1.mine), channel_id=1, source_target_pairs={{0,32},{32,0},{64,96},{96,64},{128,160},{160,128},{192,224},{224,1... | collective-permute-start | bytes 1191944 | tf_op jit(solution)/shard_map/ppermute | solution.py:56
  72.5 8.1 %collective-permute-start.20 = (bf16[128,1536]{1,0:T(8,128)(2,1)S(1)}, bf16[128,1536]{1,0:T(8,128)(2,1)S(1)}, u32[]{:S(2)}, u32[]{:S(2)}) collective-permute-start(bf16[128,1536]{1,0:T(8,128)(2,1)S(1)} %stack_inputs.1.a0), channel_id=1, source_target_pairs={{0,8},{1,9},{2,10},{3,11},{4,12},{5,13},{6,14},{7,15},{8,16},{9,17... | collective-permute-start | bytes 1179656 | tf_op jit(solution)/shard_map/ppermute | solution.py:48
  73.0 12.9 %collective-permute-start.19 = (bf16[128,1536]{1,0:T(8,128)(2,1)S(1)}, bf16[128,1536]{1,0:T(8,128)(2,1)S(1)}, u32[]{:S(2)}, u32[]{:S(2)}) collective-permute-start(bf16[128,1536]{1,0:T(8,128)(2,1)S(1)} %stack_inputs.1.a0), channel_id=1, source_target_pairs={{0,16},{1,17},{2,18},{3,19},{4,20},{5,21},{6,22},{7,23},{8,24},{9,... | collective-permute-start | bytes 1179656 | tf_op jit(solution)/shard_map/ppermute | solution.py:48
  76.5 9.4 %collective-permute-start.18 = (bf16[128,1536]{1,0:T(8,128)(2,1)S(1)}, bf16[128,1536]{1,0:T(8,128)(2,1)S(1)}, u32[]{:S(2)}, u32[]{:S(2)}) collective-permute-start(bf16[128,1536]{1,0:T(8,128)(2,1)S(1)} %stack_inputs.1.a0), channel_id=1, source_target_pairs={{0,24},{1,25},{2,26},{3,27},{4,28},{5,29},{6,30},{7,31},{8,0},{9,1... | collective-permute-start | bytes 1179656 | tf_op jit(solution)/shard_map/ppermute | solution.py:48
  76.5 10.2 %collective-permute-start.17 = (bf16[2,128,768]{2,1,0:T(8,128)(2,1)S(1)}, bf16[2,128,768]{2,1,0:T(8,128)(2,1)S(1)}, u32[]{:S(2)}, u32[]{:S(2)}) collective-permute-start(bf16[2,128,768]{2,1,0:T(8,128)(2,1)S(1)} %bitcast.10), channel_id=1, source_target_pairs={{0,128},{32,160},{64,192},{96,224},{128,0},{160,32},{192,64},{224,... | collective-permute-start | bytes 1179656 | tf_op jit(solution)/shard_map/ppermute | solution.py:52
  87.3 39.8 %collective-permute-start.24 = (bf16[512,1536]{1,0:T(8,128)(2,1)S(1)}, bf16[512,1536]{1,0:T(8,128)(2,1)S(1)}, u32[]{:S(2)}, u32[]{:S(2)}) collective-permute-start(bf16[512,1536]{1,0:T(8,128)(2,1)S(1)} %bitcast.8), channel_id=1, source_target_pairs={{0,1},{1,0},{2,3},{3,2},{4,5},{5,4},{6,7},{7,6},{8,9},{9,8},{10,11... | collective-permute-start | bytes 4718600 | tf_op jit(solution)/shard_map/ppermute | solution.py:40
  104.1 23.0 %collective-permute-start.25 = (bf16[4,128,1536]{2,1,0:T(8,128)(2,1)S(1)}, bf16[4,128,1536]{2,1,0:T(8,128)(2,1)S(1)}, u32[]{:S(2)}, u32[]{:S(2)}) collective-permute-start(bf16[4,128,1536]{2,1,0:T(8,128)(2,1)S(1)} %join_inputs.1.inputs), channel_id=1, source_target_pairs={{0,1},{1,0},{2,3},{3,2},{4,5},{5,4},{6,7},{7,6},{8,9},{9,8},{10,11... | collective-permute-start | bytes 4718600 | tf_op jit(solution)/shard_map/ppermute | solution.py:40
  104.2 13.6 %collective-permute-start.23 = (bf16[1552,128]{1,0:T(8,128)(2,1)S(1)}, bf16[1552,128]{1,0:T(8,128)(2,1)S(1)}, u32[]{:S(2)}, u32[]{:S(2)}) collective-permute-start(bf16[1552,128]{1,0:T(8,128)(2,1)S(1)} %slope.1.m0), channel_id=1, source_target_pairs={{0,64},{32,96},{64,128},{96,160},{128,192},{160,224},{192,0},{224,... | collective-permute-start | bytes 1191944 | tf_op jit(solution)/shard_map/ppermute | solution.py:52
  104.2 22.9 %collective-permute-start.22 = (bf16[1552,128]{1,0:T(8,128)(2,1)S(1)}, bf16[1552,128]{1,0:T(8,128)(2,1)S(1)}, u32[]{:S(2)}, u32[]{:S(2)}) collective-permute-start(bf16[1552,128]{1,0:T(8,128)(2,1)S(1)} %slope.1.m0), channel_id=1, source_target_pairs={{0,128},{32,160},{64,192},{96,224},{128,0},{160,32},{192,64},{224,... | collective-permute-start | bytes 1191944 | tf_op jit(solution)/shard_map/ppermute | solution.py:52
  109.7 17.4 %collective-permute-start.21 = (bf16[1552,128]{1,0:T(8,128)(2,1)S(1)}, bf16[1552,128]{1,0:T(8,128)(2,1)S(1)}, u32[]{:S(2)}, u32[]{:S(2)}) collective-permute-start(bf16[1552,128]{1,0:T(8,128)(2,1)S(1)} %slope.1.m0), channel_id=1, source_target_pairs={{0,192},{32,224},{64,0},{96,32},{128,64},{160,96},{192,128},{224,1... | collective-permute-start | bytes 1191944 | tf_op jit(solution)/shard_map/ppermute | solution.py:52
  133.3 18.4 %collective-permute-start.27 = (bf16[1552,128]{1,0:T(8,128)(2,1)S(1)}, bf16[1552,128]{1,0:T(8,128)(2,1)S(1)}, u32[]{:S(2)}, u32[]{:S(2)}) collective-permute-start(bf16[1552,128]{1,0:T(8,128)(2,1)S(1)} %get-tuple-element.130), channel_id=1, source_target_pairs={{0,16},{1,17},{2,18},{3,19},{4,20},{5,21},{6,22},{7,23},{8,24},{9,... | collective-permute-start | bytes 1191944 | tf_op jit(solution)/shard_map/ppermute | solution.py:48
  133.4 19.0 %collective-permute-start.28 = (bf16[1552,128]{1,0:T(8,128)(2,1)S(1)}, bf16[1552,128]{1,0:T(8,128)(2,1)S(1)}, u32[]{:S(2)}, u32[]{:S(2)}) collective-permute-start(bf16[1552,128]{1,0:T(8,128)(2,1)S(1)} %get-tuple-element.131), channel_id=1, source_target_pairs={{0,24},{1,25},{2,26},{3,27},{4,28},{5,29},{6,30},{7,31},{8,0},{9,1... | collective-permute-start | bytes 1191944 | tf_op jit(solution)/shard_map/ppermute | solution.py:48
  135.2 19.3 %collective-permute-start.26 = (bf16[1552,128]{1,0:T(8,128)(2,1)S(1)}, bf16[1552,128]{1,0:T(8,128)(2,1)S(1)}, u32[]{:S(2)}, u32[]{:S(2)}) collective-permute-start(bf16[1552,128]{1,0:T(8,128)(2,1)S(1)} %get-tuple-element.129.mine), channel_id=1, source_target_pairs={{0,8},{1,9},{2,10},{3,11},{4,12},{5,13},{6,14},{7,15},{8,16},{9,17... | collective-permute-start | bytes 1191944 | tf_op jit(solution)/shard_map/ppermute | solution.py:48
  135.7 10.0 %collective-permute-start.30 = (bf16[2,128,768]{2,1,0:T(8,128)(2,1)S(1)}, bf16[2,128,768]{2,1,0:T(8,128)(2,1)S(1)}, u32[]{:S(2)}, u32[]{:S(2)}) collective-permute-start(bf16[2,128,768]{2,1,0:T(8,128)(2,1)S(1)} %bitcast.12), channel_id=1, source_target_pairs={{0,64},{32,96},{64,128},{96,160},{128,192},{160,224},{192,0},{224,... | collective-permute-start | bytes 1179656 | tf_op jit(solution)/shard_map/ppermute | solution.py:52
  135.9 9.9 %collective-permute-start.29 = (bf16[2,128,768]{2,1,0:T(8,128)(2,1)S(1)}, bf16[2,128,768]{2,1,0:T(8,128)(2,1)S(1)}, u32[]{:S(2)}, u32[]{:S(2)}) collective-permute-start(bf16[2,128,768]{2,1,0:T(8,128)(2,1)S(1)} %bitcast.13), channel_id=1, source_target_pairs={{0,192},{32,224},{64,0},{96,32},{128,64},{160,96},{192,128},{224,1... | collective-permute-start | bytes 1179656 | tf_op jit(solution)/shard_map/ppermute | solution.py:52
  155.2 9.6 %collective-permute-start.32 = (bf16[400,128]{1,0:T(8,128)(2,1)S(1)}, bf16[400,128]{1,0:T(8,128)(2,1)S(1)}, u32[]{:S(2)}, u32[]{:S(2)}) collective-permute-start(bf16[400,128]{1,0:T(8,128)(2,1)S(1)} %get-tuple-element.142), channel_id=1, source_target_pairs={{0,4},{1,5},{2,6},{3,7},{4,0},{5,1},{6,2},{7,3},{8,12},{9,13},{10,... | collective-permute-start | bytes 307208 | tf_op jit(solution)/shard_map/ppermute | solution.py:44
  155.3 9.5 %collective-permute-start.33 = (bf16[400,128]{1,0:T(8,128)(2,1)S(1)}, bf16[400,128]{1,0:T(8,128)(2,1)S(1)}, u32[]{:S(2)}, u32[]{:S(2)}) collective-permute-start(bf16[400,128]{1,0:T(8,128)(2,1)S(1)} %get-tuple-element.143), channel_id=1, source_target_pairs={{0,6},{1,7},{2,4},{3,5},{4,2},{5,3},{6,0},{7,1},{8,14},{9,15},{10,... | collective-permute-start | bytes 307208 | tf_op jit(solution)/shard_map/ppermute | solution.py:44
  156.9 8.7 %collective-permute-start.31 = (bf16[400,128]{1,0:T(8,128)(2,1)S(1)}, bf16[400,128]{1,0:T(8,128)(2,1)S(1)}, u32[]{:S(2)}, u32[]{:S(2)}) collective-permute-start(bf16[400,128]{1,0:T(8,128)(2,1)S(1)} %get-tuple-element.141.mine), channel_id=1, source_target_pairs={{0,2},{1,3},{2,0},{3,1},{4,6},{5,7},{6,4},{7,5},{8,10},{9,11},{10,... | collective-permute-start | bytes 307208 | tf_op jit(solution)/shard_map/ppermute | solution.py:44
  (9 other events, 111.5 us)
